TPU v7x, 128 devices: a whole 4x4x4 slice. The times are simulated.
128 devices in a mesh: src: 16 (over x_lo, y, core), tgt: 8 (over x_hi, z).
Axes of the slice: x: 4 (x_hi: 2, x_lo: 2; x = x_hi * 2 + x_lo), y: 4, z: 4, core: 2. Of those that a mesh axis runs over, the one named last changes fastest.
Arguments:
- h_src: bfloat16 [8192, 768], P(('src', 'tgt')), may hold values from -6 to 6
- rel_table: bfloat16 [1387, 768], replicated, may hold values from -6 to 6
- cotangent: bfloat16 [4096, 768], P(('tgt', 'src')), may hold values from -6 to 6
- h_tgt: bfloat16 [4096, 768], P(('tgt', 'src')), may hold values from -6 to 6
- loop_rel: bfloat16 [768], replicated, may hold values from -6 to 6
- weights: bfloat16 [3, 768, 768], replicated, may hold values from -0.21875 to 0.21875
- src_index: int32 [16, 8, 16, 128], P('src', 'tgt'), may hold values from 0 to 511
- tgt_index: int32 [16, 8, 16, 128], P('src', 'tgt'), may hold values from 0 to 511
- rel_ids: int32 [16, 8, 16, 128], P('src', 'tgt'), may hold values from 0 to 1386
- direction: int32 [16, 8, 16, 128], P('src', 'tgt'), may hold values from 0 to 1
- counts: int32 [16, 8], P('src', 'tgt'), may hold values from 2 to 16, as said below
Outputs:
- grad_src: float32 [8192, 768], P(('src', 'tgt'))
- grad_tgt: float32 [4096, 768], P(('tgt', 'src'))
- grad_weights: float32 [3, 768, 768], replicated
- grad_rel: float32 [1387, 768], replicated
- grad_loop: float32 [768], replicated
Inputs may be any that keep to these rules, and one draw needn't show every extreme that they name: `counts`: each device has 16, 8, 4 or 2 live tiles; some device has all 16.
All inputs are finite; a program needn't handle non-finite values.
Results may differ from a plain program's by a relative error of at most 0.0031.
Values may be sent and summed in bfloat16 or wider, within the bound.
A program may use at most 128 MiB of HBM per device.

v0:
```python
import jax
import jax.numpy as jnp
from jax import lax
from jax.sharding import PartitionSpec as P


def one_hot_rows(indices, extent, dtype):
    return (indices[:, None] == jnp.arange(extent, dtype=jnp.int32)[None, :]).astype(dtype)


def body(
    h_src,
    rel_table,
    cotangent,
    h_tgt,
    loop_rel,
    weights,
    src_index,
    tgt_index,
    rel_ids,
    direction,
    counts,
):
    width = weights.shape[1]
    tiles = src_index.shape[2]
    edge = src_index.shape[3]
    block = 4 * edge
    rel_count = rel_table.shape[0]
    src_panel = lax.all_gather(h_src, "tgt", axis=0, tiled=True)
    tgt_panel = lax.all_gather(cotangent, "src", axis=0, tiled=True)
    src_rows_all = src_panel.shape[0]
    tgt_rows_all = tgt_panel.shape[0]
    w_cat = jnp.concatenate([weights[0], weights[1]], axis=1)
    source_all = src_index.reshape(tiles * edge)
    target_all = tgt_index.reshape(tiles * edge)
    relation_all = rel_ids.reshape(tiles * edge)
    flag_all = direction.reshape(tiles * edge)
    live_tiles = counts.reshape(())
    zero_rows = jnp.zeros((block, width), jnp.bfloat16)

    def step(number, carry):
        acc_src, acc_w, acc_rel = carry
        start = number * block
        source = lax.dynamic_slice_in_dim(source_all, start, block)
        target = lax.dynamic_slice_in_dim(target_all, start, block)
        relation = lax.dynamic_slice_in_dim(relation_all, start, block)
        flags = lax.dynamic_slice_in_dim(flag_all, start, block)
        live = (start + jnp.arange(block, dtype=jnp.int32)) // edge < live_tiles
        src_hot = one_hot_rows(source, src_rows_all, jnp.bfloat16)
        tgt_hot = one_hot_rows(target, tgt_rows_all, jnp.bfloat16)
        h_rows = jnp.dot(src_hot, src_panel, preferred_element_type=jnp.float32)
        z_rows = jnp.take(rel_table, relation, axis=0).astype(jnp.float32)
        comp = (h_rows * z_rows).astype(jnp.bfloat16)
        g_rows = jnp.dot(tgt_hot, tgt_panel, preferred_element_type=jnp.float32).astype(
            jnp.bfloat16
        )
        g_in = jnp.where((live & (flags == 0))[:, None], g_rows, zero_rows)
        g_out = jnp.where((live & (flags == 1))[:, None], g_rows, zero_rows)
        g_cat = jnp.concatenate([g_in, g_out], axis=1)
        dcomp = lax.dot_general(
            g_cat, w_cat, (((1,), (1,)), ((), ())), preferred_element_type=jnp.float32
        )
        acc_w = acc_w + lax.dot_general(
            comp, g_cat, (((0,), (0,)), ((), ())), preferred_element_type=jnp.float32
        )
        src_wide = src_hot.astype(jnp.float32)
        acc_src = acc_src + lax.dot_general(
            src_wide,
            dcomp * z_rows,
            (((0,), (0,)), ((), ())),
            precision=lax.Precision.HIGHEST,
            preferred_element_type=jnp.float32,
        )
        rel_hot = one_hot_rows(relation, rel_count, jnp.float32)
        acc_rel = acc_rel + lax.dot_general(
            rel_hot,
            dcomp * h_rows,
            (((0,), (0,)), ((), ())),
            precision=lax.Precision.HIGHEST,
            preferred_element_type=jnp.float32,
        )
        return (acc_src, acc_w, acc_rel)

    init = (
        jnp.zeros((src_rows_all, width), jnp.float32),
        jnp.zeros((width, 2 * width), jnp.float32),
        jnp.zeros((rel_count, width), jnp.float32),
    )
    steps_needed = tiles * edge // block
    acc_src, acc_w, acc_rel = lax.fori_loop(0, steps_needed, step, init)
    grad_src = lax.psum_scatter(acc_src, "tgt", scatter_dimension=0, tiled=True)
    loop_wide = loop_rel.astype(jnp.float32)
    back = lax.dot_general(
        cotangent, weights[2], (((1,), (1,)), ((), ())), preferred_element_type=jnp.float32
    )
    grad_tgt = back * loop_wide[None, :]
    self_comp = (h_tgt.astype(jnp.float32) * loop_wide[None, :]).astype(jnp.bfloat16)
    wself = lax.dot_general(
        self_comp, cotangent, (((0,), (0,)), ((), ())), preferred_element_type=jnp.float32
    )
    lsum = jnp.sum(back * h_tgt.astype(jnp.float32), axis=0)
    wsum, wself, rsum, lsum = lax.psum((acc_w, wself, acc_rel, lsum), ("src", "tgt"))
    devices_all = lax.axis_size("src") * lax.axis_size("tgt")
    edges_all = devices_all * tiles * edge
    targets_all = devices_all * cotangent.shape[0]
    edge_scale = float(edges_all) ** (-0.5)
    self_scale = float(targets_all) ** (-0.5)
    grad_weights = jnp.stack(
        [wsum[:, :width] * edge_scale, wsum[:, width:] * edge_scale, wself * self_scale]
    )
    grad_rel = rsum * (float(rel_count) / float(edges_all)) ** 0.5
    grad_loop = lsum * self_scale
    return (grad_src, grad_tgt, grad_weights, grad_rel, grad_loop)


def solution(mesh):
    return jax.shard_map(
        body,
        mesh=mesh,
        in_specs=(
            P(("src", "tgt"), None),
            P(),
            P(("tgt", "src"), None),
            P(("tgt", "src"), None),
            P(),
            P(),
            P("src", "tgt", None, None),
            P("src", "tgt", None, None),
            P("src", "tgt", None, None),
            P("src", "tgt", None, None),
            P("src", "tgt"),
        ),
        out_specs=(P(("src", "tgt"), None), P(("tgt", "src"), None), P(), P(), P()),
        check_vma=False,
    )
```

profile of v0, /device:TPU:1, one launch (start us, length us, event | category | flops | bytes accessed | tf_op | source)
XLA Modules:
  0.0 382.0 jit_solution(11634151250089393319)
XLA Ops:
  8.1 2.8 slice_bitcast_fusion.1
  10.9 24.7 %all_gather.6 = bf16[512,768]{1,0:T(8,128)(2,1)} all-gather(bf16[32,768]{1,0:T(8,128)(2,1)S(1)} %copy-done.6), channel_id=1, replica_groups=mesh['src'=16,'tgt'=8] {'src'}, dimensions={0}, use_global_device_ids=true | all-gather | bytes 835584 | tf_op jit(solution)/shard_map/all_gather | solution.py:30
  35.7 33.1 %all_gather.7 = bf16[512,768]{1,0:T(8,128)(2,1)} all-gather(bf16[64,768]{1,0:T(8,128)(2,1)S(1)} %copy-done.8), channel_id=1, replica_groups=mesh['src'=16,'tgt'=8] {'tgt'}, dimensions={0}, use_global_device_ids=true | all-gather | bytes 884736 | tf_op jit(solution)/shard_map/all_gather | solution.py:29
  68.8 3.0 pad_maximum_fusion.4
  71.8 117.3 %while.20 = (s32[]{:T(128)}, f32[512,768]{1,0:T(8,128)}, f32[768,1536]{1,0:T(8,128)}, f32[1387,768]{1,0:T(8,128)}, s32[2048]{0:T(1024)}, /*index=5*/s32[]{:T(128...) while((s32[]{:T(128)}, f32[512,768]{1,0:T(8,128)}, ...), condition=%wide.region_1.2_spmd.clone, body=%wide.region_0.1_spmd.clone.sunk | while | flops 12199237632 | bytes 66627424 | solution.py:90
  71.8 1.4 compare_and_fusion.4
  74.0 3.0 broadcast_select_fusion.6
  77.0 2.0 gather_fusion
  79.8 1.8 fusion.46
  81.6 5.3 %select_add_fusion.7 = f32[768,1536]{1,0:T(8,128)} fusion(f32[768,1536]{1,0:T(8,128)} %get-tuple-element.514, pred[]{:T(512)S(6)} %compare.13, bf16[512,768]{1,0:T(8,128)(2,1)} %get-tuple-element.491, bf16[512,768]{1,0:T(8,128)(2,1)} %get-tuple-element.492, f32[512,768]{1,0:T(8,128)S(1)} %fusion.46, bf16[512,768]{1,0:T(8,128)(2,1)S(1)} %gather_fusion, ...), kind=kOutput, calls=%fused_computation.1.clone.1 | convolution fusion | flops 1215037440 | bytes 13369857 | tf_op jit(solution)/shard_map/while/body/eval_jaxpr/dot_general | solution.py:63
  86.9 1.4 fusion.45
  88.3 6.2 %select_add_fusion.8 = f32[1387,768]{1,0:T(8,128)} fusion(f32[1387,768]{1,0:T(8,128)} %get-tuple-element.515, pred[]{:T(512)S(6)} %compare.13, f32[512,768]{1,0:T(8,128)S(1)} %fusion.45, f32[512,768]{1,0:T(8,128)S(1)} %fusion.46, s32[512]{0:T(512)S(1)} %get-tuple-element.493), kind=kOutput, calls=%fused_computation.2.clone.1 | convolution fusion | flops 6547920896 | bytes 11669505 | tf_op jit(solution)/shard_map/while/body/eval_jaxpr/dot_general | solution.py:75
  94.6 3.1 select_add_fusion.6
  97.7 1.4 compare_and_fusion.4
  99.9 3.0 broadcast_select_fusion.6
  102.9 2.0 gather_fusion
  104.9 0.8 dynamic_slice.52
  105.7 1.8 fusion.46
  107.5 6.7 %select_add_fusion.7 = f32[768,1536]{1,0:T(8,128)} fusion(f32[768,1536]{1,0:T(8,128)} %get-tuple-element.514, pred[]{:T(512)S(6)} %compare.13, bf16[512,768]{1,0:T(8,128)(2,1)} %get-tuple-element.491, bf16[512,768]{1,0:T(8,128)(2,1)} %get-tuple-element.492, f32[512,768]{1,0:T(8,128)S(1)} %fusion.46, bf16[512,768]{1,0:T(8,128)(2,1)S(1)} %gather_fusion, ...), kind=kOutput, calls=%fused_computation.1.clone.1 | convolution fusion | flops 1215037440 | bytes 13369857 | tf_op jit(solution)/shard_map/while/body/eval_jaxpr/dot_general | solution.py:63
  114.2 1.4 fusion.45
  115.6 7.9 %select_add_fusion.8 = f32[1387,768]{1,0:T(8,128)} fusion(f32[1387,768]{1,0:T(8,128)} %get-tuple-element.515, pred[]{:T(512)S(6)} %compare.13, f32[512,768]{1,0:T(8,128)S(1)} %fusion.45, f32[512,768]{1,0:T(8,128)S(1)} %fusion.46, s32[512]{0:T(512)S(1)} %get-tuple-element.493), kind=kOutput, calls=%fused_computation.2.clone.1 | convolution fusion | flops 6547920896 | bytes 11669505 | tf_op jit(solution)/shard_map/while/body/eval_jaxpr/dot_general | solution.py:75
  123.5 4.7 %select_add_fusion.6 = f32[512,768]{1,0:T(8,128)} fusion(f32[512,768]{1,0:T(8,128)} %get-tuple-element.513, f32[512,768]{1,0:T(8,128)S(1)} %fusion.45, pred[]{:T(512)S(6)} %compare.13, s32[512]{0:T(512)S(1)} %dynamic_slice.52, bf16[512,768]{1,0:T(8,128)(2,1)S(1)} %gather_fusion, pred[512]{0:T(512)(128)(4,1)S(1)} %get-tuple-element.494), kind=kOutput, calls=%fused_computation.9.clone.1 | convolution fusion | flops 2418147328 | bytes 5507585 | tf_op jit(solution)/shard_map/while/body/eval_jaxpr/dot_general | solution.py:67
  128.2 1.4 compare_and_fusion.4
  130.4 3.0 broadcast_select_fusion.6
  133.3 2.0 gather_fusion
  135.4 0.8 dynamic_slice.52
  136.1 1.8 fusion.46
  137.9 6.7 %select_add_fusion.7 = f32[768,1536]{1,0:T(8,128)} fusion(f32[768,1536]{1,0:T(8,128)} %get-tuple-element.514, pred[]{:T(512)S(6)} %compare.13, bf16[512,768]{1,0:T(8,128)(2,1)} %get-tuple-element.491, bf16[512,768]{1,0:T(8,128)(2,1)} %get-tuple-element.492, f32[512,768]{1,0:T(8,128)S(1)} %fusion.46, bf16[512,768]{1,0:T(8,128)(2,1)S(1)} %gather_fusion, ...), kind=kOutput, calls=%fused_computation.1.clone.1 | convolution fusion | flops 1215037440 | bytes 13369857 | tf_op jit(solution)/shard_map/while/body/eval_jaxpr/dot_general | solution.py:63
  144.7 1.4 fusion.45
  146.1 7.9 %select_add_fusion.8 = f32[1387,768]{1,0:T(8,128)} fusion(f32[1387,768]{1,0:T(8,128)} %get-tuple-element.515, pred[]{:T(512)S(6)} %compare.13, f32[512,768]{1,0:T(8,128)S(1)} %fusion.45, f32[512,768]{1,0:T(8,128)S(1)} %fusion.46, s32[512]{0:T(512)S(1)} %get-tuple-element.493), kind=kOutput, calls=%fused_computation.2.clone.1 | convolution fusion | flops 6547920896 | bytes 11669505 | tf_op jit(solution)/shard_map/while/body/eval_jaxpr/dot_general | solution.py:75
  154.0 4.7 %select_add_fusion.6 = f32[512,768]{1,0:T(8,128)} fusion(f32[512,768]{1,0:T(8,128)} %get-tuple-element.513, f32[512,768]{1,0:T(8,128)S(1)} %fusion.45, pred[]{:T(512)S(6)} %compare.13, s32[512]{0:T(512)S(1)} %dynamic_slice.52, bf16[512,768]{1,0:T(8,128)(2,1)S(1)} %gather_fusion, pred[512]{0:T(512)(128)(4,1)S(1)} %get-tuple-element.494), kind=kOutput, calls=%fused_computation.9.clone.1 | convolution fusion | flops 2418147328 | bytes 5507585 | tf_op jit(solution)/shard_map/while/body/eval_jaxpr/dot_general | solution.py:67
  158.6 1.4 compare_and_fusion.4
  160.8 3.0 broadcast_select_fusion.6
  163.8 2.0 gather_fusion
  165.8 0.8 dynamic_slice.52
  166.6 1.8 fusion.46
  168.4 6.7 %select_add_fusion.7 = f32[768,1536]{1,0:T(8,128)} fusion(f32[768,1536]{1,0:T(8,128)} %get-tuple-element.514, pred[]{:T(512)S(6)} %compare.13, bf16[512,768]{1,0:T(8,128)(2,1)} %get-tuple-element.491, bf16[512,768]{1,0:T(8,128)(2,1)} %get-tuple-element.492, f32[512,768]{1,0:T(8,128)S(1)} %fusion.46, bf16[512,768]{1,0:T(8,128)(2,1)S(1)} %gather_fusion, ...), kind=kOutput, calls=%fused_computation.1.clone.1 | convolution fusion | flops 1215037440 | bytes 13369857 | tf_op jit(solution)/shard_map/while/body/eval_jaxpr/dot_general | solution.py:63
  175.2 1.4 fusion.45
  176.6 7.9 %select_add_fusion.8 = f32[1387,768]{1,0:T(8,128)} fusion(f32[1387,768]{1,0:T(8,128)} %get-tuple-element.515, pred[]{:T(512)S(6)} %compare.13, f32[512,768]{1,0:T(8,128)S(1)} %fusion.45, f32[512,768]{1,0:T(8,128)S(1)} %fusion.46, s32[512]{0:T(512)S(1)} %get-tuple-element.493), kind=kOutput, calls=%fused_computation.2.clone.1 | convolution fusion | flops 6547920896 | bytes 11669505 | tf_op jit(solution)/shard_map/while/body/eval_jaxpr/dot_general | solution.py:75
  184.5 4.7 %select_add_fusion.6 = f32[512,768]{1,0:T(8,128)} fusion(f32[512,768]{1,0:T(8,128)} %get-tuple-element.513, f32[512,768]{1,0:T(8,128)S(1)} %fusion.45, pred[]{:T(512)S(6)} %compare.13, s32[512]{0:T(512)S(1)} %dynamic_slice.52, bf16[512,768]{1,0:T(8,128)(2,1)S(1)} %gather_fusion, pred[512]{0:T(512)(128)(4,1)S(1)} %get-tuple-element.494), kind=kOutput, calls=%fused_computation.9.clone.1 | convolution fusion | flops 2418147328 | bytes 5507585 | tf_op jit(solution)/shard_map/while/body/eval_jaxpr/dot_general | solution.py:67
  189.1 2.0 fusion.25
  191.8 2.4 fusion.24
  194.2 71.1 %psum.31 = f32[768]{0:T(1024)S(1)} all-reduce(f32[768]{0:T(1024)S(1)} %get-tuple-element.402), channel_id=1, replica_groups=mesh['src'=16,'tgt'=8] {'src','tgt'}, use_global_device_ids=true, to_apply=%region_7.8 | all-reduce | flops 768 | bytes 6144 | tf_op jit(solution)/shard_map/psum | solution.py:102
  265.9 99.4 %all-reduce.3.cloned.1.call-done = (f32[768,768]{1,0:T(8,128)}, f32[768,1536]{1,0:T(8,128)}, f32[1387,768]{1,0:T(8,128)}) async-done(((f32[768,768]{1,0:T(8,128)}, f32[768,1536]{1,0:T(8,128)}, f32[1387,768]{1,0:T(8,128)}), (f32[768,768]{1,0:T(8,128)}, f32[768,1536]{1,0:T(8,128)}, f32[1387,768]{1,0:T(8,128)})) %all-reduce.3.cloned.1.call-update) | async-done | bytes 11338768 | tf_op jit(solution)/shard_map/psum | solution.py:102
  365.3 2.0 multiply_bitcast_fusion
  367.3 1.1 copy-done.4
  368.7 3.4 pad_maximum_fusion.3
  372.1 2.5 broadcast_multiply_fusion
  (72 shorter events, 5.5 us)
Async XLA Ops:
  8.0 357.3 %all-reduce.3.cloned.1.call-start = ((), (), s32[]{:S(2)}) async-start(), calls=%async_computation.2 | async-start | bytes 22708224 | tf_op jit(solution)/shard_map/psum | solution.py:102
  8.1 2.9 copy-start.6
  8.1 27.6 %copy-start.8 = (bf16[64,768]{1,0:T(8,128)(2,1)S(1)}, bf16[64,768]{1,0:T(8,128)(2,1)}, u32[]{:S(2)}) copy-start(bf16[64,768]{1,0:T(8,128)(2,1)} %param.13) | copy-start | bytes 294916
  68.8 3.0 copy-start
  71.8 117.3 %copy-start.9 = (bf16[768]{0:T(1024)(128)(2,1)S(1)}, bf16[768]{0:T(1024)(128)(2,1)}, u32[]{:S(2)}) copy-start(bf16[768]{0:T(1024)(128)(2,1)} %param.17) | copy-start | bytes 4612
  71.8 117.3 %copy-start.7 = (bf16[32,768]{1,0:T(8,128)(2,1)S(1)}, bf16[32,768]{1,0:T(8,128)(2,1)}, u32[]{:S(2)}) copy-start(bf16[32,768]{1,0:T(8,128)(2,1)} %param.16) | copy-start | bytes 147460
  81.6 5.3 %copy-start.2 = (bf16[512,768]{1,0:T(8,128)(2,1)S(1)}, bf16[512,768]{1,0:T(8,128)(2,1)}, u32[]{:S(2)}) copy-start(bf16[512,768]{1,0:T(8,128)(2,1)} %get-tuple-element.492) | copy-start | bytes 2359300 | tf_op jit(solution)/shard_map/while
  81.6 5.3 %copy-start.3 = (bf16[512,768]{1,0:T(8,128)(2,1)S(1)}, bf16[512,768]{1,0:T(8,128)(2,1)}, u32[]{:S(2)}) copy-start(bf16[512,768]{1,0:T(8,128)(2,1)} %get-tuple-element.491) | copy-start | bytes 2359300 | tf_op jit(solution)/shard_map/while
  81.6 5.3 %copy-start.5 = (bf16[768,1536]{1,0:T(8,128)(2,1)S(1)}, bf16[768,1536]{1,0:T(8,128)(2,1)}, u32[]{:S(2)}) copy-start(bf16[768,1536]{1,0:T(8,128)(2,1)} %get-tuple-element.538) | copy-start | bytes 7077892 | tf_op jit(solution)/shard_map/while
  94.6 3.1 copy-start.1
  107.4 6.8 %copy-start.2 = (bf16[512,768]{1,0:T(8,128)(2,1)S(1)}, bf16[512,768]{1,0:T(8,128)(2,1)}, u32[]{:S(2)}) copy-start(bf16[512,768]{1,0:T(8,128)(2,1)} %get-tuple-element.492) | copy-start | bytes 2359300 | tf_op jit(solution)/shard_map/while
  107.4 6.8 %copy-start.3 = (bf16[512,768]{1,0:T(8,128)(2,1)S(1)}, bf16[512,768]{1,0:T(8,128)(2,1)}, u32[]{:S(2)}) copy-start(bf16[512,768]{1,0:T(8,128)(2,1)} %get-tuple-element.491) | copy-start | bytes 2359300 | tf_op jit(solution)/shard_map/while
  107.4 6.7 %copy-start.5 = (bf16[768,1536]{1,0:T(8,128)(2,1)S(1)}, bf16[768,1536]{1,0:T(8,128)(2,1)}, u32[]{:S(2)}) copy-start(bf16[768,1536]{1,0:T(8,128)(2,1)} %get-tuple-element.538) | copy-start | bytes 7077892 | tf_op jit(solution)/shard_map/while
  123.5 4.7 %copy-start.1 = (bf16[1387,768]{1,0:T(8,128)(2,1)S(1)}, bf16[1387,768]{1,0:T(8,128)(2,1)}, u32[]{:S(2)}) copy-start(bf16[1387,768]{1,0:T(8,128)(2,1)} %get-tuple-element.570) | copy-start | bytes 6391300 | tf_op jit(solution)/shard_map/while
  137.9 6.8 %copy-start.2 = (bf16[512,768]{1,0:T(8,128)(2,1)S(1)}, bf16[512,768]{1,0:T(8,128)(2,1)}, u32[]{:S(2)}) copy-start(bf16[512,768]{1,0:T(8,128)(2,1)} %get-tuple-element.492) | copy-start | bytes 2359300 | tf_op jit(solution)/shard_map/while
  137.9 6.8 %copy-start.3 = (bf16[512,768]{1,0:T(8,128)(2,1)S(1)}, bf16[512,768]{1,0:T(8,128)(2,1)}, u32[]{:S(2)}) copy-start(bf16[512,768]{1,0:T(8,128)(2,1)} %get-tuple-element.491) | copy-start | bytes 2359300 | tf_op jit(solution)/shard_map/while
  137.9 6.7 %copy-start.5 = (bf16[768,1536]{1,0:T(8,128)(2,1)S(1)}, bf16[768,1536]{1,0:T(8,128)(2,1)}, u32[]{:S(2)}) copy-start(bf16[768,1536]{1,0:T(8,128)(2,1)} %get-tuple-element.538) | copy-start | bytes 7077892 | tf_op jit(solution)/shard_map/while
  154.0 4.7 %copy-start.1 = (bf16[1387,768]{1,0:T(8,128)(2,1)S(1)}, bf16[1387,768]{1,0:T(8,128)(2,1)}, u32[]{:S(2)}) copy-start(bf16[1387,768]{1,0:T(8,128)(2,1)} %get-tuple-element.570) | copy-start | bytes 6391300 | tf_op jit(solution)/shard_map/while
  168.4 6.8 %copy-start.2 = (bf16[512,768]{1,0:T(8,128)(2,1)S(1)}, bf16[512,768]{1,0:T(8,128)(2,1)}, u32[]{:S(2)}) copy-start(bf16[512,768]{1,0:T(8,128)(2,1)} %get-tuple-element.492) | copy-start | bytes 2359300 | tf_op jit(solution)/shard_map/while
  168.4 6.8 %copy-start.3 = (bf16[512,768]{1,0:T(8,128)(2,1)S(1)}, bf16[512,768]{1,0:T(8,128)(2,1)}, u32[]{:S(2)}) copy-start(bf16[512,768]{1,0:T(8,128)(2,1)} %get-tuple-element.491) | copy-start | bytes 2359300 | tf_op jit(solution)/shard_map/while
  168.4 6.7 %copy-start.5 = (bf16[768,1536]{1,0:T(8,128)(2,1)S(1)}, bf16[768,1536]{1,0:T(8,128)(2,1)}, u32[]{:S(2)}) copy-start(bf16[768,1536]{1,0:T(8,128)(2,1)} %get-tuple-element.538) | copy-start | bytes 7077892 | tf_op jit(solution)/shard_map/while
  184.5 4.7 %copy-start.1 = (bf16[1387,768]{1,0:T(8,128)(2,1)S(1)}, bf16[1387,768]{1,0:T(8,128)(2,1)}, u32[]{:S(2)}) copy-start(bf16[1387,768]{1,0:T(8,128)(2,1)} %get-tuple-element.570) | copy-start | bytes 6391300 | tf_op jit(solution)/shard_map/while
  191.2 183.4 %reduce-scatter.2.cloned.1.call-start = ((), (), s32[]{:S(2)}) async-start(), calls=%async_computation.1 | async-start | bytes 1769472 | tf_op jit(solution)/shard_map/reduce_scatter | solution.py:91
  365.3 3.0 copy-start.4
  368.4 3.8 slice-start
  368.7 3.4 slice-start.1
Sparse Core Ops, SparseCore 0:
  191.3 173.9 all-reduce.2
Sparse Core Ops, SparseCore 1:
  195.9 78.7 reduce-scatter.1
where the time goes:
time: 383 us; the launch traced here: 382 us
  blocking collectives  129 us (34%)
  matrix products  101 us (26%)
  waiting for transfers between devices  99.9 us (26%)
  local copies, waits for them, and re-layouts  18.2 us (5%)
  other arithmetic  17.6 us (5%)
  between operations  15.6 us (4%)
    psum x1, waiting for transfers between devices, body(): lax.psum((acc_w, wself, acc_rel, lsum), ('src', 'tgt'))  99.4 us
    psum x1, blocking collectives, body(): lax.psum((acc_w, wself, acc_rel, lsum), ('src', 'tgt'))  71.1 us
    all_gather x1, blocking collectives, body(): src_panel = lax.all_gather(h_src, 'tgt', axis=0, tiled=True)  33.1 us
    dot_general x4, matrix products, step(): lax.dot_general(rel_hot, dcomp * h_rows, (((0,), (0,)), ((), ())), precis...  29.9 us
    dot_general x4, matrix products, step(): lax.dot_general(comp, g_cat, (((0,), (0,)), ((), ())), preferred_element_...  25.5 us
    all_gather x1, blocking collectives, body(): tgt_panel = lax.all_gather(cotangent, 'src', axis=0, tiled=True)  24.7 us
    dot_general x4, matrix products, step(): lax.dot_general(src_wide, dcomp * z_rows, (((0,), (0,)), ((), ())), preci...  17.1 us
    dot_general x4, matrix products, step(): jnp.dot(tgt_hot, tgt_panel, preferred_element_type=jnp.float32)  11.9 us
  transfers between devices with their start and end apart: 2, of which 1 were waited for; matrix products, arithmetic and copies ran while one was open for 3% of the time, Pallas kernels for 0%

commit v1 on v0

v1 whole, which is shorter than its diff:
```python
import functools

import jax
import jax.numpy as jnp
from jax import lax
from jax.experimental import pallas as pl
from jax.experimental.pallas import tpu as pltpu
from jax.sharding import PartitionSpec as P

F32 = jnp.float32
BF16 = jnp.bfloat16
MESH = pl.DeviceIdType.MESH
ANY = pl.BlockSpec(memory_space=pl.ANY)
VMEM = pl.BlockSpec(memory_space=pltpu.VMEM)
SMEM = pl.BlockSpec(memory_space=pltpu.SMEM)
DMA = pltpu.SemaphoreType.DMA

HALF_BLOCKS = 116
HALF_ROWS = 11264
W_BLOCKS = 144
PARTS = ((("x", "y", "z"), 64), (("y", "z", "x"), 64), (("z", "x", "y"), 48))
BASES = (0, 4096, 8192)
UNROLL = 8


class Place:
    def __init__(self):
        s, t = lax.axis_index("src"), lax.axis_index("tgt")
        self.x_lo, self.core = s // 8, s % 2
        self.x_hi = t // 4
        self.at = {"x": self.x_hi * 2 + self.x_lo, "y": (s // 2) % 4, "z": t % 4}

    def device(self, at, core):
        return ((at["x"] % 2) * 8 + at["y"] * 2 + core, (at["x"] // 2) * 4 + at["z"])

    def along(self, axis, offset):
        at = dict(self.at)
        at[axis] = (at[axis] + offset) % 4
        return self.device(at, self.core)

    def sibling(self):
        return self.device(self.at, 1 - self.core)

    def x_lo_partner(self):
        at = dict(self.at)
        at["x"] = self.x_hi * 2 + (1 - self.x_lo)
        return self.device(at, self.core)


def greet(partners):
    barrier = pltpu.get_barrier_semaphore()
    for partner in partners:
        pl.semaphore_signal(barrier, inc=1, device_id=partner, device_id_type=MESH)
    pl.semaphore_wait(barrier, len(partners))


def push(src, dst, send, recv, device):
    return pltpu.make_async_remote_copy(
        src_ref=src, dst_ref=dst, send_sem=send, recv_sem=recv, device_id=device, device_id_type=MESH
    )


def gather_kernel(
    h_ref, c_ref, h_all, c_all, local, hx_s, hx_r, hz_s, hz_r, cy_s, cy_r, cx_s, cx_r, cs_s, cs_r
):
    me = Place()
    x_lo, x_hi, core, y, z = me.x_lo, me.x_hi, me.core, me.at["y"], me.at["z"]
    sibling, across = me.sibling(), me.x_lo_partner()
    own_h = pltpu.make_async_copy(h_ref, h_all.at[x_hi, z], local.at[0])
    own_c = pltpu.make_async_copy(c_ref, c_all.at[x_lo, y, core], local.at[1])
    own_h.start()
    own_c.start()
    greet(
        [me.along("x", 2), across, sibling]
        + [me.along("y", k) for k in (1, 2, 3)]
        + [me.along("z", k) for k in (1, 2, 3)]
    )
    hx = push(h_ref, h_all.at[x_hi, z], hx_s, hx_r, me.along("x", 2))
    hx.start()
    cy = []
    for k in (1, 2, 3):
        copy = push(c_ref, c_all.at[x_lo, y, core], cy_s.at[k - 1], cy_r.at[k - 1], me.along("y", k))
        copy.start()
        cy.append(copy)
    own_h.wait()
    own_c.wait()
    hx.wait()
    hz = []
    for k in (1, 2, 3):
        copy = push(h_all.at[:, z], h_all.at[:, z], hz_s.at[k - 1], hz_r.at[k - 1], me.along("z", k))
        copy.start()
        hz.append(copy)
    for copy in cy:
        copy.wait()
    mine = c_all.at[x_lo, :, core]
    theirs = c_all.at[1 - x_lo, :, core]
    cx = push(mine, mine, cx_s, cx_r, across)
    cx.start()
    first = push(mine, mine, cs_s.at[0], cs_r.at[0], sibling)
    first.start()
    cx.wait()
    second = push(theirs, theirs, cs_s.at[1], cs_r.at[1], sibling)
    second.start()
    first.wait()
    second.wait()
    for copy in hz:
        copy.wait()


def gather(h_src, cotangent):
    rows, width = h_src.shape
    trows = cotangent.shape[0]
    h_all, c_all = pl.pallas_call(
        gather_kernel,
        out_shape=(
            jax.ShapeDtypeStruct((2, 4, rows, width), BF16),
            jax.ShapeDtypeStruct((2, 4, 2, trows, width), BF16),
        ),
        in_specs=[ANY] * 2,
        out_specs=[ANY] * 2,
        scratch_shapes=[
            DMA((2,)), DMA, DMA, DMA((3,)), DMA((3,)), DMA((3,)), DMA((3,)), DMA, DMA, DMA((2,)), DMA((2,)),
        ],
        compiler_params=pltpu.CompilerParams(collective_id=0, has_side_effects=True),
        name="gather_panels",
    )(h_src, cotangent)
    return h_all.reshape(8 * rows, width), c_all.reshape(16 * trows, width)


def edge_kernel(
    live_ref, src_ref, tgt_ref, rel_ref, h_ref, c_ref, w_ref, z_ref, own_c, own_h, loop_ref,
    g_out, t_out, keep, give, hx, px, zx, gs, aa, rr, hi, lo,
):
    core = lax.axis_index("src") % 2
    rows = h_ref.shape[0]
    trows = c_ref.shape[0]
    rels, width = z_ref.shape
    chunks = width // 128

    def spread(dst, row, value):
        for c in range(chunks):
            dst[pl.ds(row * 8 + c, value.shape[0], stride=8), :] = value[:, c * 128 : (c + 1) * 128]

    def put(half, row, tile):
        @pl.when(core == half)
        def _():
            keep[pl.ds(row, 16), :] = tile

        @pl.when(core != half)
        def _():
            give[pl.ds(row, 16), :] = tile.astype(BF16)

    def put_blocks(block, value):
        for half in range(2):
            first = max(block, half * HALF_BLOCKS)
            last = min(block + value.shape[0] // 16, (half + 1) * HALF_BLOCKS)
            if first >= last:
                continue

            def store(ref, half=half, first=first, last=last):
                for b in range(first, last):
                    for c in range(chunks):
                        row = ((b - half * HALF_BLOCKS) * chunks + c) * 16
                        part = value[(b - block) * 16 : (b - block + 1) * 16, c * 128 : (c + 1) * 128]
                        ref[row : row + 16, :] = part.astype(ref.dtype)

            @pl.when(core == half)
            def _(store=store):
                store(keep)

            @pl.when(core != half)
            def _(store=store):
                store(give)

    @pl.loop(0, rows // 16)
    def _(i):
        r = pl.multiple_of(i * 16, 16)
        spread(hx, r, h_ref[pl.ds(r, 16), :].astype(F32))

    @pl.loop(0, rels // 16)
    def _(i):
        r = pl.multiple_of(i * 16, 16)
        spread(zx, r, z_ref[pl.ds(r, 16), :].astype(F32))

    tail = rels // 16 * 16
    if tail < rels:
        spread(zx, tail, z_ref[tail:rels, :].astype(F32))
    for d in range(2):
        for k in range(width // 256):
            p = lax.dot_general(
                c_ref[...], w_ref[d, k * 256 : (k + 1) * 256, :], (((1,), (1,)), ((), ())),
                preferred_element_type=F32,
            )
            for h in range(2):
                px[pl.ds(d * trows * 8 + 2 * k + h, trows, stride=8), :] = p[:, h * 128 : (h + 1) * 128]
    zero = jnp.zeros((64, 128), F32)
    for ref in (gs, aa, rr):

        @pl.loop(0, ref.shape[0] // 64)
        def _(i, ref=ref):
            ref[pl.ds(pl.multiple_of(i * 64, 64), 64), :] = zero

    @pl.loop(0, live_ref[0])
    def _(i):
        for u in range(UNROLL):
            e = i * UNROLL + u
            s = pl.ds(pl.multiple_of(src_ref[e], 8), 8)
            t = pl.ds(pl.multiple_of(tgt_ref[e], 8), 8)
            r = pl.ds(pl.multiple_of(rel_ref[e], 8), 8)
            h = hx[s, :]
            p = px[t, :]
            z = zx[r, :]
            gs[s, :] += p * z
            aa[t, :] += (h * z).astype(BF16).astype(F32)
            rr[r, :] += p * h

    loop_wide = loop_ref[...].astype(F32)
    h_wide = own_h[...].astype(F32)
    back = lax.dot_general(
        own_c[...], w_ref[2], (((1,), (1,)), ((), ())), preferred_element_type=F32
    )
    t_out[...] = back * loop_wide
    lsum = jnp.sum(back * h_wide, axis=0, keepdims=True)
    for c in range(chunks):
        rr[rels * 8 + c : rels * 8 + c + 1, :] = lsum[:, c * 128 : (c + 1) * 128]
    self_comp = (h_wide * loop_wide).astype(BF16)
    for k in range(width // 256):
        wself = lax.dot_general(
            self_comp[:, k * 256 : (k + 1) * 256], own_c[...], (((0,), (0,)), ((), ())),
            preferred_element_type=F32,
        )
        put_blocks(96 + k * 16, wself)

    @pl.loop(0, rows // 16)
    def _(i):
        r = pl.multiple_of(i * 16, 16)
        for c in range(chunks):
            g_out[pl.ds(r, 16), c * 128 : (c + 1) * 128] = gs[pl.ds(r * 8 + c, 16, stride=8), :].astype(BF16)

    @pl.loop(0, 2 * trows // 16)
    def _(i):
        r = pl.multiple_of(i * 16, 16)
        for c in range(chunks):
            a = aa[pl.ds(r * 8 + c, 16, stride=8), :]
            top = a.astype(BF16)
            hi[pl.ds(r, 16), c * 128 : (c + 1) * 128] = top
            lo[pl.ds(r, 16), c * 128 : (c + 1) * 128] = (a - top.astype(F32)).astype(BF16)

    for d in range(2):
        at = slice(d * trows, (d + 1) * trows)
        for k in range(width // 256):
            cols = slice(k * 256, (k + 1) * 256)
            w = lax.dot_general(
                hi[at, cols], c_ref[...], (((0,), (0,)), ((), ())), preferred_element_type=F32
            ) + lax.dot_general(
                lo[at, cols], c_ref[...], (((0,), (0,)), ((), ())), preferred_element_type=F32
            )
            put_blocks(d * 48 + k * 16, w)

    rel_base = (W_BLOCKS - HALF_BLOCKS) * chunks * 16

    @pl.loop(0, rr.shape[0] // 128)
    def _(i):
        for c in range(chunks):
            put(
                1,
                pl.multiple_of(rel_base + (i * chunks + c) * 16, 16),
                rr[pl.ds(i * 128 + c, 16, stride=8), :],
            )

    low = rel_base + rr.shape[0] // 128 * chunks * 16
    high = HALF_BLOCKS * chunks * 16
    for half, end in ((0, high), (1, low)):

        @pl.when(core == half)
        def _(end=end):
            keep[end:, :] = jnp.zeros((HALF_ROWS - end, 128), F32)

        @pl.when(core != half)
        def _(end=end):
            give[end:, :] = jnp.zeros((HALF_ROWS - end, 128), BF16)


def edges(live, s8, t8, r8, h, c, w, z, own_c, own_h, loop):
    rows, width = h.shape
    trows = c.shape[0]
    rpad = (z.shape[0] + 16) // 16 * 16
    return pl.pallas_call(
        edge_kernel,
        out_shape=(
            jax.ShapeDtypeStruct((rows, width), BF16),
            jax.ShapeDtypeStruct((own_c.shape[0], width), F32),
            jax.ShapeDtypeStruct((HALF_ROWS, 128), F32),
            jax.ShapeDtypeStruct((HALF_ROWS, 128), BF16),
        ),
        in_specs=[SMEM] * 4 + [VMEM] * 7,
        out_specs=[VMEM] * 4,
        scratch_shapes=[
            pltpu.VMEM((rows * 8, 128), F32),
            pltpu.VMEM((2 * trows * 8, 128), F32),
            pltpu.VMEM((rpad * 8, 128), F32),
            pltpu.VMEM((rows * 8, 128), F32),
            pltpu.VMEM((2 * trows * 8, 128), F32),
            pltpu.VMEM((rpad * 8, 128), F32),
            pltpu.VMEM((2 * trows, width), BF16),
            pltpu.VMEM((2 * trows, width), BF16),
        ],
        compiler_params=pltpu.CompilerParams(vmem_limit_bytes=58 * 2**20),
        name="edges",
    )(live, s8, t8, r8, h, c, w, z, own_c, own_h, loop)


def reduce_kernel(
    keep, give, g_ref, full, g_out,
    pair, out1, in1, acc1, in2, acc2, in3, unit, g_in, g_acc, g_side,
    pair_s, pair_r, s1, r1, s2, r2, s3, r3, s4, r4, s5, r5, s6, r6, sib_s, sib_r, gz_s, gz_r, gx_s, gx_r,
    local,
):
    me = Place()
    core = me.core
    sibling = me.sibling()
    x_hi, z = me.x_hi, me.at["z"]
    greet([me.along(axis, k) for axis in ("x", "y", "z") for k in (1, 2, 3)] + [sibling])

    sent = []
    gz = []
    for k in (1, 2, 3):
        copy = push(
            g_ref.at[:, (z + k) % 4], g_in.at[k - 1], gz_s.at[k - 1], gz_r.at[k - 1], me.along("z", k)
        )
        copy.start()
        gz.append(copy)

    def rows_of(p, a):
        size = PARTS[p][1] * 16
        return pl.ds(pl.multiple_of(BASES[p] + a * size, 16), size)

    def first(p):
        return me.at[PARTS[p][0][0]]

    def second(p):
        return me.at[PARTS[p][0][1]]

    def third(p):
        return me.at[PARTS[p][0][2]]

    pairs = {}
    for j in (1, 2, 3, 0):
        for p in range(3):
            where = rows_of(p, (first(p) + j) % 4)
            copy = push(give.at[where], pair.at[where], pair_s.at[p * 4 + j], pair_r.at[p * 4 + j], sibling)
            copy.start()
            pairs[p, j] = copy

    step1 = {}
    for j in (1, 2, 3):
        for p in range(3):
            axis, unit_rows = PARTS[p][0][0], PARTS[p][1]
            base = BASES[p] + ((first(p) + j) % 4) * (unit_rows * 16)
            pairs[p, j].wait_recv()

            @pl.loop(0, unit_rows * 16 // 128)
            def _(i, base=base):
                r = pl.ds(pl.multiple_of(base + i * 128, 16), 128)
                out1[r, :] = (keep[r, :] + pair[r, :].astype(F32)).astype(BF16)

            where = rows_of(p, (first(p) + j) % 4)
            copy = push(
                out1.at[where],
                in1.at[j - 1, pl.ds(BASES[p] // 4, unit_rows * 16)],
                s1.at[p * 3 + j - 1],
                r1.at[p * 3 + j - 1],
                me.along(axis, j),
            )
            copy.start()
            step1[p, j] = copy

    for copy in gz:
        copy.wait_recv()
    for half in range(2):
        g_acc[half] = (
            g_ref[half, z].astype(F32)
            + g_in[0, half].astype(F32)
            + g_in[1, half].astype(F32)
            + g_in[2, half].astype(F32)
        )
    gx = push(g_acc.at[1 - x_hi], g_side, gx_s, gx_r, me.along("x", 2))
    gx.start()

    step2 = {}
    for p in range(3):
        axis, unit_rows = PARTS[p][0][1], PARTS[p][1]
        base = BASES[p] + first(p) * (unit_rows * 16)
        low = BASES[p] // 4
        pairs[p, 0].wait_recv()
        for j in (1, 2, 3):
            step1[p, j].wait_recv()

        @pl.loop(0, unit_rows * 16 // 128)
        def _(i, base=base, low=low):
            r = pl.ds(pl.multiple_of(base + i * 128, 16), 128)
            q = pl.ds(pl.multiple_of(low + i * 128, 16), 128)
            acc1[q, :] = (
                keep[r, :]
                + pair[r, :].astype(F32)
                + in1[0, q, :].astype(F32)
                + in1[1, q, :].astype(F32)
                + in1[2, q, :].astype(F32)
            )

        for j in (1, 2, 3):
            where = pl.ds(pl.multiple_of(low + ((second(p) + j) % 4) * (unit_rows * 4), 16), unit_rows * 4)
            copy = push(
                acc1.at[where],
                in2.at[j - 1, pl.ds(BASES[p] // 16, unit_rows * 4)],
                s2.at[p * 3 + j - 1],
                r2.at[p * 3 + j - 1],
                me.along(axis, j),
            )
            copy.start()
            step2[p, j] = copy

    step3 = {}
    for p in range(3):
        axis, unit_rows = PARTS[p][0][2], PARTS[p][1]
        for j in (1, 2, 3):
            step2[p, j].wait_recv()
        size = unit_rows * 4
        q = pl.ds(BASES[p] // 16, size)
        mine = pl.ds(pl.multiple_of(BASES[p] // 4 + second(p) * size, 16), size)
        acc2[q, :] = acc1[mine, :] + in2[0, q, :] + in2[1, q, :] + in2[2, q, :]
        for j in (1, 2, 3):
            where = pl.ds(
                pl.multiple_of(BASES[p] // 16 + ((third(p) + j) % 4) * unit_rows, 16), unit_rows
            )
            copy = push(
                acc2.at[where],
                in3.at[j - 1, pl.ds(BASES[p] // 64, unit_rows)],
                s3.at[p * 3 + j - 1],
                r3.at[p * 3 + j - 1],
                me.along(axis, j),
            )
            copy.start()
            step3[p, j] = copy

    def place(p, depth):
        unit_rows = PARTS[p][1]
        row = core * HALF_ROWS + BASES[p] + first(p) * (unit_rows * 16)
        if depth > 1:
            row = row + second(p) * (unit_rows * 4)
        if depth > 2:
            row = row + third(p) * unit_rows
        size = (unit_rows * 16, unit_rows * 4, unit_rows)[depth - 1]
        return pl.ds(pl.multiple_of(row, 16), size)

    step4, own = {}, {}
    for p in range(3):
        axis, unit_rows = PARTS[p][0][2], PARTS[p][1]
        for j in (1, 2, 3):
            step3[p, j].wait_recv()
        q = pl.ds(BASES[p] // 64, unit_rows)
        mine = pl.ds(pl.multiple_of(BASES[p] // 16 + third(p) * unit_rows, 16), unit_rows)
        unit[q, :] = (acc2[mine, :] + in3[0, q, :] + in3[1, q, :] + in3[2, q, :]).astype(BF16)
        own[p] = pltpu.make_async_copy(unit.at[q], full.at[place(p, 3)], local.at[p])
        own[p].start()
        for j in (1, 2, 3):
            copy = push(
                unit.at[q], full.at[place(p, 3)], s4.at[p * 3 + j - 1], r4.at[p * 3 + j - 1], me.along(axis, j)
            )
            copy.start()
            step4[p, j] = copy

    step5 = {}
    for p in range(3):
        own[p].wait()
        for j in (1, 2, 3):
            step4[p, j].wait_recv()
        for j in (1, 2, 3):
            block = full.at[place(p, 2)]
            copy = push(block, block, s5.at[p * 3 + j - 1], r5.at[p * 3 + j - 1], me.along(PARTS[p][0][1], j))
            copy.start()
            step5[p, j] = copy

    step6, side = {}, {}
    for p in range(3):
        for j in (1, 2, 3):
            step5[p, j].wait_recv()
        block = full.at[place(p, 1)]
        for j in (1, 2, 3):
            copy = push(block, block, s6.at[p * 3 + j - 1], r6.at[p * 3 + j - 1], me.along(PARTS[p][0][0], j))
            copy.start()
            step6[p, j] = copy
        side[p, 0] = push(block, block, sib_s.at[p * 4], sib_r.at[p * 4], sibling)
        side[p, 0].start()

    gx.wait_recv()
    g_out[...] = g_acc[x_hi] + g_side[...]

    for j in (1, 3, 2):
        for p in range(3):
            size = PARTS[p][1] * 16
            step6[p, j].wait_recv()
            row = core * HALF_ROWS + BASES[p] + ((first(p) + 4 - j) % 4) * size
            block = full.at[pl.ds(pl.multiple_of(row, 16), size)]
            side[p, j] = push(block, block, sib_s.at[p * 4 + j], sib_r.at[p * 4 + j], sibling)
            side[p, j].start()

    for copy in side.values():
        copy.wait_recv()
    gx.wait_send()
    for group in (gz, pairs.values(), step1.values(), step2.values(), step3.values(), step4.values()):
        for copy in group:
            copy.wait_send()
    for group in (step5.values(), step6.values(), side.values()):
        for copy in group:
            copy.wait_send()


def reduce_all(keep, give, g):
    rows, width = g.shape
    g = g.reshape(2, 4, rows // 8, width)
    return pl.pallas_call(
        reduce_kernel,
        out_shape=(
            jax.ShapeDtypeStruct((2 * HALF_ROWS, 128), BF16),
            jax.ShapeDtypeStruct((rows // 8, width), F32),
        ),
        in_specs=[VMEM, ANY, VMEM],
        out_specs=[ANY, VMEM],
        scratch_shapes=[
            pltpu.VMEM((HALF_ROWS, 128), BF16),
            pltpu.VMEM((HALF_ROWS, 128), BF16),
            pltpu.VMEM((3, HALF_ROWS // 4, 128), BF16),
            pltpu.VMEM((HALF_ROWS // 4, 128), F32),
            pltpu.VMEM((3, HALF_ROWS // 16, 128), F32),
            pltpu.VMEM((HALF_ROWS // 16, 128), F32),
            pltpu.VMEM((3, HALF_ROWS // 64, 128), F32),
            pltpu.VMEM((HALF_ROWS // 64, 128), BF16),
            pltpu.VMEM((3, 2, rows // 8, width), BF16),
            pltpu.VMEM((2, rows // 8, width), F32),
            pltpu.VMEM((rows // 8, width), F32),
            DMA((12,)), DMA((12,)),
            *[DMA((9,)) for _ in range(12)],
            DMA((12,)), DMA((12,)), DMA((3,)), DMA((3,)), DMA, DMA, DMA((3,)),
        ],
        compiler_params=pltpu.CompilerParams(
            collective_id=1, has_side_effects=True, vmem_limit_bytes=48 * 2**20
        ),
        name="reduce_all",
    )(keep, give, g)


def unpack_kernel(full, w_out, r_out, l_out, *, edge_scale, self_scale, rel_scale):
    rels, width = r_out.shape
    chunks = width // 128
    per = width // 16

    def tile(block, c):
        half = block // HALF_BLOCKS
        row = half * HALF_ROWS + ((block - half * HALF_BLOCKS) * chunks + c) * 16
        return full[pl.ds(pl.multiple_of(row, 16), 16), :].astype(F32)

    for d, scale in enumerate((edge_scale, edge_scale, self_scale)):

        @pl.loop(0, per)
        def _(i, d=d, scale=scale):
            for c in range(chunks):
                w_out[d, pl.ds(pl.multiple_of(i * 16, 16), 16), c * 128 : (c + 1) * 128] = (
                    tile(d * per + i, c) * scale
                )

    whole = rels // 16

    @pl.loop(0, whole)
    def _(i):
        for c in range(chunks):
            r_out[pl.ds(pl.multiple_of(i * 16, 16), 16), c * 128 : (c + 1) * 128] = (
                tile(W_BLOCKS + i, c) * rel_scale
            )

    rest = rels - whole * 16
    for c in range(chunks):
        last = tile(W_BLOCKS + whole, c)
        cols = slice(c * 128, (c + 1) * 128)
        if rest:
            r_out[whole * 16 : rels, cols] = last[:rest] * rel_scale
        l_out[:, cols] = last[rest : rest + 1] * self_scale


def unpack(full, rels, width, **scales):
    return pl.pallas_call(
        functools.partial(unpack_kernel, **scales),
        out_shape=(
            jax.ShapeDtypeStruct((3, width, width), F32),
            jax.ShapeDtypeStruct((rels, width), F32),
            jax.ShapeDtypeStruct((1, width), F32),
        ),
        in_specs=[VMEM],
        out_specs=[VMEM] * 3,
        compiler_params=pltpu.CompilerParams(vmem_limit_bytes=48 * 2**20),
        name="unpack",
    )(full)


def body(
    h_src, rel_table, cotangent, h_tgt, loop_rel, weights, src_index, tgt_index, rel_ids, direction, counts
):
    width = weights.shape[1]
    tiles, edge = src_index.shape[2:]
    rels = rel_table.shape[0]
    h_all, c_all = gather(h_src, cotangent)
    trows = c_all.shape[0]
    live = (counts * (edge // UNROLL)).reshape(1)
    s8 = (src_index * 8).reshape(tiles * edge)
    t8 = ((tgt_index + direction * trows) * 8).reshape(tiles * edge)
    r8 = (rel_ids * 8).reshape(tiles * edge)
    g, grad_tgt, keep, give = edges(
        live, s8, t8, r8, h_all, c_all, weights, rel_table, cotangent, h_tgt, loop_rel.reshape(1, width)
    )
    full, grad_src = reduce_all(keep, give, g)
    devices = lax.axis_size("src") * lax.axis_size("tgt")
    edges_all = float(devices * tiles * edge)
    targets_all = float(devices * cotangent.shape[0])
    grad_weights, grad_rel, grad_loop = unpack(
        full,
        rels,
        width,
        edge_scale=edges_all**-0.5,
        self_scale=targets_all**-0.5,
        rel_scale=(float(rels) / edges_all) ** 0.5,
    )
    return grad_src, grad_tgt, grad_weights, grad_rel, grad_loop.reshape(width)


def solution(mesh):
    return jax.shard_map(
        body,
        mesh=mesh,
        in_specs=(
            P(("src", "tgt"), None),
            P(),
            P(("tgt", "src"), None),
            P(("tgt", "src"), None),
            P(),
            P(),
            P("src", "tgt", None, None),
            P("src", "tgt", None, None),
            P("src", "tgt", None, None),
            P("src", "tgt", None, None),
            P("src", "tgt"),
        ),
        out_specs=(P(("src", "tgt"), None), P(("tgt", "src"), None), P(), P(), P()),
        check_vma=False,
    )
```

time: 383 us -> 140 us (0.37)
  blocking collectives: 129 us -> 0 us
  Pallas kernels: 0 us -> 127 us
  matrix products: 101 us -> 0 us
  waiting for transfers between devices: 99.9 us -> 0 us
  other arithmetic: 17.6 us -> 3.23 us
  between operations: 15.6 us -> 1.31 us
  local copies, waits for them, and re-layouts: 18.2 us -> 7.51 us
    pallas_call x0 -> x4, Pallas kernels: none -> 127 us  [the longest x1 61.5 us: reduce_all(): pl.pallas_call(reduce_kernel, out_shape=(jax.ShapeDtypeStruct((2 * HALF_R...]
    dot_general x26 -> x0, matrix products: 101 us -> none  [the longest x4 29.9 us: step(): lax.dot_general(rel_hot, dcomp * h_rows, (((0,), (0,)), ((), ())), precis...]
    psum x1 -> x0, waiting for transfers between devices: 99.4 us -> none  [body(): lax.psum((acc_w, wself, acc_rel, lsum), ('src', 'tgt'))]
    psum x1 -> x0, blocking collectives: 71.1 us -> none  [body(): lax.psum((acc_w, wself, acc_rel, lsum), ('src', 'tgt'))]
    all_gather x2 -> x0, blocking collectives: 57.8 us -> none  [the longest x1 33.1 us: body(): src_panel = lax.all_gather(h_src, 'tgt', axis=0, tiled=True)]
    gather x4 -> x0, local copies, waits for them, and re-layouts: 8.1 us -> none  [step(): z_rows = jnp.take(rel_table, relation, axis=0).astype(jnp.float32)]
    dynamic_slice x8 -> x0, local copies, waits for them, and re-layouts: 6.1 us -> none  [the longest x4 3.06 us: step(): source = lax.dynamic_slice_in_dim(source_all, start, block)]
    and x4 -> x0, other arithmetic: 5.74 us -> none  [step(): z_rows = jnp.take(rel_table, relation, axis=0).astype(jnp.float32)]
  transfers between devices with their start and end apart: 2 -> 0, of which waited for: 1 -> 0; matrix products, arithmetic and copies ran while one was open for 3% -> 0% of each run, Pallas kernels for 0% -> 0%
where the time goes in v1:
time: 140 us; the launch traced here: 139 us
  Pallas kernels  127 us (91%)
  local copies, waits for them, and re-layouts  7.51 us (5%)
  other arithmetic  3.23 us (2%)
    pallas_call x1, Pallas kernels, reduce_all(): pl.pallas_call(reduce_kernel, out_shape=(jax.ShapeDtypeStruct((2 * HALF_R...  61.5 us
    pallas_call x1, Pallas kernels, edges(): pl.pallas_call(edge_kernel, out_shape=(jax.ShapeDtypeStruct((rows, width)...  35.3 us
    pallas_call x1, Pallas kernels, gather(): pl.pallas_call(gather_kernel, out_shape=(jax.ShapeDtypeStruct((2, 4, rows...  20.5 us
    pallas_call x1, Pallas kernels, unpack(): pl.pallas_call(functools.partial(unpack_kernel, **scales), out_shape=(jax...  10.1 us
    unnamed x7, local copies, waits for them, and re-layouts  6.25 us

profile of v1, /device:TPU:1, one launch (start us, length us, event | category | flops | bytes accessed | tf_op | source)
XLA Modules:
  0.0 139.5 jit_solution(2988691917723967131)
XLA Ops:
  1.3 1.3 reshape.43.loop_ref
  2.5 1.3 multiply_bitcast_fusion.2.src_ref
  3.8 1.3 multiply_bitcast_fusion
  5.2 20.5 %gather_panels.1 = (bf16[2,4,64,768]{3,2,1,0:T(8,128)(2,1)}, bf16[2,4,2,32,768]{4,3,2,1,0:T(8,128)(2,1)}) custom-call(bf16[64,768]{1,0:T(8,128)(2,1)} %h_ref.1, bf16[32,768]{1,0:T(8,128)(2,1)} %own_c.1), custom_call_target="tpu_custom_call" | custom-call | tf_op jit(solution)/shard_map/gather_panels/pallas_call | solution.py:113
  25.7 35.3 %edges.1 = (bf16[512,768]{1,0:T(8,128)(2,1)}, f32[32,768]{1,0:T(8,128)}, f32[11264,128]{1,0:T(8,128)}, bf16[11264,128]{1,0:T(8,128)(2,1)}) custom-call(s32[1]{0:T(128)} %bitcast.live_ref, s32[2048]{0:T(1024)} %multiply_bitcast_fusion.2.src_ref, s32[2048]{0:T(1024)} %get-tuple-element.28.tgt_ref, s32[2048]{0:T(1024)} %get-tuple-element.27.rel_ref, ...), custom_call_target="tpu_custom_call" | custom-call | tf_op jit(solution)/shard_map/edges/pallas_call | solution.py:288
  61.0 0.0 copy-start.1
  61.0 1.8 %copy-done.1 = bf16[11264,128]{1,0:T(8,128)(2,1)S(1)} copy-done((bf16[11264,128]{1,0:T(8,128)(2,1)S(1)}, bf16[11264,128]{1,0:T(8,128)(2,1)}, u32[]{:S(2)}) %copy-start.1) | copy-done | bytes 2883608
  62.9 0.0 copy-start.2
  62.9 1.1 copy-done.2
  64.0 61.5 %reduce_all.1 = (bf16[22528,128]{1,0:T(8,128)(2,1)}, f32[64,768]{1,0:T(8,128)S(1)}) custom-call(f32[11264,128]{1,0:T(8,128)} %get-tuple-element.18.keep, bf16[11264,128]{1,0:T(8,128)(2,1)S(1)} %copy-done.1, bf16[2,4,64,768]{3,2,1,0:T(8,128)(2,1)S(1)} %bitcast.10), custom_call_target="tpu_custom_call" | custom-call | tf_op jit(solution)/shard_map/reduce_all/pallas_call | solution.py:522
  125.5 0.0 copy-start
  125.5 2.6 %copy-done = bf16[22528,128]{1,0:T(8,128)(2,1)S(1)} copy-done((bf16[22528,128]{1,0:T(8,128)(2,1)S(1)}, bf16[22528,128]{1,0:T(8,128)(2,1)}, u32[]{:S(2)}) %copy-start) | copy-done | bytes 5767192
  128.1 10.1 %unpack.1 = (f32[3,768,768]{2,1,0:T(8,128)}, f32[1387,768]{1,0:T(8,128)}, f32[1,768]{1,0:T(1,128)S(1)}) custom-call(bf16[22528,128]{1,0:T(8,128)(2,1)S(1)} %copy-done), custom_call_target="tpu_custom_call" | custom-call | tf_op jit(solution)/shard_map/unpack/pallas_call | solution.py:591
  138.2 0.6 reduce
  138.8 0.7 copy.18
Async XLA Ops:
  61.0 1.8 %copy-start.1 = (bf16[11264,128]{1,0:T(8,128)(2,1)S(1)}, bf16[11264,128]{1,0:T(8,128)(2,1)}, u32[]{:S(2)}) copy-start(bf16[11264,128]{1,0:T(8,128)(2,1)} %get-tuple-element.19.give) | copy-start | bytes 8650756
  62.9 1.1 copy-start.2
  125.5 2.6 %copy-start = (bf16[22528,128]{1,0:T(8,128)(2,1)S(1)}, bf16[22528,128]{1,0:T(8,128)(2,1)}, u32[]{:S(2)}) copy-start(bf16[22528,128]{1,0:T(8,128)(2,1)} %get-tuple-element.23.full) | copy-start | bytes 17301508

commit v2 on v1

--- a/solution.py
+++ b/solution.py
@@ -20,7 +20,8 @@
 W_BLOCKS = 144
 PARTS = ((("x", "y", "z"), 64), (("y", "z", "x"), 64), (("z", "x", "y"), 48))
 BASES = (0, 4096, 8192)
-UNROLL = 8
+UNROLL = 16
+VMEM_BYTES = 63 * 2**20
 
 
 class Place:
@@ -61,7 +62,7 @@
 
 
 def gather_kernel(
-    h_ref, c_ref, h_all, c_all, local, hx_s, hx_r, hz_s, hz_r, cy_s, cy_r, cx_s, cx_r, cs_s, cs_r
+    h_ref, c_ref, src_ref, tgt_ref, rel_ref, dir_ref, h_all, c_all, s8, t8, r8, local, hx_s, hx_r, hz_s, hz_r, cy_s, cy_r, cx_s, cx_r, cs_s, cs_r
 ):
     me = Place()
     x_lo, x_hi, core, y, z = me.x_lo, me.x_hi, me.core, me.at["y"], me.at["z"]
@@ -70,6 +71,9 @@
     own_c = pltpu.make_async_copy(c_ref, c_all.at[x_lo, y, core], local.at[1])
     own_h.start()
     own_c.start()
+    s8[...] = src_ref[...] * 8
+    t8[...] = (tgt_ref[...] + dir_ref[...] * (16 * c_ref.shape[0])) * 8
+    r8[...] = rel_ref[...] * 8
     greet(
         [me.along("x", 2), across, sibling]
         + [me.along("y", k) for k in (1, 2, 3)]
@@ -107,30 +111,38 @@
         copy.wait()
 
 
-def gather(h_src, cotangent):
+def gather(h_src, cotangent, *indices):
     rows, width = h_src.shape
     trows = cotangent.shape[0]
-    h_all, c_all = pl.pallas_call(
+    h_all, c_all, s8, t8, r8 = pl.pallas_call(
         gather_kernel,
         out_shape=(
             jax.ShapeDtypeStruct((2, 4, rows, width), BF16),
             jax.ShapeDtypeStruct((2, 4, 2, trows, width), BF16),
+            *[jax.ShapeDtypeStruct(indices[0].shape, jnp.int32)] * 3,
         ),
-        in_specs=[ANY] * 2,
-        out_specs=[ANY] * 2,
+        in_specs=[ANY] * 2 + [VMEM] * 4,
+        out_specs=[ANY] * 2 + [VMEM] * 3,
         scratch_shapes=[
             DMA((2,)), DMA, DMA, DMA((3,)), DMA((3,)), DMA((3,)), DMA((3,)), DMA, DMA, DMA((2,)), DMA((2,)),
         ],
-        compiler_params=pltpu.CompilerParams(collective_id=0, has_side_effects=True),
+        compiler_params=pltpu.CompilerParams(collective_id=0, has_side_effects=True, vmem_limit_bytes=VMEM_BYTES),
         name="gather_panels",
-    )(h_src, cotangent)
-    return h_all.reshape(8 * rows, width), c_all.reshape(16 * trows, width)
+    )(h_src, cotangent, *indices)
+    return h_all.reshape(8 * rows, width), c_all.reshape(16 * trows, width), s8, t8, r8
 
 
 def edge_kernel(
-    live_ref, src_ref, tgt_ref, rel_ref, h_ref, c_ref, w_ref, z_ref, own_c, own_h, loop_ref,
-    g_out, t_out, keep, give, hx, px, zx, gs, aa, rr, hi, lo,
+    live_ref, src_ref, tgt_ref, rel_ref, h_hbm, c_hbm, w_hbm, z_hbm, own_c, own_h, loop_ref,
+    g_out, t_out, keep_out, give_out,
+    h_ref, c_ref, w_ref, z_ref, g_ref, keep, give, hx, px, zx, gs, aa, rr, hi, lo, in_sem, out_sem,
 ):
+    loads = [
+        pltpu.make_async_copy(a, b, in_sem.at[i])
+        for i, (a, b) in enumerate(((h_hbm, h_ref), (z_hbm, z_ref), (c_hbm, c_ref), (w_hbm, w_ref)))
+    ]
+    for load in loads:
+        load.start()
     core = lax.axis_index("src") % 2
     rows = h_ref.shape[0]
     trows = c_ref.shape[0]
@@ -172,11 +184,33 @@
             def _(store=store):
                 store(give)
 
+    flushed = []
+
+    def flush(half, first, last):
+        n = len(flushed)
+        where = pl.ds(first, last - first)
+        kept = pltpu.make_async_copy(keep.at[where], keep_out.at[where], out_sem.at[2 * n])
+        given = pltpu.make_async_copy(give.at[where], give_out.at[where], out_sem.at[2 * n + 1])
+        flushed.append((half, kept, given))
+        pl.when(core == half)(kept.start)
+        pl.when(core != half)(given.start)
+
+    zero = jnp.zeros((64, 128), F32)
+    for ref in (gs, aa, rr):
+
+        @pl.loop(0, ref.shape[0] // 64)
+        def _(i, ref=ref):
+            ref[pl.ds(pl.multiple_of(i * 64, 64), 64), :] = zero
+
+    loads[0].wait()
+
     @pl.loop(0, rows // 16)
     def _(i):
         r = pl.multiple_of(i * 16, 16)
         spread(hx, r, h_ref[pl.ds(r, 16), :].astype(F32))
 
+    loads[1].wait()
+
     @pl.loop(0, rels // 16)
     def _(i):
         r = pl.multiple_of(i * 16, 16)
@@ -185,6 +219,8 @@
     tail = rels // 16 * 16
     if tail < rels:
         spread(zx, tail, z_ref[tail:rels, :].astype(F32))
+    loads[2].wait()
+    loads[3].wait()
     for d in range(2):
         for k in range(width // 256):
             p = lax.dot_general(
@@ -193,28 +229,33 @@
             )
             for h in range(2):
                 px[pl.ds(d * trows * 8 + 2 * k + h, trows, stride=8), :] = p[:, h * 128 : (h + 1) * 128]
-    zero = jnp.zeros((64, 128), F32)
-    for ref in (gs, aa, rr):
-
-        @pl.loop(0, ref.shape[0] // 64)
-        def _(i, ref=ref):
-            ref[pl.ds(pl.multiple_of(i * 64, 64), 64), :] = zero
-
-    @pl.loop(0, live_ref[0])
+    def row(at):
+        return pl.ds(pl.multiple_of(at, 8), 8)
+
+    edge = src_ref.shape[1]
+
+    @pl.loop(0, live_ref[0] * (edge // UNROLL))
     def _(i):
-        for u in range(UNROLL):
-            e = i * UNROLL + u
-            s = pl.ds(pl.multiple_of(src_ref[e], 8), 8)
-            t = pl.ds(pl.multiple_of(tgt_ref[e], 8), 8)
-            r = pl.ds(pl.multiple_of(rel_ref[e], 8), 8)
-            h = hx[s, :]
-            p = px[t, :]
-            z = zx[r, :]
-            gs[s, :] += p * z
-            aa[t, :] += (h * z).astype(BF16).astype(F32)
-            rr[r, :] += p * h
-
-    loop_wide = loop_ref[...].astype(F32)
+        tile = i // (edge // UNROLL)
+        start = (i % (edge // UNROLL)) * UNROLL
+        for u in range(0, UNROLL, 2):
+            s0, s1 = src_ref[tile, start + u], src_ref[tile, start + u + 1]
+            t0, t1 = tgt_ref[tile, start + u], tgt_ref[tile, start + u + 1]
+            r0, r1 = rel_ref[tile, start + u], rel_ref[tile, start + u + 1]
+            h0, h1 = hx[row(s0), :], hx[row(s1), :]
+            p0, p1 = px[row(t0), :], px[row(t1), :]
+            z0, z1 = zx[row(r0), :], zx[row(r1), :]
+            for ref, at0, at1, v0, v1 in (
+                (gs, s0, s1, p0 * z0, p1 * z1),
+                (aa, t0, t1, (h0 * z0).astype(BF16).astype(F32), (h1 * z1).astype(BF16).astype(F32)),
+                (rr, r0, r1, p0 * h0, p1 * h1),
+            ):
+                sum0 = ref[row(at0), :] + v0
+                sum1 = ref[row(at1), :] + v1 + jnp.where(at0 == at1, v0, jnp.zeros_like(v0))
+                ref[row(at0), :] = sum0
+                ref[row(at1), :] = sum1
+
+    loop_wide = loop_ref[...].astype(F32).reshape(1, width)
     h_wide = own_h[...].astype(F32)
     back = lax.dot_general(
         own_c[...], w_ref[2], (((1,), (1,)), ((), ())), preferred_element_type=F32
@@ -223,6 +264,30 @@
     lsum = jnp.sum(back * h_wide, axis=0, keepdims=True)
     for c in range(chunks):
         rr[rels * 8 + c : rels * 8 + c + 1, :] = lsum[:, c * 128 : (c + 1) * 128]
+    rel_base = (W_BLOCKS - HALF_BLOCKS) * chunks * 16
+
+    @pl.loop(0, rr.shape[0] // 128)
+    def _(i):
+        for c in range(chunks):
+            put(
+                1,
+                pl.multiple_of(rel_base + (i * chunks + c) * 16, 16),
+                rr[pl.ds(i * 128 + c, 16, stride=8), :],
+            )
+
+    low = rel_base + rr.shape[0] // 128 * chunks * 16
+    high = HALF_BLOCKS * chunks * 16
+    for half, end in ((0, high), (1, low)):
+
+        @pl.when(core == half)
+        def _(end=end):
+            keep[end:, :] = jnp.zeros((HALF_ROWS - end, 128), F32)
+
+        @pl.when(core != half)
+        def _(end=end):
+            give[end:, :] = jnp.zeros((HALF_ROWS - end, 128), BF16)
+
+    flush(1, rel_base, HALF_ROWS)
     self_comp = (h_wide * loop_wide).astype(BF16)
     for k in range(width // 256):
         wself = lax.dot_general(
@@ -230,12 +295,17 @@
             preferred_element_type=F32,
         )
         put_blocks(96 + k * 16, wself)
+    flush(0, 96 * chunks * 16, HALF_ROWS)
+    flush(1, 0, rel_base)
 
     @pl.loop(0, rows // 16)
     def _(i):
         r = pl.multiple_of(i * 16, 16)
         for c in range(chunks):
-            g_out[pl.ds(r, 16), c * 128 : (c + 1) * 128] = gs[pl.ds(r * 8 + c, 16, stride=8), :].astype(BF16)
+            g_ref[pl.ds(r, 16), c * 128 : (c + 1) * 128] = gs[pl.ds(r * 8 + c, 16, stride=8), :].astype(BF16)
+
+    g_copy = pltpu.make_async_copy(g_ref, g_out, in_sem.at[4])
+    g_copy.start()
 
     @pl.loop(0, 2 * trows // 16)
     def _(i):
@@ -256,29 +326,12 @@
                 lo[at, cols], c_ref[...], (((0,), (0,)), ((), ())), preferred_element_type=F32
             )
             put_blocks(d * 48 + k * 16, w)
-
-    rel_base = (W_BLOCKS - HALF_BLOCKS) * chunks * 16
-
-    @pl.loop(0, rr.shape[0] // 128)
-    def _(i):
-        for c in range(chunks):
-            put(
-                1,
-                pl.multiple_of(rel_base + (i * chunks + c) * 16, 16),
-                rr[pl.ds(i * 128 + c, 16, stride=8), :],
-            )
-
-    low = rel_base + rr.shape[0] // 128 * chunks * 16
-    high = HALF_BLOCKS * chunks * 16
-    for half, end in ((0, high), (1, low)):
-
-        @pl.when(core == half)
-        def _(end=end):
-            keep[end:, :] = jnp.zeros((HALF_ROWS - end, 128), F32)
-
-        @pl.when(core != half)
-        def _(end=end):
-            give[end:, :] = jnp.zeros((HALF_ROWS - end, 128), BF16)
+        flush(0, d * 48 * chunks * 16, (d + 1) * 48 * chunks * 16)
+
+    g_copy.wait()
+    for half, kept, given in flushed:
+        pl.when(core == half)(kept.wait)
+        pl.when(core != half)(given.wait)
 
 
 def edges(live, s8, t8, r8, h, c, w, z, own_c, own_h, loop):
@@ -293,9 +346,16 @@
             jax.ShapeDtypeStruct((HALF_ROWS, 128), F32),
             jax.ShapeDtypeStruct((HALF_ROWS, 128), BF16),
         ),
-        in_specs=[SMEM] * 4 + [VMEM] * 7,
-        out_specs=[VMEM] * 4,
+        in_specs=[SMEM] * 4 + [ANY] * 4 + [VMEM] * 3,
+        out_specs=[ANY, VMEM, ANY, ANY],
         scratch_shapes=[
+            pltpu.VMEM(h.shape, BF16),
+            pltpu.VMEM(c.shape, BF16),
+            pltpu.VMEM(w.shape, BF16),
+            pltpu.VMEM(z.shape, BF16),
+            pltpu.VMEM((rows, width), BF16),
+            pltpu.VMEM((HALF_ROWS, 128), F32),
+            pltpu.VMEM((HALF_ROWS, 128), BF16),
             pltpu.VMEM((rows * 8, 128), F32),
             pltpu.VMEM((2 * trows * 8, 128), F32),
             pltpu.VMEM((rpad * 8, 128), F32),
@@ -304,25 +364,48 @@
             pltpu.VMEM((rpad * 8, 128), F32),
             pltpu.VMEM((2 * trows, width), BF16),
             pltpu.VMEM((2 * trows, width), BF16),
+            DMA((5,)),
+            DMA((10,)),
         ],
-        compiler_params=pltpu.CompilerParams(vmem_limit_bytes=58 * 2**20),
+        compiler_params=pltpu.CompilerParams(vmem_limit_bytes=VMEM_BYTES),
         name="edges",
     )(live, s8, t8, r8, h, c, w, z, own_c, own_h, loop)
 
 
 def reduce_kernel(
-    keep, give, g_ref, full, g_out,
-    pair, out1, in1, acc1, in2, acc2, in3, unit, g_in, g_acc, g_side,
+    keep_hbm, give, g_ref, full, g_out,
+    keep, g_own, pair, out1, in1, acc1, in2, acc2, in3, unit, g_in, g_acc, g_side,
     pair_s, pair_r, s1, r1, s2, r2, s3, r3, s4, r4, s5, r5, s6, r6, sib_s, sib_r, gz_s, gz_r, gx_s, gx_r,
-    local,
+    local, kept,
 ):
     me = Place()
     core = me.core
     sibling = me.sibling()
     x_hi, z = me.x_hi, me.at["z"]
+
+    def rows_of(p, a):
+        size = PARTS[p][1] * 16
+        return pl.ds(pl.multiple_of(BASES[p] + a * size, 16), size)
+
+    def first(p):
+        return me.at[PARTS[p][0][0]]
+
+    def second(p):
+        return me.at[PARTS[p][0][1]]
+
+    def third(p):
+        return me.at[PARTS[p][0][2]]
+
+    order = [(p, j) for j in (1, 2, 3, 0) for p in range(3)]
+    keeps = {}
+    for p, j in order:
+        where = rows_of(p, (first(p) + j) % 4)
+        keeps[p, j] = pltpu.make_async_copy(keep_hbm.at[where], keep.at[where], kept.at[p * 4 + j])
+        keeps[p, j].start()
+    own_g = pltpu.make_async_copy(g_ref.at[:, z], g_own, kept.at[12])
+    own_g.start()
     greet([me.along(axis, k) for axis in ("x", "y", "z") for k in (1, 2, 3)] + [sibling])
 
-    sent = []
     gz = []
     for k in (1, 2, 3):
         copy = push(
@@ -331,32 +414,19 @@
         copy.start()
         gz.append(copy)
 
-    def rows_of(p, a):
-        size = PARTS[p][1] * 16
-        return pl.ds(pl.multiple_of(BASES[p] + a * size, 16), size)
-
-    def first(p):
-        return me.at[PARTS[p][0][0]]
-
-    def second(p):
-        return me.at[PARTS[p][0][1]]
-
-    def third(p):
-        return me.at[PARTS[p][0][2]]
-
     pairs = {}
-    for j in (1, 2, 3, 0):
-        for p in range(3):
-            where = rows_of(p, (first(p) + j) % 4)
-            copy = push(give.at[where], pair.at[where], pair_s.at[p * 4 + j], pair_r.at[p * 4 + j], sibling)
-            copy.start()
-            pairs[p, j] = copy
+    for p, j in order:
+        where = rows_of(p, (first(p) + j) % 4)
+        copy = push(give.at[where], pair.at[where], pair_s.at[p * 4 + j], pair_r.at[p * 4 + j], sibling)
+        copy.start()
+        pairs[p, j] = copy
 
     step1 = {}
     for j in (1, 2, 3):
         for p in range(3):
             axis, unit_rows = PARTS[p][0][0], PARTS[p][1]
             base = BASES[p] + ((first(p) + j) % 4) * (unit_rows * 16)
+            keeps[p, j].wait()
             pairs[p, j].wait_recv()
 
             @pl.loop(0, unit_rows * 16 // 128)
@@ -375,11 +445,12 @@
             copy.start()
             step1[p, j] = copy
 
+    own_g.wait()
     for copy in gz:
         copy.wait_recv()
     for half in range(2):
         g_acc[half] = (
-            g_ref[half, z].astype(F32)
+            g_own[half].astype(F32)
             + g_in[0, half].astype(F32)
             + g_in[1, half].astype(F32)
             + g_in[2, half].astype(F32)
@@ -392,6 +463,7 @@
         axis, unit_rows = PARTS[p][0][1], PARTS[p][1]
         base = BASES[p] + first(p) * (unit_rows * 16)
         low = BASES[p] // 4
+        keeps[p, 0].wait()
         pairs[p, 0].wait_recv()
         for j in (1, 2, 3):
             step1[p, j].wait_recv()
@@ -525,9 +597,11 @@
             jax.ShapeDtypeStruct((2 * HALF_ROWS, 128), BF16),
             jax.ShapeDtypeStruct((rows // 8, width), F32),
         ),
-        in_specs=[VMEM, ANY, VMEM],
+        in_specs=[ANY] * 3,
         out_specs=[ANY, VMEM],
         scratch_shapes=[
+            pltpu.VMEM((HALF_ROWS, 128), F32),
+            pltpu.VMEM((2, rows // 8, width), BF16),
             pltpu.VMEM((HALF_ROWS, 128), BF16),
             pltpu.VMEM((HALF_ROWS, 128), BF16),
             pltpu.VMEM((3, HALF_ROWS // 4, 128), BF16),
@@ -541,35 +615,66 @@
             pltpu.VMEM((rows // 8, width), F32),
             DMA((12,)), DMA((12,)),
             *[DMA((9,)) for _ in range(12)],
-            DMA((12,)), DMA((12,)), DMA((3,)), DMA((3,)), DMA, DMA, DMA((3,)),
+            DMA((12,)), DMA((12,)), DMA((3,)), DMA((3,)), DMA, DMA, DMA((3,)), DMA((13,)),
         ],
         compiler_params=pltpu.CompilerParams(
-            collective_id=1, has_side_effects=True, vmem_limit_bytes=48 * 2**20
+            collective_id=1, has_side_effects=True, vmem_limit_bytes=VMEM_BYTES
         ),
         name="reduce_all",
     )(keep, give, g)
 
 
-def unpack_kernel(full, w_out, r_out, l_out, *, edge_scale, self_scale, rel_scale):
+def unpack_kernel(
+    full_hbm, w_hbm, r_out, l_out, full, w_out, in_sem, out_sem, *, edge_scale, self_scale, rel_scale
+):
     rels, width = r_out.shape
     chunks = width // 128
     per = width // 16
+    pieces = in_sem.shape[0]
+    size = full.shape[0] // pieces
+    loads = []
+    for i in range(pieces):
+        where = pl.ds(i * size, size)
+        loads.append(pltpu.make_async_copy(full_hbm.at[where], full.at[where], in_sem.at[i]))
+        loads[-1].start()
+    waited = [0]
+
+    def start_of(block):
+        half = block // HALF_BLOCKS
+        return half * HALF_ROWS + (block - half * HALF_BLOCKS) * chunks * 16
+
+    def need(blocks):
+        end = start_of(blocks - 1) + chunks * 16
+        while waited[0] * size < end:
+            loads[waited[0]].wait()
+            waited[0] += 1
 
     def tile(block, c):
         half = block // HALF_BLOCKS
         row = half * HALF_ROWS + ((block - half * HALF_BLOCKS) * chunks + c) * 16
         return full[pl.ds(pl.multiple_of(row, 16), 16), :].astype(F32)
 
+    stores = []
     for d, scale in enumerate((edge_scale, edge_scale, self_scale)):
-
-        @pl.loop(0, per)
-        def _(i, d=d, scale=scale):
-            for c in range(chunks):
-                w_out[d, pl.ds(pl.multiple_of(i * 16, 16), 16), c * 128 : (c + 1) * 128] = (
-                    tile(d * per + i, c) * scale
-                )
+        for k in range(3):
+            group = per // 3
+            need(d * per + (k + 1) * group)
+
+            @pl.loop(k * group, (k + 1) * group)
+            def _(i, d=d, scale=scale):
+                for c in range(chunks):
+                    w_out[d, pl.ds(pl.multiple_of(i * 16, 16), 16), c * 128 : (c + 1) * 128] = (
+                        tile(d * per + i, c) * scale
+                    )
+
+            where = pl.ds(k * group * 16, group * 16)
+            stores.append(
+                pltpu.make_async_copy(w_out.at[d, where], w_hbm.at[d, where], out_sem.at[d * 3 + k])
+            )
+            stores[-1].start()
 
     whole = rels // 16
+    need(W_BLOCKS + whole + 1)
 
     @pl.loop(0, whole)
     def _(i):
@@ -584,7 +689,12 @@
         cols = slice(c * 128, (c + 1) * 128)
         if rest:
             r_out[whole * 16 : rels, cols] = last[:rest] * rel_scale
-        l_out[:, cols] = last[rest : rest + 1] * self_scale
+        l_out[cols] = (last[rest : rest + 1] * self_scale).reshape(128)
+    while waited[0] < pieces:
+        loads[waited[0]].wait()
+        waited[0] += 1
+    for store in stores:
+        store.wait()
 
 
 def unpack(full, rels, width, **scales):
@@ -593,11 +703,17 @@
         out_shape=(
             jax.ShapeDtypeStruct((3, width, width), F32),
             jax.ShapeDtypeStruct((rels, width), F32),
-            jax.ShapeDtypeStruct((1, width), F32),
+            jax.ShapeDtypeStruct((width,), F32),
         ),
-        in_specs=[VMEM],
-        out_specs=[VMEM] * 3,
-        compiler_params=pltpu.CompilerParams(vmem_limit_bytes=48 * 2**20),
+        in_specs=[ANY],
+        out_specs=[ANY, VMEM, VMEM],
+        scratch_shapes=[
+            pltpu.VMEM(full.shape, BF16),
+            pltpu.VMEM((3, width, width), F32),
+            DMA((11,)),
+            DMA((9,)),
+        ],
+        compiler_params=pltpu.CompilerParams(vmem_limit_bytes=VMEM_BYTES),
         name="unpack",
     )(full)
 
@@ -608,14 +724,11 @@
     width = weights.shape[1]
     tiles, edge = src_index.shape[2:]
     rels = rel_table.shape[0]
-    h_all, c_all = gather(h_src, cotangent)
-    trows = c_all.shape[0]
-    live = (counts * (edge // UNROLL)).reshape(1)
-    s8 = (src_index * 8).reshape(tiles * edge)
-    t8 = ((tgt_index + direction * trows) * 8).reshape(tiles * edge)
-    r8 = (rel_ids * 8).reshape(tiles * edge)
+    h_all, c_all, s8, t8, r8 = gather(
+        h_src, cotangent, *[a.reshape(tiles, edge) for a in (src_index, tgt_index, rel_ids, direction)]
+    )
     g, grad_tgt, keep, give = edges(
-        live, s8, t8, r8, h_all, c_all, weights, rel_table, cotangent, h_tgt, loop_rel.reshape(1, width)
+        counts.reshape(1), s8, t8, r8, h_all, c_all, weights, rel_table, cotangent, h_tgt, loop_rel
     )
     full, grad_src = reduce_all(keep, give, g)
     devices = lax.axis_size("src") * lax.axis_size("tgt")
@@ -629,7 +742,7 @@
         self_scale=targets_all**-0.5,
         rel_scale=(float(rels) / edges_all) ** 0.5,
     )
-    return grad_src, grad_tgt, grad_weights, grad_rel, grad_loop.reshape(width)
+    return grad_src, grad_tgt, grad_weights, grad_rel, grad_loop
 
 
 def solution(mesh):

time: 140 us -> 128 us (0.914)
  local copies, waits for them, and re-layouts: 7.51 us -> 0.68 us
  other arithmetic: 3.23 us -> 0 us
    pallas_call x1, Pallas kernels: 35.3 us -> 23.8 us  [edges(): pl.pallas_call(edge_kernel, out_shape=(jax.ShapeDtypeStruct((rows, width)...]
    pallas_call x1, Pallas kernels: 61.5 us -> 71.6 us  [reduce_all(): pl.pallas_call(reduce_kernel, out_shape=(jax.ShapeDtypeStruct((2 * HALF_R...]
    unnamed x7 -> x3, local copies, waits for them, and re-layouts: 6.25 us -> 0.68 us
    reshape x2 -> x0, other arithmetic: 2.63 us -> none  [the longest x1 1.33 us: body(): r8 = (rel_ids * 8).reshape(tiles * edge)]
    pallas_call x1, Pallas kernels: 20.5 us -> 22 us  [gather(): pl.pallas_call(gather_kernel, out_shape=(jax.ShapeDtypeStruct((2, 4, rows...]
where the time goes in v2:
time: 128 us
  Pallas kernels  126 us (98%)
  between operations  1.33 us (1%)
    pallas_call x1, Pallas kernels, reduce_all(): pl.pallas_call(reduce_kernel, out_shape=(jax.ShapeDtypeStruct((2 * HALF_R...  71.6 us
    pallas_call x1, Pallas kernels, edges(): pl.pallas_call(edge_kernel, out_shape=(jax.ShapeDtypeStruct((rows, width)...  23.8 us
    pallas_call x1, Pallas kernels, gather(): pl.pallas_call(gather_kernel, out_shape=(jax.ShapeDtypeStruct((2, 4, rows...  22 us
    pallas_call x1, Pallas kernels, unpack(): pl.pallas_call(functools.partial(unpack_kernel, **scales), out_shape=(jax...  8.86 us

profile of v2, /device:TPU:1, one launch (start us, length us, event | category | flops | bytes accessed | tf_op | source)
XLA Modules:
  0.0 128.2 jit_solution(12461810582359701160)
XLA Ops:
  1.3 22.0 %gather_panels.1 = (bf16[2,4,64,768]{3,2,1,0:T(8,128)(2,1)}, bf16[2,4,2,32,768]{4,3,2,1,0:T(8,128)(2,1)}, s32[16,128]{1,0:T(8,128)}, s32[16,128]{1,0:T(8,128)}, s32[16,128]{1,0:T(8,128)}) custom-call(bf16[64,768]{1,0:T(8,128)(2,1)} %h_ref.1, bf16[32,768]{1,0:T(8,128)(2,1)} %own_c.1, s32[16,128]{1,0:T(8,128)} %bitcast.12, s32[16,128]{1,0:T(8,128)} %bitcast.13, ...), custom_call_target="tpu_custom_call" | custom-call | tf_op jit(solution)/shard_map/gather_panels/pallas_call | solution.py:117
  23.2 23.8 %edges.1 = (bf16[512,768]{1,0:T(8,128)(2,1)}, f32[32,768]{1,0:T(8,128)}, f32[11264,128]{1,0:T(8,128)}, bf16[11264,128]{1,0:T(8,128)(2,1)}) custom-call(s32[1]{0:T(128)} %bitcast.8.live_ref, s32[16,128]{1,0:T(8,128)} %get-tuple-element.19.src_ref, s32[16,128]{1,0:T(8,128)} %get-tuple-element.20.tgt_ref, s32[16,128]{1,0:T(8,128)} %get-tuple-element.21.rel_ref, ...), custom_call_target="tpu_custom_call" | custom-call | tf_op jit(solution)/shard_map/edges/pallas_call | solution.py:341
  47.0 71.6 %reduce_all.1 = (bf16[22528,128]{1,0:T(8,128)(2,1)}, f32[64,768]{1,0:T(8,128)}) custom-call(f32[11264,128]{1,0:T(8,128)} %get-tuple-element.24.keep_hbm, bf16[11264,128]{1,0:T(8,128)(2,1)} %get-tuple-element.25.give, bf16[2,4,64,768]{3,2,1,0:T(8,128)(2,1)} %bitcast.9), custom_call_target="tpu_custom_call" | custom-call | tf_op jit(solution)/shard_map/reduce_all/pallas_call | solution.py:594
  118.6 0.0 copy-start
  118.7 8.9 %unpack.1 = (f32[3,768,768]{2,1,0:T(8,128)}, f32[1387,768]{1,0:T(8,128)}, f32[768]{0:T(1024)}) custom-call(bf16[22528,128]{1,0:T(8,128)(2,1)} %get-tuple-element.29.full_hbm), custom_call_target="tpu_custom_call" | custom-call | tf_op jit(solution)/shard_map/unpack/pallas_call | solution.py:701
  127.5 0.0 copy-done
  127.5 0.7 copy.18
Async XLA Ops:
  118.6 8.9 %copy-start = (f32[64,768]{1,0:T(8,128)S(1)}, f32[64,768]{1,0:T(8,128)}, u32[]{:S(2)}) copy-start(f32[64,768]{1,0:T(8,128)} %get-tuple-element.38) | copy-start | bytes 589828

commit v3 on v2

--- a/solution.py
+++ b/solution.py
@@ -21,6 +21,7 @@
 PARTS = ((("x", "y", "z"), 64), (("y", "z", "x"), 64), (("z", "x", "y"), 48))
 BASES = (0, 4096, 8192)
 UNROLL = 16
+EDGE = 128
 VMEM_BYTES = 63 * 2**20
 
 
@@ -79,34 +80,37 @@
         + [me.along("y", k) for k in (1, 2, 3)]
         + [me.along("z", k) for k in (1, 2, 3)]
     )
-    hx = push(h_ref, h_all.at[x_hi, z], hx_s, hx_r, me.along("x", 2))
+    mine, theirs = h_all.at[x_hi, z], h_all.at[1 - x_hi, z]
+    hx = push(h_ref, mine, hx_s, hx_r, me.along("x", 2))
     hx.start()
-    cy = []
-    for k in (1, 2, 3):
+    cy, hz = [], []
+    for k in (1, 3, 2):
+        copy = push(h_ref, mine, hz_s.at[k - 1], hz_r.at[k - 1], me.along("z", k))
+        copy.start()
+        hz.append(copy)
         copy = push(c_ref, c_all.at[x_lo, y, core], cy_s.at[k - 1], cy_r.at[k - 1], me.along("y", k))
         copy.start()
         cy.append(copy)
-    own_h.wait()
-    own_c.wait()
     hx.wait()
-    hz = []
-    for k in (1, 2, 3):
-        copy = push(h_all.at[:, z], h_all.at[:, z], hz_s.at[k - 1], hz_r.at[k - 1], me.along("z", k))
+    for k in (1, 3, 2):
+        copy = push(theirs, theirs, hz_s.at[k + 2], hz_r.at[k + 2], me.along("z", k))
         copy.start()
         hz.append(copy)
+    own_c.wait()
     for copy in cy:
         copy.wait()
-    mine = c_all.at[x_lo, :, core]
-    theirs = c_all.at[1 - x_lo, :, core]
-    cx = push(mine, mine, cx_s, cx_r, across)
+    near = c_all.at[x_lo, :, core]
+    far = c_all.at[1 - x_lo, :, core]
+    cx = push(near, near, cx_s, cx_r, across)
     cx.start()
-    first = push(mine, mine, cs_s.at[0], cs_r.at[0], sibling)
+    first = push(near, near, cs_s.at[0], cs_r.at[0], sibling)
     first.start()
     cx.wait()
-    second = push(theirs, theirs, cs_s.at[1], cs_r.at[1], sibling)
+    second = push(far, far, cs_s.at[1], cs_r.at[1], sibling)
     second.start()
     first.wait()
     second.wait()
+    own_h.wait()
     for copy in hz:
         copy.wait()
 
@@ -124,12 +128,13 @@
         in_specs=[ANY] * 2 + [VMEM] * 4,
         out_specs=[ANY] * 2 + [VMEM] * 3,
         scratch_shapes=[
-            DMA((2,)), DMA, DMA, DMA((3,)), DMA((3,)), DMA((3,)), DMA((3,)), DMA, DMA, DMA((2,)), DMA((2,)),
+            DMA((2,)), DMA, DMA, DMA((6,)), DMA((6,)), DMA((3,)), DMA((3,)), DMA, DMA, DMA((2,)), DMA((2,)),
         ],
         compiler_params=pltpu.CompilerParams(collective_id=0, has_side_effects=True, vmem_limit_bytes=VMEM_BYTES),
         name="gather_panels",
     )(h_src, cotangent, *indices)
-    return h_all.reshape(8 * rows, width), c_all.reshape(16 * trows, width), s8, t8, r8
+    flat = [a.reshape(-1) for a in (s8, t8, r8)]
+    return h_all.reshape(8 * rows, width), c_all.reshape(16 * trows, width), *flat
 
 
 def edge_kernel(
@@ -232,16 +237,13 @@
     def row(at):
         return pl.ds(pl.multiple_of(at, 8), 8)
 
-    edge = src_ref.shape[1]
-
-    @pl.loop(0, live_ref[0] * (edge // UNROLL))
+    @pl.loop(0, live_ref[0] * (EDGE // UNROLL))
     def _(i):
-        tile = i // (edge // UNROLL)
-        start = (i % (edge // UNROLL)) * UNROLL
+        start = i * UNROLL
         for u in range(0, UNROLL, 2):
-            s0, s1 = src_ref[tile, start + u], src_ref[tile, start + u + 1]
-            t0, t1 = tgt_ref[tile, start + u], tgt_ref[tile, start + u + 1]
-            r0, r1 = rel_ref[tile, start + u], rel_ref[tile, start + u + 1]
+            s0, s1 = src_ref[start + u], src_ref[start + u + 1]
+            t0, t1 = tgt_ref[start + u], tgt_ref[start + u + 1]
+            r0, r1 = rel_ref[start + u], rel_ref[start + u + 1]
             h0, h1 = hx[row(s0), :], hx[row(s1), :]
             p0, p1 = px[row(t0), :], px[row(t1), :]
             z0, z1 = zx[row(r0), :], zx[row(r1), :]
@@ -406,6 +408,71 @@
     own_g.start()
     greet([me.along(axis, k) for axis in ("x", "y", "z") for k in (1, 2, 3)] + [sibling])
 
+    pairs = {}
+    for p, j in order:
+        where = rows_of(p, (first(p) + j) % 4)
+        copy = push(give.at[where], pair.at[where], pair_s.at[p * 4 + j], pair_r.at[p * 4 + j], sibling)
+        copy.start()
+        pairs[p, j] = copy
+
+    step1 = {}
+    for j in (1, 2, 3):
+        for p in range(3):
+            axis, unit_rows = PARTS[p][0][0], PARTS[p][1]
+            base = BASES[p] + ((first(p) + j) % 4) * (unit_rows * 16)
+            keeps[p, j].wait()
+            pairs[p, j].wait_recv()
+
+            @pl.loop(0, unit_rows * 16 // 128)
+            def _(i, base=base):
+                r = pl.ds(pl.multiple_of(base + i * 128, 16), 128)
+                out1[r, :] = (keep[r, :] + pair[r, :].astype(F32)).astype(BF16)
+
+            where = rows_of(p, (first(p) + j) % 4)
+            copy = push(
+                out1.at[where],
+                in1.at[j - 1, pl.ds(BASES[p] // 4, unit_rows * 16)],
+                s1.at[p * 3 + j - 1],
+                r1.at[p * 3 + j - 1],
+                me.along(axis, j),
+            )
+            copy.start()
+            step1[p, j] = copy
+
+    step2 = {}
+    for p in range(3):
+        axis, unit_rows = PARTS[p][0][1], PARTS[p][1]
+        base = BASES[p] + first(p) * (unit_rows * 16)
+        low = BASES[p] // 4
+        keeps[p, 0].wait()
+        pairs[p, 0].wait_recv()
+        for j in (1, 2, 3):
+            step1[p, j].wait_recv()
+
+        @pl.loop(0, unit_rows * 16 // 128)
+        def _(i, base=base, low=low):
+            r = pl.ds(pl.multiple_of(base + i * 128, 16), 128)
+            q = pl.ds(pl.multiple_of(low + i * 128, 16), 128)
+            acc1[q, :] = (
+                keep[r, :]
+                + pair[r, :].astype(F32)
+                + in1[0, q, :].astype(F32)
+                + in1[1, q, :].astype(F32)
+                + in1[2, q, :].astype(F32)
+            )
+
+        for j in (1, 2, 3):
+            where = pl.ds(pl.multiple_of(low + ((second(p) + j) % 4) * (unit_rows * 4), 16), unit_rows * 4)
+            copy = push(
+                acc1.at[where],
+                in2.at[j - 1, pl.ds(BASES[p] // 16, unit_rows * 4)],
+                s2.at[p * 3 + j - 1],
+                r2.at[p * 3 + j - 1],
+                me.along(axis, j),
+            )
+            copy.start()
+            step2[p, j] = copy
+
     gz = []
     for k in (1, 2, 3):
         copy = push(
@@ -414,36 +481,55 @@
         copy.start()
         gz.append(copy)
 
-    pairs = {}
-    for p, j in order:
-        where = rows_of(p, (first(p) + j) % 4)
-        copy = push(give.at[where], pair.at[where], pair_s.at[p * 4 + j], pair_r.at[p * 4 + j], sibling)
-        copy.start()
-        pairs[p, j] = copy
-
-    step1 = {}
-    for j in (1, 2, 3):
-        for p in range(3):
-            axis, unit_rows = PARTS[p][0][0], PARTS[p][1]
-            base = BASES[p] + ((first(p) + j) % 4) * (unit_rows * 16)
-            keeps[p, j].wait()
-            pairs[p, j].wait_recv()
-
-            @pl.loop(0, unit_rows * 16 // 128)
-            def _(i, base=base):
-                r = pl.ds(pl.multiple_of(base + i * 128, 16), 128)
-                out1[r, :] = (keep[r, :] + pair[r, :].astype(F32)).astype(BF16)
-
-            where = rows_of(p, (first(p) + j) % 4)
+    step3 = {}
+    for p in range(3):
+        axis, unit_rows = PARTS[p][0][2], PARTS[p][1]
+        for j in (1, 2, 3):
+            step2[p, j].wait_recv()
+        size = unit_rows * 4
+        q = pl.ds(BASES[p] // 16, size)
+        mine = pl.ds(pl.multiple_of(BASES[p] // 4 + second(p) * size, 16), size)
+        acc2[q, :] = acc1[mine, :] + in2[0, q, :] + in2[1, q, :] + in2[2, q, :]
+        for j in (1, 2, 3):
+            where = pl.ds(
+                pl.multiple_of(BASES[p] // 16 + ((third(p) + j) % 4) * unit_rows, 16), unit_rows
+            )
             copy = push(
-                out1.at[where],
-                in1.at[j - 1, pl.ds(BASES[p] // 4, unit_rows * 16)],
-                s1.at[p * 3 + j - 1],
-                r1.at[p * 3 + j - 1],
+                acc2.at[where],
+                in3.at[j - 1, pl.ds(BASES[p] // 64, unit_rows)],
+                s3.at[p * 3 + j - 1],
+                r3.at[p * 3 + j - 1],
                 me.along(axis, j),
             )
             copy.start()
-            step1[p, j] = copy
+            step3[p, j] = copy
+
+    def place(p, depth):
+        unit_rows = PARTS[p][1]
+        row = core * HALF_ROWS + BASES[p] + first(p) * (unit_rows * 16)
+        if depth > 1:
+            row = row + second(p) * (unit_rows * 4)
+        if depth > 2:
+            row = row + third(p) * unit_rows
+        size = (unit_rows * 16, unit_rows * 4, unit_rows)[depth - 1]
+        return pl.ds(pl.multiple_of(row, 16), size)
+
+    step4, own = {}, {}
+    for p in range(3):
+        axis, unit_rows = PARTS[p][0][2], PARTS[p][1]
+        for j in (1, 2, 3):
+            step3[p, j].wait_recv()
+        q = pl.ds(BASES[p] // 64, unit_rows)
+        mine = pl.ds(pl.multiple_of(BASES[p] // 16 + third(p) * unit_rows, 16), unit_rows)
+        unit[q, :] = (acc2[mine, :] + in3[0, q, :] + in3[1, q, :] + in3[2, q, :]).astype(BF16)
+        own[p] = pltpu.make_async_copy(unit.at[q], full.at[place(p, 3)], local.at[p])
+        own[p].start()
+        for j in (1, 2, 3):
+            copy = push(
+                unit.at[q], full.at[place(p, 3)], s4.at[p * 3 + j - 1], r4.at[p * 3 + j - 1], me.along(axis, j)
+            )
+            copy.start()
+            step4[p, j] = copy
 
     own_g.wait()
     for copy in gz:
@@ -458,90 +544,6 @@
     gx = push(g_acc.at[1 - x_hi], g_side, gx_s, gx_r, me.along("x", 2))
     gx.start()
 
-    step2 = {}
-    for p in range(3):
-        axis, unit_rows = PARTS[p][0][1], PARTS[p][1]
-        base = BASES[p] + first(p) * (unit_rows * 16)
-        low = BASES[p] // 4
-        keeps[p, 0].wait()
-        pairs[p, 0].wait_recv()
-        for j in (1, 2, 3):
-            step1[p, j].wait_recv()
-
-        @pl.loop(0, unit_rows * 16 // 128)
-        def _(i, base=base, low=low):
-            r = pl.ds(pl.multiple_of(base + i * 128, 16), 128)
-            q = pl.ds(pl.multiple_of(low + i * 128, 16), 128)
-            acc1[q, :] = (
-                keep[r, :]
-                + pair[r, :].astype(F32)
-                + in1[0, q, :].astype(F32)
-                + in1[1, q, :].astype(F32)
-                + in1[2, q, :].astype(F32)
-            )
-
-        for j in (1, 2, 3):
-            where = pl.ds(pl.multiple_of(low + ((second(p) + j) % 4) * (unit_rows * 4), 16), unit_rows * 4)
-            copy = push(
-                acc1.at[where],
-                in2.at[j - 1, pl.ds(BASES[p] // 16, unit_rows * 4)],
-                s2.at[p * 3 + j - 1],
-                r2.at[p * 3 + j - 1],
-                me.along(axis, j),
-            )
-            copy.start()
-            step2[p, j] = copy
-
-    step3 = {}
-    for p in range(3):
-        axis, unit_rows = PARTS[p][0][2], PARTS[p][1]
-        for j in (1, 2, 3):
-            step2[p, j].wait_recv()
-        size = unit_rows * 4
-        q = pl.ds(BASES[p] // 16, size)
-        mine = pl.ds(pl.multiple_of(BASES[p] // 4 + second(p) * size, 16), size)
-        acc2[q, :] = acc1[mine, :] + in2[0, q, :] + in2[1, q, :] + in2[2, q, :]
-        for j in (1, 2, 3):
-            where = pl.ds(
-                pl.multiple_of(BASES[p] // 16 + ((third(p) + j) % 4) * unit_rows, 16), unit_rows
-            )
-            copy = push(
-                acc2.at[where],
-                in3.at[j - 1, pl.ds(BASES[p] // 64, unit_rows)],
-                s3.at[p * 3 + j - 1],
-                r3.at[p * 3 + j - 1],
-                me.along(axis, j),
-            )
-            copy.start()
-            step3[p, j] = copy
-
-    def place(p, depth):
-        unit_rows = PARTS[p][1]
-        row = core * HALF_ROWS + BASES[p] + first(p) * (unit_rows * 16)
-        if depth > 1:
-            row = row + second(p) * (unit_rows * 4)
-        if depth > 2:
-            row = row + third(p) * unit_rows
-        size = (unit_rows * 16, unit_rows * 4, unit_rows)[depth - 1]
-        return pl.ds(pl.multiple_of(row, 16), size)
-
-    step4, own = {}, {}
-    for p in range(3):
-        axis, unit_rows = PARTS[p][0][2], PARTS[p][1]
-        for j in (1, 2, 3):
-            step3[p, j].wait_recv()
-        q = pl.ds(BASES[p] // 64, unit_rows)
-        mine = pl.ds(pl.multiple_of(BASES[p] // 16 + third(p) * unit_rows, 16), unit_rows)
-        unit[q, :] = (acc2[mine, :] + in3[0, q, :] + in3[1, q, :] + in3[2, q, :]).astype(BF16)
-        own[p] = pltpu.make_async_copy(unit.at[q], full.at[place(p, 3)], local.at[p])
-        own[p].start()
-        for j in (1, 2, 3):
-            copy = push(
-                unit.at[q], full.at[place(p, 3)], s4.at[p * 3 + j - 1], r4.at[p * 3 + j - 1], me.along(axis, j)
-            )
-            copy.start()
-            step4[p, j] = copy
-
     step5 = {}
     for p in range(3):
         own[p].wait()
@@ -553,29 +555,49 @@
             copy.start()
             step5[p, j] = copy
 
+    def half_of(p, offset, half):
+        size = PARTS[p][1] * 8
+        row = core * HALF_ROWS + BASES[p] + ((first(p) + 4 + offset) % 4) * (2 * size) + half * size
+        return full.at[pl.ds(pl.multiple_of(row, 16), size)]
+
     step6, side = {}, {}
     for p in range(3):
         for j in (1, 2, 3):
             step5[p, j].wait_recv()
+        for n, (to, half) in enumerate(((1, 0), (3, 1), (1, 1), (3, 0))):
+            block = half_of(p, 0, half)
+            copy = push(block, block, s6.at[p * 6 + n], r6.at[p * 6 + n], me.along(PARTS[p][0][0], to))
+            copy.start()
+            step6[p, n] = copy
         block = full.at[place(p, 1)]
-        for j in (1, 2, 3):
-            copy = push(block, block, s6.at[p * 3 + j - 1], r6.at[p * 3 + j - 1], me.along(PARTS[p][0][0], j))
+        side[p, 0] = push(block, block, sib_s.at[p * 7], sib_r.at[p * 7], sibling)
+        side[p, 0].start()
+
+    def across(p, n, offset, half):
+        block = half_of(p, offset, half)
+        side[p, n] = push(block, block, sib_s.at[p * 7 + n], sib_r.at[p * 7 + n], sibling)
+        side[p, n].start()
+
+    for p in range(3):
+        for n, (to, half) in enumerate(((1, 0), (3, 1))):
+            step6[p, n].wait_recv()
+            block = half_of(p, -to, half)
+            copy = push(block, block, s6.at[p * 6 + 4 + n], r6.at[p * 6 + 4 + n], me.along(PARTS[p][0][0], to))
             copy.start()
-            step6[p, j] = copy
-        side[p, 0] = push(block, block, sib_s.at[p * 4], sib_r.at[p * 4], sibling)
-        side[p, 0].start()
+            step6[p, 4 + n] = copy
+            across(p, 1 + n, -to, half)
 
     gx.wait_recv()
     g_out[...] = g_acc[x_hi] + g_side[...]
 
-    for j in (1, 3, 2):
-        for p in range(3):
-            size = PARTS[p][1] * 16
-            step6[p, j].wait_recv()
-            row = core * HALF_ROWS + BASES[p] + ((first(p) + 4 - j) % 4) * size
-            block = full.at[pl.ds(pl.multiple_of(row, 16), size)]
-            side[p, j] = push(block, block, sib_s.at[p * 4 + j], sib_r.at[p * 4 + j], sibling)
-            side[p, j].start()
+    for p in range(3):
+        for n, (to, half) in enumerate(((1, 1), (3, 0))):
+            step6[p, 2 + n].wait_recv()
+            across(p, 3 + n, -to, half)
+    for p in range(3):
+        for half in range(2):
+            step6[p, 4 + half].wait_recv()
+            across(p, 5 + half, 2, half)
 
     for copy in side.values():
         copy.wait_recv()
@@ -614,8 +636,8 @@
             pltpu.VMEM((2, rows // 8, width), F32),
             pltpu.VMEM((rows // 8, width), F32),
             DMA((12,)), DMA((12,)),
-            *[DMA((9,)) for _ in range(12)],
-            DMA((12,)), DMA((12,)), DMA((3,)), DMA((3,)), DMA, DMA, DMA((3,)), DMA((13,)),
+            *[DMA((9,)) for _ in range(10)],
+            *[DMA((18,))] * 2, *[DMA((21,))] * 2, DMA((3,)), DMA((3,)), DMA, DMA, DMA((3,)), DMA((13,)),
         ],
         compiler_params=pltpu.CompilerParams(
             collective_id=1, has_side_effects=True, vmem_limit_bytes=VMEM_BYTES

time: 128 us -> 125 us (0.977)
  Pallas kernels: 126 us -> 123 us
    pallas_call x1, Pallas kernels: 22 us -> 20.2 us  [gather(): pl.pallas_call(gather_kernel, out_shape=(jax.ShapeDtypeStruct((2, 4, rows...]
where the time goes in v3:
time: 125 us
  Pallas kernels  123 us (98%)
  between operations  1.33 us (1%)
    pallas_call x1, Pallas kernels, reduce_all(): pl.pallas_call(reduce_kernel, out_shape=(jax.ShapeDtypeStruct((2 * HALF_R...  70.8 us
    pallas_call x1, Pallas kernels, edges(): pl.pallas_call(edge_kernel, out_shape=(jax.ShapeDtypeStruct((rows, width)...  23 us
    pallas_call x1, Pallas kernels, gather(): pl.pallas_call(gather_kernel, out_shape=(jax.ShapeDtypeStruct((2, 4, rows...  20.2 us
    pallas_call x1, Pallas kernels, unpack(): pl.pallas_call(functools.partial(unpack_kernel, **scales), out_shape=(jax...  8.86 us

profile of v3, /device:TPU:1, one launch (start us, length us, event | category | flops | bytes accessed | tf_op | source)
XLA Modules:
  0.0 124.9 jit_solution(3048171555546328314)
XLA Ops:
  1.3 20.2 %gather_panels.1 = (bf16[2,4,64,768]{3,2,1,0:T(8,128)(2,1)}, bf16[2,4,2,32,768]{4,3,2,1,0:T(8,128)(2,1)}, s32[16,128]{1,0:T(8,128)}, s32[16,128]{1,0:T(8,128)}, s32[16,128]{1,0:T(8,128)}) custom-call(bf16[64,768]{1,0:T(8,128)(2,1)} %h_ref.1, bf16[32,768]{1,0:T(8,128)(2,1)} %own_c.1, s32[16,128]{1,0:T(8,128)} %bitcast.15, s32[16,128]{1,0:T(8,128)} %bitcast.16, ...), custom_call_target="tpu_custom_call" | custom-call | tf_op jit(solution)/shard_map/gather_panels/pallas_call | solution.py:121
  21.5 23.0 %edges.1 = (bf16[512,768]{1,0:T(8,128)(2,1)}, f32[32,768]{1,0:T(8,128)}, f32[11264,128]{1,0:T(8,128)}, bf16[11264,128]{1,0:T(8,128)(2,1)}) custom-call(s32[1]{0:T(128)} %bitcast.11.live_ref, s32[2048]{0:T(1024)} %bitcast.19, s32[2048]{0:T(1024)} %bitcast.20, s32[2048]{0:T(1024)} %bitcast.21, bf16[512,768]{1,0:T(8,128)(2,1)} %bitcast.13, ...), custom_call_target="tpu_custom_call" | custom-call | tf_op jit(solution)/shard_map/edges/pallas_call | solution.py:343
  44.5 70.8 %reduce_all.1 = (bf16[22528,128]{1,0:T(8,128)(2,1)}, f32[64,768]{1,0:T(8,128)}) custom-call(f32[11264,128]{1,0:T(8,128)} %get-tuple-element.24.keep_hbm, bf16[11264,128]{1,0:T(8,128)(2,1)} %get-tuple-element.25.give, bf16[2,4,64,768]{3,2,1,0:T(8,128)(2,1)} %bitcast.12), custom_call_target="tpu_custom_call" | custom-call | tf_op jit(solution)/shard_map/reduce_all/pallas_call | solution.py:616
  115.3 0.0 copy-start
  115.3 8.9 %unpack.1 = (f32[3,768,768]{2,1,0:T(8,128)}, f32[1387,768]{1,0:T(8,128)}, f32[768]{0:T(1024)}) custom-call(bf16[22528,128]{1,0:T(8,128)(2,1)} %get-tuple-element.29.full_hbm), custom_call_target="tpu_custom_call" | custom-call | tf_op jit(solution)/shard_map/unpack/pallas_call | solution.py:723
  124.2 0.0 copy-done
  124.2 0.7 copy.18
Async XLA Ops:
  115.3 8.9 %copy-start = (f32[64,768]{1,0:T(8,128)S(1)}, f32[64,768]{1,0:T(8,128)}, u32[]{:S(2)}) copy-start(f32[64,768]{1,0:T(8,128)} %get-tuple-element.38) | copy-start | bytes 589828

commit v4 on v3

v4 whole, which is shorter than its diff:
```python
import functools

import jax
import jax.numpy as jnp
from jax import lax
from jax.experimental import pallas as pl
from jax.experimental.pallas import tpu as pltpu
from jax.sharding import PartitionSpec as P

F32 = jnp.float32
BF16 = jnp.bfloat16
MESH = pl.DeviceIdType.MESH
ANY = pl.BlockSpec(memory_space=pl.ANY)
VMEM = pl.BlockSpec(memory_space=pltpu.VMEM)
SMEM = pl.BlockSpec(memory_space=pltpu.SMEM)
DMA = pltpu.SemaphoreType.DMA

WAVE_HALF = (4096, 7168)
HALF_ROWS = sum(WAVE_HALF)
FIRST_TILES = 2 * WAVE_HALF[0] // 16
SECOND_HALF_TILES = WAVE_HALF[1] // 16
W_TILES = 864
PARTS = (
    (("x", "y", "z"), 32),
    (("y", "z", "x"), 32),
    (("x", "y", "z"), 32),
    (("y", "z", "x"), 32),
    (("z", "x", "y"), 48),
)
BASES = (0, 2048, 4096, 6144, 8192)
UNROLL = 16
EDGE = 128
VMEM_BYTES = 63 * 2**20


class Place:
    def __init__(self):
        s, t = lax.axis_index("src"), lax.axis_index("tgt")
        self.x_lo, self.core = s // 8, s % 2
        self.x_hi = t // 4
        self.at = {"x": self.x_hi * 2 + self.x_lo, "y": (s // 2) % 4, "z": t % 4}

    def device(self, at, core):
        return ((at["x"] % 2) * 8 + at["y"] * 2 + core, (at["x"] // 2) * 4 + at["z"])

    def along(self, axis, offset):
        at = dict(self.at)
        at[axis] = (at[axis] + offset) % 4
        return self.device(at, self.core)

    def sibling(self):
        return self.device(self.at, 1 - self.core)

    def x_lo_partner(self):
        at = dict(self.at)
        at["x"] = self.x_hi * 2 + (1 - self.x_lo)
        return self.device(at, self.core)


def greet(partners):
    barrier = pltpu.get_barrier_semaphore()
    for partner in partners:
        pl.semaphore_signal(barrier, inc=1, device_id=partner, device_id_type=MESH)
    pl.semaphore_wait(barrier, len(partners))


def push(src, dst, send, recv, device):
    return pltpu.make_async_remote_copy(
        src_ref=src, dst_ref=dst, send_sem=send, recv_sem=recv, device_id=device, device_id_type=MESH
    )


def gather_kernel(
    h_ref, c_ref, src_ref, tgt_ref, rel_ref, dir_ref, h_all, c_all, s8, t8, r8, local, hx_s, hx_r, hz_s, hz_r, cy_s, cy_r, cx_s, cx_r, cs_s, cs_r
):
    me = Place()
    x_lo, x_hi, core, y, z = me.x_lo, me.x_hi, me.core, me.at["y"], me.at["z"]
    sibling, across = me.sibling(), me.x_lo_partner()
    own_h = pltpu.make_async_copy(h_ref, h_all.at[x_hi, z], local.at[0])
    own_c = pltpu.make_async_copy(c_ref, c_all.at[x_lo, y, core], local.at[1])
    own_h.start()
    own_c.start()
    s8[...] = src_ref[...] * 8
    t8[...] = (tgt_ref[...] + dir_ref[...] * (16 * c_ref.shape[0])) * 8
    r8[...] = rel_ref[...] * 8
    greet(
        [me.along("x", 2), across, sibling]
        + [me.along("y", k) for k in (1, 2, 3)]
        + [me.along("z", k) for k in (1, 2, 3)]
    )
    mine, theirs = h_all.at[x_hi, z], h_all.at[1 - x_hi, z]
    hx = push(h_ref, mine, hx_s, hx_r, me.along("x", 2))
    hx.start()
    cy, hz = [], []
    for k in (1, 3, 2):
        copy = push(h_ref, mine, hz_s.at[k - 1], hz_r.at[k - 1], me.along("z", k))
        copy.start()
        hz.append(copy)
        copy = push(c_ref, c_all.at[x_lo, y, core], cy_s.at[k - 1], cy_r.at[k - 1], me.along("y", k))
        copy.start()
        cy.append(copy)
    hx.wait()
    for k in (1, 3, 2):
        copy = push(theirs, theirs, hz_s.at[k + 2], hz_r.at[k + 2], me.along("z", k))
        copy.start()
        hz.append(copy)
    own_c.wait()
    for copy in cy:
        copy.wait()
    near = c_all.at[x_lo, :, core]
    far = c_all.at[1 - x_lo, :, core]
    cx = push(near, near, cx_s, cx_r, across)
    cx.start()
    first = push(near, near, cs_s.at[0], cs_r.at[0], sibling)
    first.start()
    cx.wait()
    second = push(far, far, cs_s.at[1], cs_r.at[1], sibling)
    second.start()
    first.wait()
    second.wait()
    own_h.wait()
    for copy in hz:
        copy.wait()


def gather(h_src, cotangent, *indices):
    rows, width = h_src.shape
    trows = cotangent.shape[0]
    h_all, c_all, s8, t8, r8 = pl.pallas_call(
        gather_kernel,
        out_shape=(
            jax.ShapeDtypeStruct((2, 4, rows, width), BF16),
            jax.ShapeDtypeStruct((2, 4, 2, trows, width), BF16),
            *[jax.ShapeDtypeStruct(indices[0].shape, jnp.int32)] * 3,
        ),
        in_specs=[ANY] * 2 + [VMEM] * 4,
        out_specs=[ANY] * 2 + [VMEM] * 3,
        scratch_shapes=[
            DMA((2,)), DMA, DMA, DMA((6,)), DMA((6,)), DMA((3,)), DMA((3,)), DMA, DMA, DMA((2,)), DMA((2,)),
        ],
        compiler_params=pltpu.CompilerParams(collective_id=0, has_side_effects=True, vmem_limit_bytes=VMEM_BYTES),
        name="gather_panels",
    )(h_src, cotangent, *indices)
    flat = [a.reshape(-1) for a in (s8, t8, r8)]
    return h_all.reshape(8 * rows, width), c_all.reshape(16 * trows, width), *flat


def edge_kernel(
    live_ref, src_ref, tgt_ref, rel_ref, h_hbm, c_hbm, w_hbm, z_hbm, own_c, own_h, loop_ref,
    g_out, t_out, hi_out, lo_out, rest_out, keep_out, give_out,
    h_ref, c_ref, w_ref, z_ref, g_ref, keep, give, hx, px, zx, gs, aa, rr, hi, lo, in_sem, out_sem,
):
    loads = [
        pltpu.make_async_copy(a, b, in_sem.at[i])
        for i, (a, b) in enumerate(((h_hbm, h_ref), (z_hbm, z_ref), (c_hbm, c_ref), (w_hbm, w_ref)))
    ]
    for load in loads:
        load.start()
    core = lax.axis_index("src") % 2
    rows = h_ref.shape[0]
    trows = c_ref.shape[0]
    rels, width = z_ref.shape
    chunks = width // 128

    def spread(dst, row, value):
        for c in range(chunks):
            dst[pl.ds(row * 8 + c, value.shape[0], stride=8), :] = value[:, c * 128 : (c + 1) * 128]

    zero = jnp.zeros((64, 128), F32)
    for ref in (gs, aa, rr):

        @pl.loop(0, ref.shape[0] // 64)
        def _(i, ref=ref):
            ref[pl.ds(pl.multiple_of(i * 64, 64), 64), :] = zero

    loads[0].wait()

    @pl.loop(0, rows // 16)
    def _(i):
        r = pl.multiple_of(i * 16, 16)
        spread(hx, r, h_ref[pl.ds(r, 16), :].astype(F32))

    loads[1].wait()

    @pl.loop(0, rels // 16)
    def _(i):
        r = pl.multiple_of(i * 16, 16)
        spread(zx, r, z_ref[pl.ds(r, 16), :].astype(F32))

    tail = rels // 16 * 16
    if tail < rels:
        spread(zx, tail, z_ref[tail:rels, :].astype(F32))
    loads[2].wait()
    loads[3].wait()
    for d in range(2):
        for k in range(width // 256):
            p = lax.dot_general(
                c_ref[...], w_ref[d, k * 256 : (k + 1) * 256, :], (((1,), (1,)), ((), ())),
                preferred_element_type=F32,
            )
            for h in range(2):
                px[pl.ds(d * trows * 8 + 2 * k + h, trows, stride=8), :] = p[:, h * 128 : (h + 1) * 128]
    def row(at):
        return pl.ds(pl.multiple_of(at, 8), 8)

    @pl.loop(0, live_ref[0] * (EDGE // UNROLL))
    def _(i):
        start = i * UNROLL
        for u in range(0, UNROLL, 2):
            s0, s1 = src_ref[start + u], src_ref[start + u + 1]
            t0, t1 = tgt_ref[start + u], tgt_ref[start + u + 1]
            r0, r1 = rel_ref[start + u], rel_ref[start + u + 1]
            h0, h1 = hx[row(s0), :], hx[row(s1), :]
            p0, p1 = px[row(t0), :], px[row(t1), :]
            z0, z1 = zx[row(r0), :], zx[row(r1), :]
            for ref, at0, at1, v0, v1 in (
                (gs, s0, s1, p0 * z0, p1 * z1),
                (aa, t0, t1, (h0 * z0).astype(BF16).astype(F32), (h1 * z1).astype(BF16).astype(F32)),
                (rr, r0, r1, p0 * h0, p1 * h1),
            ):
                sum0 = ref[row(at0), :] + v0
                sum1 = ref[row(at1), :] + v1 + jnp.where(at0 == at1, v0, jnp.zeros_like(v0))
                ref[row(at0), :] = sum0
                ref[row(at1), :] = sum1

    loop_wide = loop_ref[...].astype(F32).reshape(1, width)
    h_wide = own_h[...].astype(F32)
    back = lax.dot_general(
        own_c[...], w_ref[2], (((1,), (1,)), ((), ())), preferred_element_type=F32
    )
    t_out[...] = back * loop_wide
    lsum = jnp.sum(back * h_wide, axis=0, keepdims=True)
    for c in range(chunks):
        rr[rels * 8 + c : rels * 8 + c + 1, :] = lsum[:, c * 128 : (c + 1) * 128]
    blocks = rr.shape[0] // 128

    def rel_tile(block, c):
        return rr[pl.ds(block * 128 + c, 16, stride=8), :]

    def collect(half, ref):
        first = half * (FIRST_TILES // 2)
        last = first + FIRST_TILES // 2

        @pl.loop(-(-first // chunks), last // chunks)
        def _(i):
            for c in range(chunks):
                row = pl.multiple_of((i * chunks + c - first) * 16, 16)
                ref[pl.ds(row, 16), :] = rel_tile(i, c).astype(ref.dtype)

        edge_tiles = [*range(first, -(-first // chunks) * chunks), *range(last // chunks * chunks, last)]
        for t in edge_tiles:
            row = (t - first) * 16
            ref[row : row + 16, :] = rel_tile(t // chunks, t % chunks).astype(ref.dtype)

    @pl.when(core == 0)
    def _():
        collect(0, keep)
        collect(1, give)

    @pl.when(core != 0)
    def _():
        collect(1, keep)
        collect(0, give)

    stores = [
        pltpu.make_async_copy(keep, keep_out, out_sem.at[0]),
        pltpu.make_async_copy(give, give_out, out_sem.at[1]),
    ]
    for store in stores:
        store.start()
    for t in range(FIRST_TILES, blocks * chunks):
        row = (t - FIRST_TILES) * 16
        rest_out[row : row + 16, :] = rel_tile(t // chunks, t % chunks)

    @pl.loop(0, 2 * trows // 16)
    def _(i):
        r = pl.multiple_of(i * 16, 16)
        for c in range(chunks):
            a = aa[pl.ds(r * 8 + c, 16, stride=8), :]
            top = a.astype(BF16)
            hi[pl.ds(r, 16), c * 128 : (c + 1) * 128] = top
            lo[pl.ds(r, 16), c * 128 : (c + 1) * 128] = (a - top.astype(F32)).astype(BF16)

    stores.append(pltpu.make_async_copy(hi, hi_out, out_sem.at[2]))
    stores.append(pltpu.make_async_copy(lo, lo_out, out_sem.at[3]))
    stores[2].start()
    stores[3].start()

    @pl.loop(0, rows // 16)
    def _(i):
        r = pl.multiple_of(i * 16, 16)
        for c in range(chunks):
            g_ref[pl.ds(r, 16), c * 128 : (c + 1) * 128] = gs[pl.ds(r * 8 + c, 16, stride=8), :].astype(BF16)

    stores.append(pltpu.make_async_copy(g_ref, g_out, out_sem.at[4]))
    stores[4].start()
    for store in stores:
        store.wait()


def edges(live, s8, t8, r8, h, c, w, z, own_c, own_h, loop):
    rows, width = h.shape
    trows = c.shape[0]
    rpad = (z.shape[0] + 16) // 16 * 16
    return pl.pallas_call(
        edge_kernel,
        out_shape=(
            jax.ShapeDtypeStruct((rows, width), BF16),
            jax.ShapeDtypeStruct((own_c.shape[0], width), F32),
            jax.ShapeDtypeStruct((2 * trows, width), BF16),
            jax.ShapeDtypeStruct((2 * trows, width), BF16),
            jax.ShapeDtypeStruct((rpad // 16 * (width // 128) * 16 - FIRST_TILES * 16, 128), F32),
            jax.ShapeDtypeStruct((WAVE_HALF[0], 128), F32),
            jax.ShapeDtypeStruct((WAVE_HALF[0], 128), BF16),
        ),
        in_specs=[SMEM] * 4 + [ANY] * 4 + [VMEM] * 3,
        out_specs=[ANY, VMEM, ANY, ANY, VMEM, ANY, ANY],
        scratch_shapes=[
            pltpu.VMEM(h.shape, BF16),
            pltpu.VMEM(c.shape, BF16),
            pltpu.VMEM(w.shape, BF16),
            pltpu.VMEM(z.shape, BF16),
            pltpu.VMEM((rows, width), BF16),
            pltpu.VMEM((WAVE_HALF[0], 128), F32),
            pltpu.VMEM((WAVE_HALF[0], 128), BF16),
            pltpu.VMEM((rows * 8, 128), F32),
            pltpu.VMEM((2 * trows * 8, 128), F32),
            pltpu.VMEM((rpad * 8, 128), F32),
            pltpu.VMEM((rows * 8, 128), F32),
            pltpu.VMEM((2 * trows * 8, 128), F32),
            pltpu.VMEM((rpad * 8, 128), F32),
            pltpu.VMEM((2 * trows, width), BF16),
            pltpu.VMEM((2 * trows, width), BF16),
            DMA((4,)),
            DMA((5,)),
        ],
        compiler_params=pltpu.CompilerParams(vmem_limit_bytes=VMEM_BYTES),
        name="edges",
    )(live, s8, t8, r8, h, c, w, z, own_c, own_h, loop)


def reduce_kernel(
    keep_hbm, give, g_ref, hi_hbm, lo_hbm, c_hbm, rest, own_c, own_h, loop_ref, full, g_out,
    keep, given, hi, lo, c_all, g_own, pair, out1, in1, acc1, in2, acc2, in3, unit, g_in, g_acc, g_side,
    pair_s, pair_r, s1, r1, s2, r2, s3, r3, s4, r4, s5, r5, s6, r6, sib_s, sib_r, gz_s, gz_r, gx_s, gx_r,
    local, kept,
):
    me = Place()
    core = me.core
    sibling = me.sibling()
    x_hi, z = me.x_hi, me.at["z"]
    width = c_all.shape[1]
    trows = c_all.shape[0]
    chunks = width // 128
    parts = range(len(PARTS))

    def at(p, depth):
        return me.at[PARTS[p][0][depth]]

    def along(p, depth, j):
        return me.along(PARTS[p][0][depth], j)

    def rows_of(p, a):
        size = PARTS[p][1] * 16
        return pl.ds(pl.multiple_of(BASES[p] + a * size, 16), size)

    first_rows = pl.ds(0, WAVE_HALF[0])
    loads = [
        pltpu.make_async_copy(a, b, kept.at[n])
        for n, (a, b) in enumerate(
            (
                (keep_hbm, keep.at[first_rows]),
                (hi_hbm, hi),
                (c_hbm, c_all),
                (lo_hbm, lo),
                (g_ref.at[:, z], g_own),
            )
        )
    ]
    for load in loads:
        load.start()
    greet([me.along(axis, k) for axis in ("x", "y", "z") for k in (1, 2, 3)] + [sibling])

    pairs, step1, step2, step3, step4, step5, step6, side, own = {}, {}, {}, {}, {}, {}, {}, {}, {}

    def send_pair(some):
        for j in (1, 2, 3, 0):
            for p in some:
                where = rows_of(p, (at(p, 0) + j) % 4)
                if BASES[p] < WAVE_HALF[0]:
                    source = give.at[where]
                else:
                    row = BASES[p] - WAVE_HALF[0] + ((at(p, 0) + j) % 4) * (PARTS[p][1] * 16)
                    source = given.at[pl.ds(pl.multiple_of(row, 16), PARTS[p][1] * 16)]
                copy = push(source, pair.at[where], pair_s.at[p * 4 + j], pair_r.at[p * 4 + j], sibling)
                copy.start()
                pairs[p, j] = copy

    def send_first(some):
        for j in (1, 2, 3):
            for p in some:
                size = PARTS[p][1] * 16
                base = BASES[p] + ((at(p, 0) + j) % 4) * size
                pairs[p, j].wait_recv()

                @pl.loop(0, size // 128)
                def _(i, base=base):
                    r = pl.ds(pl.multiple_of(base + i * 128, 16), 128)
                    out1[r, :] = (keep[r, :] + pair[r, :].astype(F32)).astype(BF16)

                copy = push(
                    out1.at[rows_of(p, (at(p, 0) + j) % 4)],
                    in1.at[j - 1, pl.ds(BASES[p] // 4, size)],
                    s1.at[p * 3 + j - 1],
                    r1.at[p * 3 + j - 1],
                    along(p, 0, j),
                )
                copy.start()
                step1[p, j] = copy

    def send_second(p):
        size = PARTS[p][1] * 4
        base = BASES[p] + at(p, 0) * (size * 4)
        low = BASES[p] // 4
        pairs[p, 0].wait_recv()
        for j in (1, 2, 3):
            step1[p, j].wait_recv()

        @pl.loop(0, size * 4 // 128)
        def _(i):
            r = pl.ds(pl.multiple_of(base + i * 128, 16), 128)
            q = pl.ds(pl.multiple_of(low + i * 128, 16), 128)
            acc1[q, :] = (
                keep[r, :]
                + pair[r, :].astype(F32)
                + in1[0, q, :].astype(F32)
                + in1[1, q, :].astype(F32)
                + in1[2, q, :].astype(F32)
            )

        for j in (1, 2, 3):
            where = pl.ds(pl.multiple_of(low + ((at(p, 1) + j) % 4) * size, 16), size)
            copy = push(
                acc1.at[where],
                in2.at[j - 1, pl.ds(BASES[p] // 16, size)],
                s2.at[p * 3 + j - 1],
                r2.at[p * 3 + j - 1],
                along(p, 1, j),
            )
            copy.start()
            step2[p, j] = copy

    def send_third(p):
        size = PARTS[p][1]
        for j in (1, 2, 3):
            step2[p, j].wait_recv()
        q = pl.ds(BASES[p] // 16, size * 4)
        mine = pl.ds(pl.multiple_of(BASES[p] // 4 + at(p, 1) * (size * 4), 16), size * 4)
        acc2[q, :] = acc1[mine, :] + in2[0, q, :] + in2[1, q, :] + in2[2, q, :]
        for j in (1, 2, 3):
            where = pl.ds(pl.multiple_of(BASES[p] // 16 + ((at(p, 2) + j) % 4) * size, 16), size)
            copy = push(
                acc2.at[where],
                in3.at[j - 1, pl.ds(BASES[p] // 64, size)],
                s3.at[p * 3 + j - 1],
                r3.at[p * 3 + j - 1],
                along(p, 2, j),
            )
            copy.start()
            step3[p, j] = copy

    def start_of(p):
        if BASES[p] < WAVE_HALF[0]:
            return core * WAVE_HALF[0] + BASES[p]
        return 2 * WAVE_HALF[0] + core * WAVE_HALF[1] + (BASES[p] - WAVE_HALF[0])

    def place(p, depth):
        size = PARTS[p][1]
        row = start_of(p) + at(p, 0) * (size * 16)
        if depth > 1:
            row = row + at(p, 1) * (size * 4)
        if depth > 2:
            row = row + at(p, 2) * size
        return full.at[pl.ds(pl.multiple_of(row, 16), (size * 16, size * 4, size)[depth - 1])]

    def half_of(p, offset, half):
        size = PARTS[p][1] * 8
        row = start_of(p) + ((at(p, 0) + 4 + offset) % 4) * (2 * size) + half * size
        return full.at[pl.ds(pl.multiple_of(row, 16), size)]

    def share_third(p):
        size = PARTS[p][1]
        for j in (1, 2, 3):
            step3[p, j].wait_recv()
        q = pl.ds(BASES[p] // 64, size)
        mine = pl.ds(pl.multiple_of(BASES[p] // 16 + at(p, 2) * size, 16), size)
        unit[q, :] = (acc2[mine, :] + in3[0, q, :] + in3[1, q, :] + in3[2, q, :]).astype(BF16)
        own[p] = pltpu.make_async_copy(unit.at[q], place(p, 3), local.at[p])
        own[p].start()
        for j in (1, 2, 3):
            copy = push(unit.at[q], place(p, 3), s4.at[p * 3 + j - 1], r4.at[p * 3 + j - 1], along(p, 2, j))
            copy.start()
            step4[p, j] = copy

    def share_second(p):
        own[p].wait()
        for j in (1, 2, 3):
            step4[p, j].wait_recv()
        for j in (1, 2, 3):
            block = place(p, 2)
            copy = push(block, block, s5.at[p * 3 + j - 1], r5.at[p * 3 + j - 1], along(p, 1, j))
            copy.start()
            step5[p, j] = copy

    def to_other_core(p, n, block):
        side[p, n] = push(block, block, sib_s.at[p * 7 + n], sib_r.at[p * 7 + n], sibling)
        side[p, n].start()

    def share_first(p):
        for j in (1, 2, 3):
            step5[p, j].wait_recv()
        for n, (to, half) in enumerate(((1, 0), (3, 1), (1, 1), (3, 0))):
            block = half_of(p, 0, half)
            copy = push(block, block, s6.at[p * 6 + n], r6.at[p * 6 + n], along(p, 0, to))
            copy.start()
            step6[p, n] = copy
        to_other_core(p, 0, place(p, 1))

    def forward(p):
        for n, (to, half) in enumerate(((1, 0), (3, 1))):
            step6[p, n].wait_recv()
            block = half_of(p, -to, half)
            copy = push(block, block, s6.at[p * 6 + 4 + n], r6.at[p * 6 + 4 + n], along(p, 0, to))
            copy.start()
            step6[p, 4 + n] = copy
            to_other_core(p, 1 + n, block)

    def finish(p):
        for n, (to, half) in enumerate(((1, 1), (3, 0))):
            step6[p, 2 + n].wait_recv()
            to_other_core(p, 3 + n, half_of(p, -to, half))
        for half in range(2):
            step6[p, 4 + half].wait_recv()
            to_other_core(p, 5 + half, half_of(p, 2, half))

    def put(first, value):
        here = value.shape[0] // 16 * chunks
        for half in range(2):
            begin = max(first, half * SECOND_HALF_TILES)
            end = min(first + here, (half + 1) * SECOND_HALF_TILES)
            if begin >= end:
                continue

            def store(ref, base, half=half, begin=begin, end=end):
                for t in range(begin, end):
                    row = base + (t - half * SECOND_HALF_TILES) * 16
                    b, c = (t - first) // chunks, (t - first) % chunks
                    ref[row : row + 16, :] = value[b * 16 : b * 16 + 16, c * 128 : c * 128 + 128].astype(ref.dtype)

            @pl.when(core == half)
            def _(store=store):
                store(keep, WAVE_HALF[0])

            @pl.when(core != half)
            def _(store=store):
                store(given, 0)

    def make_wsum(d):
        rows = slice(d * trows, (d + 1) * trows)
        for k in range(width // 256):
            cols = slice(k * 256, (k + 1) * 256)
            w = lax.dot_general(
                hi[rows, cols], c_all[...], (((0,), (0,)), ((), ())), preferred_element_type=F32
            ) + lax.dot_general(
                lo[rows, cols], c_all[...], (((0,), (0,)), ((), ())), preferred_element_type=F32
            )
            put((d * 48 + k * 16) * chunks, w)

    def make_wself():
        self_comp = (own_h[...].astype(F32) * loop_ref[...].astype(F32).reshape(1, width)).astype(BF16)
        for k in range(width // 256):
            w = lax.dot_general(
                self_comp[:, k * 256 : (k + 1) * 256], own_c[...], (((0,), (0,)), ((), ())),
                preferred_element_type=F32,
            )
            put((96 + k * 16) * chunks, w)
        low = (W_TILES - SECOND_HALF_TILES) * 16
        n = rest.shape[0]

        def store(ref, base):
            ref[base + low : base + low + n, :] = rest[...].astype(ref.dtype)
            ref[base + low + n : base + WAVE_HALF[1], :] = jnp.zeros((WAVE_HALF[1] - low - n, 128), ref.dtype)

        @pl.when(core == 1)
        def _():
            store(keep, WAVE_HALF[0])

        @pl.when(core != 1)
        def _():
            store(given, 0)

    send_pair((0, 1))
    gz = []
    for k in (1, 3, 2):
        copy = push(g_ref.at[:, (z + k) % 4], g_in.at[k - 1], gz_s.at[k - 1], gz_r.at[k - 1], me.along("z", k))
        copy.start()
        gz.append(copy)
    loads[0].wait()
    send_first((0, 1))
    for load in loads[1:]:
        load.wait()
    make_wsum(0)
    make_wsum(1)
    send_pair((2,))
    send_second(0)
    send_second(1)
    make_wself()
    send_pair((3, 4))
    send_first((2,))
    send_third(0)
    send_third(1)
    send_first((3, 4))
    for copy in gz:
        copy.wait_recv()
    for half in range(2):
        g_acc[half] = (
            g_own[half].astype(F32)
            + g_in[0, half].astype(F32)
            + g_in[1, half].astype(F32)
            + g_in[2, half].astype(F32)
        )
    gx = push(g_acc.at[1 - x_hi], g_side, gx_s, gx_r, me.along("x", 2))
    gx.start()
    share_third(0)
    share_third(1)
    send_second(2)
    share_second(0)
    share_second(1)
    send_second(3)
    send_second(4)
    share_first(0)
    share_first(1)
    send_third(2)
    send_third(3)
    send_third(4)
    forward(0)
    forward(1)
    for p in (2, 3, 4):
        share_third(p)
    finish(0)
    finish(1)
    for p in (2, 3, 4):
        share_second(p)
    for p in (2, 3, 4):
        share_first(p)
    gx.wait_recv()
    g_out[...] = g_acc[x_hi] + g_side[...]
    for p in (2, 3, 4):
        forward(p)
    for p in (2, 3, 4):
        finish(p)

    for copy in side.values():
        copy.wait_recv()
    gx.wait_send()
    for copy in gz:
        copy.wait_send()
    for group in (pairs, step1, step2, step3, step4, step5, step6, side):
        for copy in group.values():
            copy.wait_send()


def reduce_all(keep, give, g, hi, lo, c_all, rest, own_c, own_h, loop):
    rows, width = g.shape
    g = g.reshape(2, 4, rows // 8, width)
    n = len(PARTS)
    return pl.pallas_call(
        reduce_kernel,
        out_shape=(
            jax.ShapeDtypeStruct((2 * HALF_ROWS, 128), BF16),
            jax.ShapeDtypeStruct((rows // 8, width), F32),
        ),
        in_specs=[ANY] * 6 + [VMEM] * 4,
        out_specs=[ANY, VMEM],
        scratch_shapes=[
            pltpu.VMEM((HALF_ROWS, 128), F32),
            pltpu.VMEM((WAVE_HALF[1], 128), BF16),
            pltpu.VMEM(hi.shape, BF16),
            pltpu.VMEM(lo.shape, BF16),
            pltpu.VMEM(c_all.shape, BF16),
            pltpu.VMEM((2, rows // 8, width), BF16),
            pltpu.VMEM((HALF_ROWS, 128), BF16),
            pltpu.VMEM((HALF_ROWS, 128), BF16),
            pltpu.VMEM((3, HALF_ROWS // 4, 128), BF16),
            pltpu.VMEM((HALF_ROWS // 4, 128), F32),
            pltpu.VMEM((3, HALF_ROWS // 16, 128), F32),
            pltpu.VMEM((HALF_ROWS // 16, 128), F32),
            pltpu.VMEM((3, HALF_ROWS // 64, 128), F32),
            pltpu.VMEM((HALF_ROWS // 64, 128), BF16),
            pltpu.VMEM((3, 2, rows // 8, width), BF16),
            pltpu.VMEM((2, rows // 8, width), F32),
            pltpu.VMEM((rows // 8, width), F32),
            *[DMA((4 * n,))] * 2, *[DMA((3 * n,))] * 10, *[DMA((6 * n,))] * 2, *[DMA((7 * n,))] * 2,
            DMA((3,)), DMA((3,)), DMA, DMA, DMA((n,)), DMA((5,)),
        ],
        compiler_params=pltpu.CompilerParams(
            collective_id=1, has_side_effects=True, vmem_limit_bytes=VMEM_BYTES
        ),
        name="reduce_all",
    )(keep, give, g, hi, lo, c_all, rest, own_c, own_h, loop)


def unpack_kernel(
    full_hbm, w_hbm, r_out, l_out, full, w_out, in_sem, out_sem, *, edge_scale, self_scale, rel_scale
):
    rels, width = r_out.shape
    chunks = width // 128
    per = width // 16
    pieces = in_sem.shape[0]
    size = full.shape[0] // pieces
    loads = []
    for i in range(pieces):
        where = pl.ds(i * size, size)
        loads.append(pltpu.make_async_copy(full_hbm.at[where], full.at[where], in_sem.at[i]))
        loads[-1].start()
    waited = []

    def need(first, last):
        for i in range(first // size, -(-last // size)):
            if i not in waited:
                waited.append(i)
                loads[i].wait()

    def tile(first, index):
        return full[pl.ds(pl.multiple_of(first + index * 16, 16), 16), :].astype(F32)

    w_first = 2 * WAVE_HALF[0]
    rest_first = w_first + W_TILES * 16
    stores = []
    for d, scale in enumerate((edge_scale, edge_scale, self_scale)):
        for k in range(3):
            group = per // 3
            need(w_first, w_first + (d * per + (k + 1) * group) * chunks * 16)

            @pl.loop(k * group, (k + 1) * group)
            def _(i, d=d, scale=scale):
                for c in range(chunks):
                    w_out[d, pl.ds(pl.multiple_of(i * 16, 16), 16), c * 128 : (c + 1) * 128] = (
                        tile(w_first, (d * per + i) * chunks + c) * scale
                    )

            where = pl.ds(k * group * 16, group * 16)
            stores.append(
                pltpu.make_async_copy(w_out.at[d, where], w_hbm.at[d, where], out_sem.at[d * 3 + k])
            )
            stores[-1].start()

    need(0, full.shape[0])
    whole = FIRST_TILES // chunks

    @pl.loop(0, whole)
    def _(i):
        for c in range(chunks):
            r_out[pl.ds(pl.multiple_of(i * 16, 16), 16), c * 128 : (c + 1) * 128] = (
                tile(0, i * chunks + c) * rel_scale
            )

    for t in range(whole * chunks, -(-(rels + 1) // 16) * chunks):
        b, cols = t // chunks, slice(t % chunks * 128, t % chunks * 128 + 128)
        last = tile(0, t) if t < FIRST_TILES else tile(rest_first, t - FIRST_TILES)
        n = min(16, rels - b * 16)
        if n:
            r_out[b * 16 : b * 16 + n, cols] = last[:n] * rel_scale
        if n < 16:
            l_out[cols] = (last[n : n + 1] * self_scale).reshape(128)
    for store in stores:
        store.wait()


def unpack(full, rels, width, **scales):
    return pl.pallas_call(
        functools.partial(unpack_kernel, **scales),
        out_shape=(
            jax.ShapeDtypeStruct((3, width, width), F32),
            jax.ShapeDtypeStruct((rels, width), F32),
            jax.ShapeDtypeStruct((width,), F32),
        ),
        in_specs=[ANY],
        out_specs=[ANY, VMEM, VMEM],
        scratch_shapes=[
            pltpu.VMEM(full.shape, BF16),
            pltpu.VMEM((3, width, width), F32),
            DMA((11,)),
            DMA((9,)),
        ],
        compiler_params=pltpu.CompilerParams(vmem_limit_bytes=VMEM_BYTES),
        name="unpack",
    )(full)


def body(
    h_src, rel_table, cotangent, h_tgt, loop_rel, weights, src_index, tgt_index, rel_ids, direction, counts
):
    width = weights.shape[1]
    tiles, edge = src_index.shape[2:]
    rels = rel_table.shape[0]
    h_all, c_all, s8, t8, r8 = gather(
        h_src, cotangent, *[a.reshape(tiles, edge) for a in (src_index, tgt_index, rel_ids, direction)]
    )
    g, grad_tgt, hi, lo, rest, keep, give = edges(
        counts.reshape(1), s8, t8, r8, h_all, c_all, weights, rel_table, cotangent, h_tgt, loop_rel
    )
    full, grad_src = reduce_all(
        keep, give, g, hi, lo, c_all, rest, cotangent, h_tgt, loop_rel
    )
    devices = lax.axis_size("src") * lax.axis_size("tgt")
    edges_all = float(devices * tiles * edge)
    targets_all = float(devices * cotangent.shape[0])
    grad_weights, grad_rel, grad_loop = unpack(
        full,
        rels,
        width,
        edge_scale=edges_all**-0.5,
        self_scale=targets_all**-0.5,
        rel_scale=(float(rels) / edges_all) ** 0.5,
    )
    return grad_src, grad_tgt, grad_weights, grad_rel, grad_loop


def solution(mesh):
    return jax.shard_map(
        body,
        mesh=mesh,
        in_specs=(
            P(("src", "tgt"), None),
            P(),
            P(("tgt", "src"), None),
            P(("tgt", "src"), None),
            P(),
            P(),
            P("src", "tgt", None, None),
            P("src", "tgt", None, None),
            P("src", "tgt", None, None),
            P("src", "tgt", None, None),
            P("src", "tgt"),
        ),
        out_specs=(P(("src", "tgt"), None), P(("tgt", "src"), None), P(), P(), P()),
        check_vma=False,
    )
```

time: 125 us -> 116 us (0.928)
  Pallas kernels: 123 us -> 113 us
    pallas_call x1, Pallas kernels: 70.8 us -> 65.5 us  [reduce_all(): pl.pallas_call(reduce_kernel, out_shape=(jax.ShapeDtypeStruct((2 * HALF_R...]
    pallas_call x1, Pallas kernels: 23 us -> 20.6 us  [edges(): pl.pallas_call(edge_kernel, out_shape=(jax.ShapeDtypeStruct((rows, width)...]
    pallas_call x1, Pallas kernels: 8.86 us -> 7.09 us  [unpack(): pl.pallas_call(functools.partial(unpack_kernel, **scales), out_shape=(jax...]
where the time goes in v4:
time: 116 us; the launch traced here: 115 us
  Pallas kernels  113 us (97%)
  between operations  1.33 us (1%)
    pallas_call x1, Pallas kernels, reduce_all(): pl.pallas_call(reduce_kernel, out_shape=(jax.ShapeDtypeStruct((2 * HALF_R...  65.5 us
    pallas_call x1, Pallas kernels, edges(): pl.pallas_call(edge_kernel, out_shape=(jax.ShapeDtypeStruct((rows, width)...  20.6 us
    pallas_call x1, Pallas kernels, gather(): pl.pallas_call(gather_kernel, out_shape=(jax.ShapeDtypeStruct((2, 4, rows...  20.2 us
    pallas_call x1, Pallas kernels, unpack(): pl.pallas_call(functools.partial(unpack_kernel, **scales), out_shape=(jax...  7.09 us

profile of v4, /device:TPU:1, one launch (start us, length us, event | category | flops | bytes accessed | tf_op | source)
XLA Modules:
  0.0 115.4 jit_solution(4232932475696649064)
XLA Ops:
  1.3 20.2 %gather_panels.1 = (bf16[2,4,64,768]{3,2,1,0:T(8,128)(2,1)}, bf16[2,4,2,32,768]{4,3,2,1,0:T(8,128)(2,1)}, s32[16,128]{1,0:T(8,128)}, s32[16,128]{1,0:T(8,128)}, s32[16,128]{1,0:T(8,128)}) custom-call(bf16[64,768]{1,0:T(8,128)(2,1)} %h_ref.1, bf16[32,768]{1,0:T(8,128)(2,1)} %own_c.3, s32[16,128]{1,0:T(8,128)} %bitcast.16, s32[16,128]{1,0:T(8,128)} %bitcast.17, ...), custom_call_target="tpu_custom_call" | custom-call | tf_op jit(solution)/shard_map/gather_panels/pallas_call | solution.py:129
  21.5 20.6 %edges.1 = (bf16[512,768]{1,0:T(8,128)(2,1)}, f32[32,768]{1,0:T(8,128)}, bf16[1024,768]{1,0:T(8,128)(2,1)}, bf16[1024,768]{1,0:T(8,128)(2,1)}, f32[160,128]{1,0:...) custom-call(s32[1]{0:T(128)} %bitcast.11.live_ref, s32[2048]{0:T(1024)} %bitcast.20, s32[2048]{0:T(1024)} %bitcast.21, ...), custom_call_target="tpu_custom_call" | custom-call | tf_op jit(solution)/shard_map/edges/pallas_call | solution.py:305
  42.1 65.5 %reduce_all.1 = (bf16[22528,128]{1,0:T(8,128)(2,1)}, f32[64,768]{1,0:T(8,128)}) custom-call(f32[4096,128]{1,0:T(8,128)} %get-tuple-element.27.keep_hbm, bf16[4096,128]{1,0:T(8,128)(2,1)} %get-tuple-element.28.give, bf16[2,4,64,768]{3,2,1,0:T(8,128)(2,1)} %bitcast.14, bf16[1024,768]{1,0:T(8,128)(2,1)} %get-tuple-element.30.hi_hbm, ...), custom_call_target="tpu_custom_call" | custom-call | tf_op jit(solution)/shard_map/reduce_all/pallas_call | solution.py:677
  107.6 0.0 copy-start
  107.6 7.1 %unpack.1 = (f32[3,768,768]{2,1,0:T(8,128)}, f32[1387,768]{1,0:T(8,128)}, f32[768]{0:T(1024)}) custom-call(bf16[22528,128]{1,0:T(8,128)(2,1)} %get-tuple-element.35.full_hbm), custom_call_target="tpu_custom_call" | custom-call | tf_op jit(solution)/shard_map/unpack/pallas_call | solution.py:781
  114.7 0.0 copy-done
  114.7 0.7 copy.18
Async XLA Ops:
  107.6 7.1 %copy-start = (f32[64,768]{1,0:T(8,128)S(1)}, f32[64,768]{1,0:T(8,128)}, u32[]{:S(2)}) copy-start(f32[64,768]{1,0:T(8,128)} %get-tuple-element.44) | copy-start | bytes 589828

commit v5 on v4

--- a/solution.py
+++ b/solution.py
@@ -311,7 +311,7 @@
             jax.ShapeDtypeStruct((2 * trows, width), BF16),
             jax.ShapeDtypeStruct((rpad // 16 * (width // 128) * 16 - FIRST_TILES * 16, 128), F32),
             jax.ShapeDtypeStruct((WAVE_HALF[0], 128), F32),
-            jax.ShapeDtypeStruct((WAVE_HALF[0], 128), BF16),
+            jax.ShapeDtypeStruct((WAVE_HALF[0], 128), F32),
         ),
         in_specs=[SMEM] * 4 + [ANY] * 4 + [VMEM] * 3,
         out_specs=[ANY, VMEM, ANY, ANY, VMEM, ANY, ANY],
@@ -322,7 +322,7 @@
             pltpu.VMEM(z.shape, BF16),
             pltpu.VMEM((rows, width), BF16),
             pltpu.VMEM((WAVE_HALF[0], 128), F32),
-            pltpu.VMEM((WAVE_HALF[0], 128), BF16),
+            pltpu.VMEM((WAVE_HALF[0], 128), F32),
             pltpu.VMEM((rows * 8, 128), F32),
             pltpu.VMEM((2 * trows * 8, 128), F32),
             pltpu.VMEM((rpad * 8, 128), F32),
@@ -341,8 +341,8 @@
 
 def reduce_kernel(
     keep_hbm, give, g_ref, hi_hbm, lo_hbm, c_hbm, rest, own_c, own_h, loop_ref, full, g_out,
-    keep, given, hi, lo, c_all, g_own, pair, out1, in1, acc1, in2, acc2, in3, unit, g_in, g_acc, g_side,
-    pair_s, pair_r, s1, r1, s2, r2, s3, r3, s4, r4, s5, r5, s6, r6, sib_s, sib_r, gz_s, gz_r, gx_s, gx_r,
+    keep, given, hi, lo, c_all, g_own, pair, out1, in1, acc1, out2, in2, unit, g_in, g_acc, g_side,
+    pair_s, pair_r, s1, r1, s2, r2, s4, r4, s6, r6, sib_s, sib_r, gz_s, gz_r, gx_s, gx_r,
     local, kept,
 ):
     me = Place()
@@ -359,6 +359,15 @@
 
     def along(p, depth, j):
         return me.along(PARTS[p][0][depth], j)
+
+    def in_plane(p, j, k):
+        where = dict(me.at)
+        where[PARTS[p][0][1]] = (at(p, 1) + j) % 4
+        where[PARTS[p][0][2]] = (at(p, 2) + k) % 4
+        return me.device(where, core)
+
+    others = [(2, 2), (2, 1), (2, 3), (1, 2), (3, 2), (1, 1), (1, 3), (3, 1), (3, 3)]
+    others += [(2, 0), (0, 2), (1, 0), (3, 0), (0, 1), (0, 3)]
 
     def rows_of(p, a):
         size = PARTS[p][1] * 16
@@ -379,9 +388,12 @@
     ]
     for load in loads:
         load.start()
-    greet([me.along(axis, k) for axis in ("x", "y", "z") for k in (1, 2, 3)] + [sibling])
-
-    pairs, step1, step2, step3, step4, step5, step6, side, own = {}, {}, {}, {}, {}, {}, {}, {}, {}
+    plane = [me.along(axis, k) for axis in ("x", "y", "z") for k in (1, 2, 3)]
+    for p in (0, 1, 4):
+        plane += [in_plane(p, j, k) for j, k in others[:9]]
+    greet(plane + [sibling])
+
+    pairs, step1, step6, side, own = {}, {}, {}, {}, {}
 
     def send_pair(some):
         for j in (1, 2, 3, 0):
@@ -406,7 +418,7 @@
                 @pl.loop(0, size // 128)
                 def _(i, base=base):
                     r = pl.ds(pl.multiple_of(base + i * 128, 16), 128)
-                    out1[r, :] = (keep[r, :] + pair[r, :].astype(F32)).astype(BF16)
+                    out1[r, :] = (keep[r, :] + pair[r, :]).astype(BF16)
 
                 copy = push(
                     out1.at[rows_of(p, (at(p, 0) + j) % 4)],
@@ -419,55 +431,40 @@
                 step1[p, j] = copy
 
     def send_second(p):
-        size = PARTS[p][1] * 4
-        base = BASES[p] + at(p, 0) * (size * 4)
+        size = PARTS[p][1]
+        base = BASES[p] + at(p, 0) * (size * 16)
         low = BASES[p] // 4
         pairs[p, 0].wait_recv()
         for j in (1, 2, 3):
             step1[p, j].wait_recv()
 
-        @pl.loop(0, size * 4 // 128)
+        @pl.loop(0, size * 16 // 128)
         def _(i):
             r = pl.ds(pl.multiple_of(base + i * 128, 16), 128)
             q = pl.ds(pl.multiple_of(low + i * 128, 16), 128)
-            acc1[q, :] = (
+            total = (
                 keep[r, :]
-                + pair[r, :].astype(F32)
+                + pair[r, :]
                 + in1[0, q, :].astype(F32)
                 + in1[1, q, :].astype(F32)
                 + in1[2, q, :].astype(F32)
             )
-
-        for j in (1, 2, 3):
-            where = pl.ds(pl.multiple_of(low + ((at(p, 1) + j) % 4) * size, 16), size)
-            copy = push(
-                acc1.at[where],
-                in2.at[j - 1, pl.ds(BASES[p] // 16, size)],
-                s2.at[p * 3 + j - 1],
-                r2.at[p * 3 + j - 1],
-                along(p, 1, j),
-            )
-            copy.start()
-            step2[p, j] = copy
-
-    def send_third(p):
-        size = PARTS[p][1]
-        for j in (1, 2, 3):
-            step2[p, j].wait_recv()
-        q = pl.ds(BASES[p] // 16, size * 4)
-        mine = pl.ds(pl.multiple_of(BASES[p] // 4 + at(p, 1) * (size * 4), 16), size * 4)
-        acc2[q, :] = acc1[mine, :] + in2[0, q, :] + in2[1, q, :] + in2[2, q, :]
-        for j in (1, 2, 3):
-            where = pl.ds(pl.multiple_of(BASES[p] // 16 + ((at(p, 2) + j) % 4) * size, 16), size)
-            copy = push(
-                acc2.at[where],
-                in3.at[j - 1, pl.ds(BASES[p] // 64, size)],
-                s3.at[p * 3 + j - 1],
-                r3.at[p * 3 + j - 1],
-                along(p, 2, j),
-            )
-            copy.start()
-            step3[p, j] = copy
+            acc1[q, :] = total
+            out2[q, :] = total.astype(BF16)
+
+        for j, k in others:
+            row = low + (((at(p, 1) + j) % 4) * 4 + (at(p, 2) + k) % 4) * size
+            push(
+                out2.at[pl.ds(pl.multiple_of(row, 16), size)],
+                in2.at[j * 4 + k - 1, pl.ds(BASES[p] // 64, size)],
+                s2.at[p],
+                r2.at[p],
+                in_plane(p, j, k),
+            ).start()
+
+    def second(p):
+        mine = out2.at[pl.ds(BASES[p] // 4, PARTS[p][1] * 15)]
+        return push(mine, in2.at[:, pl.ds(BASES[p] // 64, PARTS[p][1])], s2.at[p], r2.at[p], in_plane(p, 1, 1))
 
     def start_of(p):
         if BASES[p] < WAVE_HALF[0]:
@@ -488,37 +485,31 @@
         row = start_of(p) + ((at(p, 0) + 4 + offset) % 4) * (2 * size) + half * size
         return full.at[pl.ds(pl.multiple_of(row, 16), size)]
 
-    def share_third(p):
+    def share_second(p):
         size = PARTS[p][1]
-        for j in (1, 2, 3):
-            step3[p, j].wait_recv()
+        second(p).wait_recv()
         q = pl.ds(BASES[p] // 64, size)
-        mine = pl.ds(pl.multiple_of(BASES[p] // 16 + at(p, 2) * size, 16), size)
-        unit[q, :] = (acc2[mine, :] + in3[0, q, :] + in3[1, q, :] + in3[2, q, :]).astype(BF16)
+        mine = pl.ds(pl.multiple_of(BASES[p] // 4 + (at(p, 1) * 4 + at(p, 2)) * size, 16), size)
+        total = acc1[mine, :]
+        for n in range(15):
+            total = total + in2[n, q, :].astype(F32)
+        unit[q, :] = total.astype(BF16)
+        for j, k in others:
+            push(unit.at[q], place(p, 3), s4.at[p], r4.at[p], in_plane(p, j, k)).start()
         own[p] = pltpu.make_async_copy(unit.at[q], place(p, 3), local.at[p])
         own[p].start()
-        for j in (1, 2, 3):
-            copy = push(unit.at[q], place(p, 3), s4.at[p * 3 + j - 1], r4.at[p * 3 + j - 1], along(p, 2, j))
-            copy.start()
-            step4[p, j] = copy
-
-    def share_second(p):
-        own[p].wait()
-        for j in (1, 2, 3):
-            step4[p, j].wait_recv()
-        for j in (1, 2, 3):
-            block = place(p, 2)
-            copy = push(block, block, s5.at[p * 3 + j - 1], r5.at[p * 3 + j - 1], along(p, 1, j))
-            copy.start()
-            step5[p, j] = copy
+
+    def shared(p):
+        where = pl.ds(pl.multiple_of(start_of(p) + at(p, 0) * (PARTS[p][1] * 16), 16), PARTS[p][1] * 15)
+        return push(full.at[where], full.at[where], s4.at[p], r4.at[p], in_plane(p, 1, 1))
 
     def to_other_core(p, n, block):
         side[p, n] = push(block, block, sib_s.at[p * 7 + n], sib_r.at[p * 7 + n], sibling)
         side[p, n].start()
 
     def share_first(p):
-        for j in (1, 2, 3):
-            step5[p, j].wait_recv()
+        own[p].wait()
+        shared(p).wait_recv()
         for n, (to, half) in enumerate(((1, 0), (3, 1), (1, 1), (3, 0))):
             block = half_of(p, 0, half)
             copy = push(block, block, s6.at[p * 6 + n], r6.at[p * 6 + n], along(p, 0, to))
@@ -606,20 +597,21 @@
         copy.start()
         gz.append(copy)
     loads[0].wait()
-    send_first((0, 1))
     for load in loads[1:]:
         load.wait()
     make_wsum(0)
     make_wsum(1)
-    send_pair((2,))
+    make_wself()
+    send_pair((2, 3, 4))
+    send_first((0, 1))
+    send_first((2, 3, 4))
     send_second(0)
     send_second(1)
-    make_wself()
-    send_pair((3, 4))
-    send_first((2,))
-    send_third(0)
-    send_third(1)
-    send_first((3, 4))
+    send_second(2)
+    send_second(3)
+    send_second(4)
+    share_second(0)
+    share_second(1)
     for copy in gz:
         copy.wait_recv()
     for half in range(2):
@@ -631,43 +623,37 @@
         )
     gx = push(g_acc.at[1 - x_hi], g_side, gx_s, gx_r, me.along("x", 2))
     gx.start()
-    share_third(0)
-    share_third(1)
-    send_second(2)
-    share_second(0)
-    share_second(1)
-    send_second(3)
-    send_second(4)
+    share_second(2)
+    share_second(3)
+    share_second(4)
     share_first(0)
     share_first(1)
-    send_third(2)
-    send_third(3)
-    send_third(4)
+    share_first(2)
+    share_first(3)
+    share_first(4)
     forward(0)
     forward(1)
-    for p in (2, 3, 4):
-        share_third(p)
+    forward(2)
+    forward(3)
+    forward(4)
     finish(0)
     finish(1)
-    for p in (2, 3, 4):
-        share_second(p)
-    for p in (2, 3, 4):
-        share_first(p)
     gx.wait_recv()
     g_out[...] = g_acc[x_hi] + g_side[...]
-    for p in (2, 3, 4):
-        forward(p)
-    for p in (2, 3, 4):
-        finish(p)
-
+    finish(2)
+    finish(3)
+    finish(4)
     for copy in side.values():
         copy.wait_recv()
     gx.wait_send()
     for copy in gz:
         copy.wait_send()
-    for group in (pairs, step1, step2, step3, step4, step5, step6, side):
+    for group in (pairs, step1, step6, side):
         for copy in group.values():
             copy.wait_send()
+    for p in parts:
+        second(p).wait_send()
+        shared(p).wait_send()
 
 
 def reduce_all(keep, give, g, hi, lo, c_all, rest, own_c, own_h, loop):
@@ -684,23 +670,22 @@
         out_specs=[ANY, VMEM],
         scratch_shapes=[
             pltpu.VMEM((HALF_ROWS, 128), F32),
-            pltpu.VMEM((WAVE_HALF[1], 128), BF16),
+            pltpu.VMEM((WAVE_HALF[1], 128), F32),
             pltpu.VMEM(hi.shape, BF16),
             pltpu.VMEM(lo.shape, BF16),
             pltpu.VMEM(c_all.shape, BF16),
             pltpu.VMEM((2, rows // 8, width), BF16),
-            pltpu.VMEM((HALF_ROWS, 128), BF16),
+            pltpu.VMEM((HALF_ROWS, 128), F32),
             pltpu.VMEM((HALF_ROWS, 128), BF16),
             pltpu.VMEM((3, HALF_ROWS // 4, 128), BF16),
             pltpu.VMEM((HALF_ROWS // 4, 128), F32),
-            pltpu.VMEM((3, HALF_ROWS // 16, 128), F32),
-            pltpu.VMEM((HALF_ROWS // 16, 128), F32),
-            pltpu.VMEM((3, HALF_ROWS // 64, 128), F32),
+            pltpu.VMEM((HALF_ROWS // 4, 128), BF16),
+            pltpu.VMEM((15, HALF_ROWS // 64, 128), BF16),
             pltpu.VMEM((HALF_ROWS // 64, 128), BF16),
             pltpu.VMEM((3, 2, rows // 8, width), BF16),
             pltpu.VMEM((2, rows // 8, width), F32),
             pltpu.VMEM((rows // 8, width), F32),
-            *[DMA((4 * n,))] * 2, *[DMA((3 * n,))] * 10, *[DMA((6 * n,))] * 2, *[DMA((7 * n,))] * 2,
+            *[DMA((4 * n,))] * 2, *[DMA((3 * n,))] * 2, *[DMA((n,))] * 4, *[DMA((6 * n,))] * 2, *[DMA((7 * n,))] * 2,
             DMA((3,)), DMA((3,)), DMA, DMA, DMA((n,)), DMA((5,)),
         ],
         compiler_params=pltpu.CompilerParams(

time: 116 us -> 108 us (0.931)
  Pallas kernels: 113 us -> 105 us
    pallas_call x1, Pallas kernels: 20.6 us -> 13.1 us  [edges(): pl.pallas_call(edge_kernel, out_shape=(jax.ShapeDtypeStruct((rows, width)...]
where the time goes in v5:
time: 108 us; the launch traced here: 107 us
  Pallas kernels  105 us (97%)
  between operations  1.33 us (1%)
    pallas_call x1, Pallas kernels, reduce_all(): pl.pallas_call(reduce_kernel, out_shape=(jax.ShapeDtypeStruct((2 * HALF_R...  65 us
    pallas_call x1, Pallas kernels, gather(): pl.pallas_call(gather_kernel, out_shape=(jax.ShapeDtypeStruct((2, 4, rows...  20.2 us
    pallas_call x1, Pallas kernels, edges(): pl.pallas_call(edge_kernel, out_shape=(jax.ShapeDtypeStruct((rows, width)...  13.1 us
    pallas_call x1, Pallas kernels, unpack(): pl.pallas_call(functools.partial(unpack_kernel, **scales), out_shape=(jax...  7.09 us

profile of v5, /device:TPU:1, one launch (start us, length us, event | category | flops | bytes accessed | tf_op | source)
XLA Modules:
  0.0 107.3 jit_solution(14066121687144788278)
XLA Ops:
  1.3 20.2 %gather_panels.1 = (bf16[2,4,64,768]{3,2,1,0:T(8,128)(2,1)}, bf16[2,4,2,32,768]{4,3,2,1,0:T(8,128)(2,1)}, s32[16,128]{1,0:T(8,128)}, s32[16,128]{1,0:T(8,128)}, s32[16,128]{1,0:T(8,128)}) custom-call(bf16[64,768]{1,0:T(8,128)(2,1)} %h_ref.1, bf16[32,768]{1,0:T(8,128)(2,1)} %own_c.3, s32[16,128]{1,0:T(8,128)} %bitcast.16, s32[16,128]{1,0:T(8,128)} %bitcast.17, ...), custom_call_target="tpu_custom_call" | custom-call | tf_op jit(solution)/shard_map/gather_panels/pallas_call | solution.py:129
  21.5 13.1 %edges.1 = (bf16[512,768]{1,0:T(8,128)(2,1)}, f32[32,768]{1,0:T(8,128)}, bf16[1024,768]{1,0:T(8,128)(2,1)}, bf16[1024,768]{1,0:T(8,128)(2,1)}, f32[160,128]{1,0:...) custom-call(s32[1]{0:T(128)} %bitcast.11.live_ref, s32[2048]{0:T(1024)} %bitcast.20, s32[2048]{0:T(1024)} %bitcast.21, ...), custom_call_target="tpu_custom_call" | custom-call | tf_op jit(solution)/shard_map/edges/pallas_call | solution.py:305
  34.6 65.0 %reduce_all.1 = (bf16[22528,128]{1,0:T(8,128)(2,1)}, f32[64,768]{1,0:T(8,128)}) custom-call(f32[4096,128]{1,0:T(8,128)} %get-tuple-element.27.keep_hbm, f32[4096,128]{1,0:T(8,128)} %get-tuple-element.28.give, bf16[2,4,64,768]{3,2,1,0:T(8,128)(2,1)} %bitcast.14, bf16[1024,768]{1,0:T(8,128)(2,1)} %get-tuple-element.30.hi_hbm, ...), custom_call_target="tpu_custom_call" | custom-call | tf_op jit(solution)/shard_map/reduce_all/pallas_call | solution.py:663
  99.5 0.0 copy-start
  99.5 7.1 %unpack.1 = (f32[3,768,768]{2,1,0:T(8,128)}, f32[1387,768]{1,0:T(8,128)}, f32[768]{0:T(1024)}) custom-call(bf16[22528,128]{1,0:T(8,128)(2,1)} %get-tuple-element.35.full_hbm), custom_call_target="tpu_custom_call" | custom-call | tf_op jit(solution)/shard_map/unpack/pallas_call | solution.py:766
  106.6 0.0 copy-done
  106.6 0.7 copy.18
Async XLA Ops:
  99.5 7.1 %copy-start = (f32[64,768]{1,0:T(8,128)S(1)}, f32[64,768]{1,0:T(8,128)}, u32[]{:S(2)}) copy-start(f32[64,768]{1,0:T(8,128)} %get-tuple-element.44) | copy-start | bytes 589828

commit v6 on v5

--- a/solution.py
+++ b/solution.py
@@ -23,12 +23,12 @@
 PARTS = (
     (("x", "y", "z"), 32),
     (("y", "z", "x"), 32),
+    (("z", "x", "y"), 48),
     (("x", "y", "z"), 32),
     (("y", "z", "x"), 32),
-    (("z", "x", "y"), 48),
 )
-BASES = (0, 2048, 4096, 6144, 8192)
-UNROLL = 16
+BASES = (0, 2048, 4096, 7168, 9216)
+UNROLL = 32
 EDGE = 128
 VMEM_BYTES = 63 * 2**20
 
@@ -71,15 +71,18 @@
 
 
 def gather_kernel(
-    h_ref, c_ref, src_ref, tgt_ref, rel_ref, dir_ref, h_all, c_all, s8, t8, r8, local, hx_s, hx_r, hz_s, hz_r, cy_s, cy_r, cx_s, cx_r, cs_s, cs_r
+    h_ref, c_ref, w_hbm, src_ref, tgt_ref, rel_ref, dir_ref, own_c, own_h, loop_ref,
+    h_all, c_all, s8, t8, r8, t_out, l_out, w_ref, local, hx_s, hx_r, hz_s, hz_r, cy_s, cy_r, cx_s, cx_r, cs_s, cs_r
 ):
     me = Place()
     x_lo, x_hi, core, y, z = me.x_lo, me.x_hi, me.core, me.at["y"], me.at["z"]
     sibling, across = me.sibling(), me.x_lo_partner()
-    own_h = pltpu.make_async_copy(h_ref, h_all.at[x_hi, z], local.at[0])
-    own_c = pltpu.make_async_copy(c_ref, c_all.at[x_lo, y, core], local.at[1])
-    own_h.start()
-    own_c.start()
+    own_h_copy = pltpu.make_async_copy(h_ref, h_all.at[x_hi, z], local.at[0])
+    own_c_copy = pltpu.make_async_copy(c_ref, c_all.at[x_lo, y, core], local.at[1])
+    w_self = pltpu.make_async_copy(w_hbm.at[2], w_ref, local.at[2])
+    w_self.start()
+    own_h_copy.start()
+    own_c_copy.start()
     s8[...] = src_ref[...] * 8
     t8[...] = (tgt_ref[...] + dir_ref[...] * (16 * c_ref.shape[0])) * 8
     r8[...] = rel_ref[...] * 8
@@ -104,55 +107,64 @@
         copy = push(theirs, theirs, hz_s.at[k + 2], hz_r.at[k + 2], me.along("z", k))
         copy.start()
         hz.append(copy)
-    own_c.wait()
+    own_c_copy.wait()
     for copy in cy:
-        copy.wait()
+        copy.wait_recv()
     near = c_all.at[x_lo, :, core]
     far = c_all.at[1 - x_lo, :, core]
     cx = push(near, near, cx_s, cx_r, across)
     cx.start()
     first = push(near, near, cs_s.at[0], cs_r.at[0], sibling)
     first.start()
+    w_self.wait()
+    back = lax.dot_general(own_c[...], w_ref[...], (((1,), (1,)), ((), ())), preferred_element_type=F32)
+    t_out[...] = back * loop_ref[...].astype(F32).reshape(1, back.shape[1])
+    l_out[...] = jnp.sum(back * own_h[...].astype(F32), axis=0, keepdims=True)
     cx.wait()
     second = push(far, far, cs_s.at[1], cs_r.at[1], sibling)
     second.start()
     first.wait()
     second.wait()
-    own_h.wait()
+    own_h_copy.wait()
     for copy in hz:
         copy.wait()
-
-
-def gather(h_src, cotangent, *indices):
+    for copy in cy:
+        copy.wait_send()
+
+
+def gather(h_src, cotangent, weights, h_tgt, loop, *indices):
     rows, width = h_src.shape
     trows = cotangent.shape[0]
-    h_all, c_all, s8, t8, r8 = pl.pallas_call(
+    h_all, c_all, s8, t8, r8, grad_tgt, lsum = pl.pallas_call(
         gather_kernel,
         out_shape=(
             jax.ShapeDtypeStruct((2, 4, rows, width), BF16),
             jax.ShapeDtypeStruct((2, 4, 2, trows, width), BF16),
             *[jax.ShapeDtypeStruct(indices[0].shape, jnp.int32)] * 3,
+            jax.ShapeDtypeStruct((trows, width), F32),
+            jax.ShapeDtypeStruct((1, width), F32),
         ),
-        in_specs=[ANY] * 2 + [VMEM] * 4,
-        out_specs=[ANY] * 2 + [VMEM] * 3,
+        in_specs=[ANY] * 3 + [VMEM] * 7,
+        out_specs=[ANY] * 2 + [VMEM] * 5,
         scratch_shapes=[
-            DMA((2,)), DMA, DMA, DMA((6,)), DMA((6,)), DMA((3,)), DMA((3,)), DMA, DMA, DMA((2,)), DMA((2,)),
+            pltpu.VMEM((width, width), BF16),
+            DMA((3,)), DMA, DMA, DMA((6,)), DMA((6,)), DMA((3,)), DMA((3,)), DMA, DMA, DMA((2,)), DMA((2,)),
         ],
         compiler_params=pltpu.CompilerParams(collective_id=0, has_side_effects=True, vmem_limit_bytes=VMEM_BYTES),
         name="gather_panels",
-    )(h_src, cotangent, *indices)
+    )(h_src, cotangent, weights, *indices, cotangent, h_tgt, loop)
     flat = [a.reshape(-1) for a in (s8, t8, r8)]
-    return h_all.reshape(8 * rows, width), c_all.reshape(16 * trows, width), *flat
+    return h_all.reshape(8 * rows, width), c_all.reshape(16 * trows, width), *flat, grad_tgt, lsum
 
 
 def edge_kernel(
-    live_ref, src_ref, tgt_ref, rel_ref, h_hbm, c_hbm, w_hbm, z_hbm, own_c, own_h, loop_ref,
-    g_out, t_out, hi_out, lo_out, rest_out, keep_out, give_out,
+    live_ref, src_ref, tgt_ref, rel_ref, h_hbm, c_hbm, w_hbm, z_hbm, lsum,
+    g_out, hi_out, lo_out, rest_out, keep_out, give_out,
     h_ref, c_ref, w_ref, z_ref, g_ref, keep, give, hx, px, zx, gs, aa, rr, hi, lo, in_sem, out_sem,
 ):
     loads = [
         pltpu.make_async_copy(a, b, in_sem.at[i])
-        for i, (a, b) in enumerate(((h_hbm, h_ref), (z_hbm, z_ref), (c_hbm, c_ref), (w_hbm, w_ref)))
+        for i, (a, b) in enumerate(((h_hbm, h_ref), (z_hbm, z_ref), (c_hbm, c_ref), (w_hbm.at[pl.ds(0, 2)], w_ref)))
     ]
     for load in loads:
         load.start()
@@ -223,13 +235,6 @@
                 ref[row(at0), :] = sum0
                 ref[row(at1), :] = sum1
 
-    loop_wide = loop_ref[...].astype(F32).reshape(1, width)
-    h_wide = own_h[...].astype(F32)
-    back = lax.dot_general(
-        own_c[...], w_ref[2], (((1,), (1,)), ((), ())), preferred_element_type=F32
-    )
-    t_out[...] = back * loop_wide
-    lsum = jnp.sum(back * h_wide, axis=0, keepdims=True)
     for c in range(chunks):
         rr[rels * 8 + c : rels * 8 + c + 1, :] = lsum[:, c * 128 : (c + 1) * 128]
     blocks = rr.shape[0] // 128
@@ -298,7 +303,7 @@
         store.wait()
 
 
-def edges(live, s8, t8, r8, h, c, w, z, own_c, own_h, loop):
+def edges(live, s8, t8, r8, h, c, w, z, lsum):
     rows, width = h.shape
     trows = c.shape[0]
     rpad = (z.shape[0] + 16) // 16 * 16
@@ -306,19 +311,18 @@
         edge_kernel,
         out_shape=(
             jax.ShapeDtypeStruct((rows, width), BF16),
-            jax.ShapeDtypeStruct((own_c.shape[0], width), F32),
             jax.ShapeDtypeStruct((2 * trows, width), BF16),
             jax.ShapeDtypeStruct((2 * trows, width), BF16),
             jax.ShapeDtypeStruct((rpad // 16 * (width // 128) * 16 - FIRST_TILES * 16, 128), F32),
             jax.ShapeDtypeStruct((WAVE_HALF[0], 128), F32),
             jax.ShapeDtypeStruct((WAVE_HALF[0], 128), F32),
         ),
-        in_specs=[SMEM] * 4 + [ANY] * 4 + [VMEM] * 3,
-        out_specs=[ANY, VMEM, ANY, ANY, VMEM, ANY, ANY],
+        in_specs=[SMEM] * 4 + [ANY] * 4 + [VMEM],
+        out_specs=[ANY, ANY, ANY, VMEM, ANY, ANY],
         scratch_shapes=[
             pltpu.VMEM(h.shape, BF16),
             pltpu.VMEM(c.shape, BF16),
-            pltpu.VMEM(w.shape, BF16),
+            pltpu.VMEM((2, width, width), BF16),
             pltpu.VMEM(z.shape, BF16),
             pltpu.VMEM((rows, width), BF16),
             pltpu.VMEM((WAVE_HALF[0], 128), F32),
@@ -336,7 +340,7 @@
         ],
         compiler_params=pltpu.CompilerParams(vmem_limit_bytes=VMEM_BYTES),
         name="edges",
-    )(live, s8, t8, r8, h, c, w, z, own_c, own_h, loop)
+    )(live, s8, t8, r8, h, c, w, z, lsum)
 
 
 def reduce_kernel(
@@ -389,7 +393,7 @@
     for load in loads:
         load.start()
     plane = [me.along(axis, k) for axis in ("x", "y", "z") for k in (1, 2, 3)]
-    for p in (0, 1, 4):
+    for p in (0, 1, 2):
         plane += [in_plane(p, j, k) for j, k in others[:9]]
     greet(plane + [sibling])
 
@@ -695,92 +699,117 @@
     )(keep, give, g, hi, lo, c_all, rest, own_c, own_h, loop)
 
 
+REL_BLOCK = 18
+
+
 def unpack_kernel(
-    full_hbm, w_hbm, r_out, l_out, full, w_out, in_sem, out_sem, *, edge_scale, self_scale, rel_scale
+    full_hbm, gs_in, gt_in, w_hbm, r_out, l_out, gs_out, gt_out, full, w_out, in_sem, out_sem,
+    *, rels, edge_scale, self_scale, rel_scale,
 ):
-    rels, width = r_out.shape
+    step = pl.program_id(0)
+    last_step = -(-(rels + 1) // (REL_BLOCK * 16)) - 1
+    width = r_out.shape[1]
     chunks = width // 128
     per = width // 16
+    group = per // 3
     pieces = in_sem.shape[0]
     size = full.shape[0] // pieces
-    loads = []
-    for i in range(pieces):
+
+    def load(i):
         where = pl.ds(i * size, size)
-        loads.append(pltpu.make_async_copy(full_hbm.at[where], full.at[where], in_sem.at[i]))
-        loads[-1].start()
-    waited = []
-
-    def need(first, last):
-        for i in range(first // size, -(-last // size)):
-            if i not in waited:
-                waited.append(i)
-                loads[i].wait()
+        return pltpu.make_async_copy(full_hbm.at[where], full.at[where], in_sem.at[i])
+
+    def store(n):
+        if n < 9:
+            where = pl.ds(n % 3 * group * 16, group * 16)
+            return pltpu.make_async_copy(w_out.at[n // 3, where], w_hbm.at[n // 3, where], out_sem.at[n])
+        source, target = ((gs_in, gs_out), (gt_in, gt_out))[n - 9]
+        return pltpu.make_async_copy(source, target, out_sem.at[n])
 
     def tile(first, index):
         return full[pl.ds(pl.multiple_of(first + index * 16, 16), 16), :].astype(F32)
 
     w_first = 2 * WAVE_HALF[0]
     rest_first = w_first + W_TILES * 16
-    stores = []
-    for d, scale in enumerate((edge_scale, edge_scale, self_scale)):
-        for k in range(3):
-            group = per // 3
-            need(w_first, w_first + (d * per + (k + 1) * group) * chunks * 16)
-
-            @pl.loop(k * group, (k + 1) * group)
+
+    @pl.when(step == 0)
+    def _():
+        order = [*range(w_first // size, pieces), *range(w_first // size)]
+        for i in order:
+            load(i).start()
+        store(9).start()
+        store(10).start()
+        waited = 0
+        for n in range(9):
+            end = w_first + (n + 1) * group * chunks * 16
+            while order[waited] * size < end and waited < pieces - w_first // size:
+                load(order[waited]).wait()
+                waited += 1
+            d, scale = n // 3, (edge_scale, edge_scale, self_scale)[n // 3]
+
+            @pl.loop(n % 3 * group, (n % 3 + 1) * group)
             def _(i, d=d, scale=scale):
                 for c in range(chunks):
                     w_out[d, pl.ds(pl.multiple_of(i * 16, 16), 16), c * 128 : (c + 1) * 128] = (
                         tile(w_first, (d * per + i) * chunks + c) * scale
                     )
 
-            where = pl.ds(k * group * 16, group * 16)
-            stores.append(
-                pltpu.make_async_copy(w_out.at[d, where], w_hbm.at[d, where], out_sem.at[d * 3 + k])
-            )
-            stores[-1].start()
-
-    need(0, full.shape[0])
-    whole = FIRST_TILES // chunks
-
-    @pl.loop(0, whole)
-    def _(i):
-        for c in range(chunks):
-            r_out[pl.ds(pl.multiple_of(i * 16, 16), 16), c * 128 : (c + 1) * 128] = (
-                tile(0, i * chunks + c) * rel_scale
-            )
-
-    for t in range(whole * chunks, -(-(rels + 1) // 16) * chunks):
-        b, cols = t // chunks, slice(t % chunks * 128, t % chunks * 128 + 128)
-        last = tile(0, t) if t < FIRST_TILES else tile(rest_first, t - FIRST_TILES)
-        n = min(16, rels - b * 16)
-        if n:
-            r_out[b * 16 : b * 16 + n, cols] = last[:n] * rel_scale
-        if n < 16:
-            l_out[cols] = (last[n : n + 1] * self_scale).reshape(128)
-    for store in stores:
-        store.wait()
-
-
-def unpack(full, rels, width, **scales):
+            store(n).start()
+        for i in order[waited:]:
+            load(i).wait()
+
+    @pl.when(step != last_step)
+    def _():
+        @pl.loop(0, REL_BLOCK)
+        def _(i):
+            for c in range(chunks):
+                r_out[pl.ds(pl.multiple_of(i * 16, 16), 16), c * 128 : (c + 1) * 128] = (
+                    tile(0, (step * REL_BLOCK + i) * chunks + c) * rel_scale
+                )
+
+    @pl.when(step == last_step)
+    def _():
+        first = last_step * REL_BLOCK
+        for t in range(first * chunks, -(-(rels + 1) // 16) * chunks):
+            b, cols = t // chunks, slice(t % chunks * 128, t % chunks * 128 + 128)
+            value = tile(0, t) if t < FIRST_TILES else tile(rest_first, t - FIRST_TILES)
+            r_out[(b - first) * 16 : (b - first) * 16 + 16, cols] = value * rel_scale
+            n = rels - b * 16
+            if n < 16:
+                l_out[cols] = (value[n : n + 1] * self_scale).reshape(128)
+        for n in range(11):
+            store(n).wait()
+
+
+def unpack(full, grad_src, grad_tgt, rels, width, **scales):
+    rows = REL_BLOCK * 16
     return pl.pallas_call(
-        functools.partial(unpack_kernel, **scales),
+        functools.partial(unpack_kernel, rels=rels, **scales),
+        grid=(-(-(rels + 1) // rows),),
         out_shape=(
             jax.ShapeDtypeStruct((3, width, width), F32),
             jax.ShapeDtypeStruct((rels, width), F32),
             jax.ShapeDtypeStruct((width,), F32),
+            jax.ShapeDtypeStruct(grad_src.shape, F32),
+            jax.ShapeDtypeStruct(grad_tgt.shape, F32),
         ),
-        in_specs=[ANY],
-        out_specs=[ANY, VMEM, VMEM],
+        in_specs=[ANY] * 3,
+        out_specs=[
+            ANY,
+            pl.BlockSpec((rows, width), lambda i: (i, 0)),
+            pl.BlockSpec((width,), lambda i: (0,)),
+            ANY,
+            ANY,
+        ],
         scratch_shapes=[
             pltpu.VMEM(full.shape, BF16),
             pltpu.VMEM((3, width, width), F32),
             DMA((11,)),
-            DMA((9,)),
+            DMA((11,)),
         ],
         compiler_params=pltpu.CompilerParams(vmem_limit_bytes=VMEM_BYTES),
         name="unpack",
-    )(full)
+    )(full, grad_src, grad_tgt)
 
 
 def body(
@@ -789,20 +818,22 @@
     width = weights.shape[1]
     tiles, edge = src_index.shape[2:]
     rels = rel_table.shape[0]
-    h_all, c_all, s8, t8, r8 = gather(
-        h_src, cotangent, *[a.reshape(tiles, edge) for a in (src_index, tgt_index, rel_ids, direction)]
+    h_all, c_all, s8, t8, r8, back, lsum = gather(
+        h_src, cotangent, weights, h_tgt, loop_rel, *[a.reshape(tiles, edge) for a in (src_index, tgt_index, rel_ids, direction)]
     )
-    g, grad_tgt, hi, lo, rest, keep, give = edges(
-        counts.reshape(1), s8, t8, r8, h_all, c_all, weights, rel_table, cotangent, h_tgt, loop_rel
+    g, hi, lo, rest, keep, give = edges(
+        counts.reshape(1), s8, t8, r8, h_all, c_all, weights, rel_table, lsum
     )
-    full, grad_src = reduce_all(
+    full, mine = reduce_all(
         keep, give, g, hi, lo, c_all, rest, cotangent, h_tgt, loop_rel
     )
     devices = lax.axis_size("src") * lax.axis_size("tgt")
     edges_all = float(devices * tiles * edge)
     targets_all = float(devices * cotangent.shape[0])
-    grad_weights, grad_rel, grad_loop = unpack(
+    grad_weights, grad_rel, grad_loop, grad_src, grad_tgt = unpack(
         full,
+        mine,
+        back,
         rels,
         width,
         edge_scale=edges_all**-0.5,

time: 108 us -> 109 us (level)
  Pallas kernels: 105 us -> 107 us
    pallas_call x1, Pallas kernels: 7.09 us -> 11.1 us  [unpack(): pl.pallas_call(functools.partial(unpack_kernel, rels=rels, **scales), gri...]
    pallas_call x1, Pallas kernels: 65 us -> 63.2 us  [reduce_all(): pl.pallas_call(reduce_kernel, out_shape=(jax.ShapeDtypeStruct((2 * HALF_R...]
where the time goes in v6:
time: 109 us; the launch traced here: 108 us
  Pallas kernels  107 us (98%)
  between operations  1.3 us (1%)
    pallas_call x1, Pallas kernels, reduce_all(): pl.pallas_call(reduce_kernel, out_shape=(jax.ShapeDtypeStruct((2 * HALF_R...  63.2 us
    pallas_call x1, Pallas kernels, gather(): pl.pallas_call(gather_kernel, out_shape=(jax.ShapeDtypeStruct((2, 4, rows...  20.4 us
    pallas_call x1, Pallas kernels, edges(): pl.pallas_call(edge_kernel, out_shape=(jax.ShapeDtypeStruct((rows, width)...  12.3 us
    pallas_call x1, Pallas kernels, unpack(): pl.pallas_call(functools.partial(unpack_kernel, rels=rels, **scales), gri...  11.1 us

profile of v6, /device:TPU:1, one launch (start us, length us, event | category | flops | bytes accessed | tf_op | source)
XLA Modules:
  0.0 108.4 jit_solution(7373099062355450691)
XLA Ops:
  1.3 20.4 %gather_panels.1 = (bf16[2,4,64,768]{3,2,1,0:T(8,128)(2,1)}, bf16[2,4,2,32,768]{4,3,2,1,0:T(8,128)(2,1)}, s32[16,128]{1,0:T(8,128)}, s32[16,128]{1,0:T(8,128)}, ...) custom-call(bf16[64,768]{1,0:T(8,128)(2,1)} %h_ref.1, bf16[32,768]{1,0:T(8,128)(2,1)} %own_c.3, ...), custom_call_target="tpu_custom_call" | custom-call | tf_op jit(solution)/shard_map/gather_panels/pallas_call | solution.py:138
  21.7 12.3 %edges.1 = (bf16[512,768]{1,0:T(8,128)(2,1)}, bf16[1024,768]{1,0:T(8,128)(2,1)}, bf16[1024,768]{1,0:T(8,128)(2,1)}, f32[160,128]{1,0:T(8,128)}, f32[4096,128]{1,0:T(8,128)}, /*index=5*/f32[4096,128]{1,0:T(8,128)}) custom-call(s32[1]{0:T(128)} %bitcast.11.live_ref, s32[2048]{0:T(1024)} %bitcast.20, s32[2048]{0:T(1024)} %bitcast.21, s32[2048]{0:T(1024)} %bitcast.22, ...), custom_call_target="tpu_custom_call" | custom-call | tf_op jit(solution)/shard_map/edges/pallas_call | solution.py:310
  34.0 63.2 %reduce_all.1 = (bf16[22528,128]{1,0:T(8,128)(2,1)}, f32[64,768]{1,0:T(8,128)}) custom-call(f32[4096,128]{1,0:T(8,128)} %get-tuple-element.31.keep_hbm, f32[4096,128]{1,0:T(8,128)} %get-tuple-element.32.give, bf16[2,4,64,768]{3,2,1,0:T(8,128)(2,1)} %bitcast.14, bf16[1024,768]{1,0:T(8,128)(2,1)} %get-tuple-element.34.hi_hbm, ...), custom_call_target="tpu_custom_call" | custom-call | tf_op jit(solution)/shard_map/reduce_all/pallas_call | solution.py:667
  97.3 11.1 %unpack.1 = (f32[3,768,768]{2,1,0:T(8,128)}, f32[1387,768]{1,0:T(8,128)}, f32[768]{0:T(1024)}, f32[64,768]{1,0:T(8,128)}, f32[32,768]{1,0:T(8,128)}) custom-call(bf16[22528,128]{1,0:T(8,128)(2,1)} %get-tuple-element.37.full_hbm, f32[64,768]{1,0:T(8,128)} %get-tuple-element.38.gs_in, f32[32,768]{1,0:T(8,128)} %get-tuple-element.39.gt_in), custom_call_target="tpu_custom_call" | custom-call | tf_op jit(solution)/shard_map/unpack/pallas_call | solution.py:786

commit v7 on v6

--- a/solution.py
+++ b/solution.py
@@ -345,7 +345,7 @@
 
 def reduce_kernel(
     keep_hbm, give, g_ref, hi_hbm, lo_hbm, c_hbm, rest, own_c, own_h, loop_ref, full, g_out,
-    keep, given, hi, lo, c_all, g_own, pair, out1, in1, acc1, out2, in2, unit, g_in, g_acc, g_side,
+    keep, given, hi, lo, c_all, g_own, pair, out1, in1, acc1, out2, in2, unit, g_in, g_acc, g_send, g_side,
     pair_s, pair_r, s1, r1, s2, r2, s4, r4, s6, r6, sib_s, sib_r, gz_s, gz_r, gx_s, gx_r,
     local, kept,
 ):
@@ -616,6 +616,9 @@
     send_second(4)
     share_second(0)
     share_second(1)
+    share_second(2)
+    share_second(3)
+    share_second(4)
     for copy in gz:
         copy.wait_recv()
     for half in range(2):
@@ -625,11 +628,9 @@
             + g_in[1, half].astype(F32)
             + g_in[2, half].astype(F32)
         )
-    gx = push(g_acc.at[1 - x_hi], g_side, gx_s, gx_r, me.along("x", 2))
+    g_send[...] = g_acc[1 - x_hi].astype(BF16)
+    gx = push(g_send, g_side, gx_s, gx_r, me.along("x", 2))
     gx.start()
-    share_second(2)
-    share_second(3)
-    share_second(4)
     share_first(0)
     share_first(1)
     share_first(2)
@@ -643,7 +644,7 @@
     finish(0)
     finish(1)
     gx.wait_recv()
-    g_out[...] = g_acc[x_hi] + g_side[...]
+    g_out[...] = g_acc[x_hi] + g_side[...].astype(F32)
     finish(2)
     finish(3)
     finish(4)
@@ -688,7 +689,8 @@
             pltpu.VMEM((HALF_ROWS // 64, 128), BF16),
             pltpu.VMEM((3, 2, rows // 8, width), BF16),
             pltpu.VMEM((2, rows // 8, width), F32),
-            pltpu.VMEM((rows // 8, width), F32),
+            pltpu.VMEM((rows // 8, width), BF16),
+            pltpu.VMEM((rows // 8, width), BF16),
             *[DMA((4 * n,))] * 2, *[DMA((3 * n,))] * 2, *[DMA((n,))] * 4, *[DMA((6 * n,))] * 2, *[DMA((7 * n,))] * 2,
             DMA((3,)), DMA((3,)), DMA, DMA, DMA((n,)), DMA((5,)),
         ],
@@ -703,7 +705,7 @@
 
 
 def unpack_kernel(
-    full_hbm, gs_in, gt_in, w_hbm, r_out, l_out, gs_out, gt_out, full, w_out, in_sem, out_sem,
+    full_hbm, gs_in, gt_in, w_hbm, r_out, l_out, gs_out, gt_out, full, w_out, gs, gt, in_sem, out_sem,
     *, rels, edge_scale, self_scale, rel_scale,
 ):
     step = pl.program_id(0)
@@ -712,10 +714,13 @@
     chunks = width // 128
     per = width // 16
     group = per // 3
-    pieces = in_sem.shape[0]
+    pieces = in_sem.shape[0] - 2
     size = full.shape[0] // pieces
 
     def load(i):
+        if i >= pieces:
+            source, target = ((gs_in, gs), (gt_in, gt))[i - pieces]
+            return pltpu.make_async_copy(source, target, in_sem.at[i])
         where = pl.ds(i * size, size)
         return pltpu.make_async_copy(full_hbm.at[where], full.at[where], in_sem.at[i])
 
@@ -723,7 +728,7 @@
         if n < 9:
             where = pl.ds(n % 3 * group * 16, group * 16)
             return pltpu.make_async_copy(w_out.at[n // 3, where], w_hbm.at[n // 3, where], out_sem.at[n])
-        source, target = ((gs_in, gs_out), (gt_in, gt_out))[n - 9]
+        source, target = ((gs, gs_out), (gt, gt_out))[n - 9]
         return pltpu.make_async_copy(source, target, out_sem.at[n])
 
     def tile(first, index):
@@ -734,11 +739,9 @@
 
     @pl.when(step == 0)
     def _():
-        order = [*range(w_first // size, pieces), *range(w_first // size)]
+        order = [*range(w_first // size, pieces), *range(w_first // size), pieces, pieces + 1]
         for i in order:
             load(i).start()
-        store(9).start()
-        store(10).start()
         waited = 0
         for n in range(9):
             end = w_first + (n + 1) * group * chunks * 16
@@ -757,6 +760,8 @@
             store(n).start()
         for i in order[waited:]:
             load(i).wait()
+        store(9).start()
+        store(10).start()
 
     @pl.when(step != last_step)
     def _():
@@ -804,7 +809,9 @@
         scratch_shapes=[
             pltpu.VMEM(full.shape, BF16),
             pltpu.VMEM((3, width, width), F32),
-            DMA((11,)),
+            pltpu.VMEM(grad_src.shape, F32),
+            pltpu.VMEM(grad_tgt.shape, F32),
+            DMA((13,)),
             DMA((11,)),
         ],
         compiler_params=pltpu.CompilerParams(vmem_limit_bytes=VMEM_BYTES),

time: 109 us -> 103 us (0.945)
  Pallas kernels: 107 us -> 101 us
    pallas_call x1, Pallas kernels: 63.2 us -> 58 us  [reduce_all(): pl.pallas_call(reduce_kernel, out_shape=(jax.ShapeDtypeStruct((2 * HALF_R...]
    pallas_call x1, Pallas kernels: 11.1 us -> 7.51 us  [unpack(): pl.pallas_call(functools.partial(unpack_kernel, rels=rels, **scales), gri...]
    pallas_call x1, Pallas kernels: 12.3 us -> 15.4 us  [edges(): pl.pallas_call(edge_kernel, out_shape=(jax.ShapeDtypeStruct((rows, width)...]
where the time goes in v7:
time: 103 us
  Pallas kernels  101 us (98%)
  between operations  1.3 us (1%)
    pallas_call x1, Pallas kernels, reduce_all(): pl.pallas_call(reduce_kernel, out_shape=(jax.ShapeDtypeStruct((2 * HALF_R...  58 us
    pallas_call x1, Pallas kernels, gather(): pl.pallas_call(gather_kernel, out_shape=(jax.ShapeDtypeStruct((2, 4, rows...  20.4 us
    pallas_call x1, Pallas kernels, edges(): pl.pallas_call(edge_kernel, out_shape=(jax.ShapeDtypeStruct((rows, width)...  15.4 us
    pallas_call x1, Pallas kernels, unpack(): pl.pallas_call(functools.partial(unpack_kernel, rels=rels, **scales), gri...  7.51 us

profile of v7, /device:TPU:1, one launch (start us, length us, event | category | flops | bytes accessed | tf_op | source)
XLA Modules:
  0.0 102.7 jit_solution(14407100225058584999)
XLA Ops:
  1.3 20.4 %gather_panels.1 = (bf16[2,4,64,768]{3,2,1,0:T(8,128)(2,1)}, bf16[2,4,2,32,768]{4,3,2,1,0:T(8,128)(2,1)}, s32[16,128]{1,0:T(8,128)}, s32[16,128]{1,0:T(8,128)}, ...) custom-call(bf16[64,768]{1,0:T(8,128)(2,1)} %h_ref.1, bf16[32,768]{1,0:T(8,128)(2,1)} %own_c.3, ...), custom_call_target="tpu_custom_call" | custom-call | tf_op jit(solution)/shard_map/gather_panels/pallas_call | solution.py:138
  21.7 15.4 %edges.1 = (bf16[512,768]{1,0:T(8,128)(2,1)}, bf16[1024,768]{1,0:T(8,128)(2,1)}, bf16[1024,768]{1,0:T(8,128)(2,1)}, f32[160,128]{1,0:T(8,128)}, f32[4096,128]{1,0:T(8,128)}, /*index=5*/f32[4096,128]{1,0:T(8,128)}) custom-call(s32[1]{0:T(128)} %bitcast.11.live_ref, s32[2048]{0:T(1024)} %bitcast.20, s32[2048]{0:T(1024)} %bitcast.21, s32[2048]{0:T(1024)} %bitcast.22, ...), custom_call_target="tpu_custom_call" | custom-call | tf_op jit(solution)/shard_map/edges/pallas_call | solution.py:310
  37.1 58.0 %reduce_all.1 = (bf16[22528,128]{1,0:T(8,128)(2,1)}, f32[64,768]{1,0:T(8,128)}) custom-call(f32[4096,128]{1,0:T(8,128)} %get-tuple-element.31.keep_hbm, f32[4096,128]{1,0:T(8,128)} %get-tuple-element.32.give, bf16[2,4,64,768]{3,2,1,0:T(8,128)(2,1)} %bitcast.14, bf16[1024,768]{1,0:T(8,128)(2,1)} %get-tuple-element.34.hi_hbm, ...), custom_call_target="tpu_custom_call" | custom-call | tf_op jit(solution)/shard_map/reduce_all/pallas_call | solution.py:668
  95.1 7.5 %unpack.1 = (f32[3,768,768]{2,1,0:T(8,128)}, f32[1387,768]{1,0:T(8,128)}, f32[768]{0:T(1024)}, f32[64,768]{1,0:T(8,128)}, f32[32,768]{1,0:T(8,128)}) custom-call(bf16[22528,128]{1,0:T(8,128)(2,1)} %get-tuple-element.37.full_hbm, f32[64,768]{1,0:T(8,128)} %get-tuple-element.38.gs_in, f32[32,768]{1,0:T(8,128)} %get-tuple-element.39.gt_in), custom_call_target="tpu_custom_call" | custom-call | tf_op jit(solution)/shard_map/unpack/pallas_call | solution.py:791

commit v8 on v7

--- a/solution.py
+++ b/solution.py
@@ -607,8 +607,7 @@
     make_wsum(1)
     make_wself()
     send_pair((2, 3, 4))
-    send_first((0, 1))
-    send_first((2, 3, 4))
+    send_first((0, 1, 2, 3, 4))
     send_second(0)
     send_second(1)
     send_second(2)

time: 103 us -> 102 us (level)
  Pallas kernels: 101 us -> 99.9 us
    pallas_call x1, Pallas kernels: 15.4 us -> 12.3 us  [edges(): pl.pallas_call(edge_kernel, out_shape=(jax.ShapeDtypeStruct((rows, width)...]
    pallas_call x1, Pallas kernels: 58 us -> 59.7 us  [reduce_all(): pl.pallas_call(reduce_kernel, out_shape=(jax.ShapeDtypeStruct((2 * HALF_R...]
where the time goes in v8:
time: 102 us; the launch traced here: 101 us
  Pallas kernels  99.9 us (98%)
  between operations  1.3 us (1%)
    pallas_call x1, Pallas kernels, reduce_all(): pl.pallas_call(reduce_kernel, out_shape=(jax.ShapeDtypeStruct((2 * HALF_R...  59.7 us
    pallas_call x1, Pallas kernels, gather(): pl.pallas_call(gather_kernel, out_shape=(jax.ShapeDtypeStruct((2, 4, rows...  20.4 us
    pallas_call x1, Pallas kernels, edges(): pl.pallas_call(edge_kernel, out_shape=(jax.ShapeDtypeStruct((rows, width)...  12.3 us
    pallas_call x1, Pallas kernels, unpack(): pl.pallas_call(functools.partial(unpack_kernel, rels=rels, **scales), gri...  7.51 us

profile of v8, /device:TPU:1, one launch (start us, length us, event | category | flops | bytes accessed | tf_op | source)
XLA Modules:
  0.0 101.2 jit_solution(1017566303849965378)
XLA Ops:
  1.3 20.4 %gather_panels.1 = (bf16[2,4,64,768]{3,2,1,0:T(8,128)(2,1)}, bf16[2,4,2,32,768]{4,3,2,1,0:T(8,128)(2,1)}, s32[16,128]{1,0:T(8,128)}, s32[16,128]{1,0:T(8,128)}, ...) custom-call(bf16[64,768]{1,0:T(8,128)(2,1)} %h_ref.1, bf16[32,768]{1,0:T(8,128)(2,1)} %own_c.3, ...), custom_call_target="tpu_custom_call" | custom-call | tf_op jit(solution)/shard_map/gather_panels/pallas_call | solution.py:138
  21.7 12.3 %edges.1 = (bf16[512,768]{1,0:T(8,128)(2,1)}, bf16[1024,768]{1,0:T(8,128)(2,1)}, bf16[1024,768]{1,0:T(8,128)(2,1)}, f32[160,128]{1,0:T(8,128)}, f32[4096,128]{1,0:T(8,128)}, /*index=5*/f32[4096,128]{1,0:T(8,128)}) custom-call(s32[1]{0:T(128)} %bitcast.11.live_ref, s32[2048]{0:T(1024)} %bitcast.20, s32[2048]{0:T(1024)} %bitcast.21, s32[2048]{0:T(1024)} %bitcast.22, ...), custom_call_target="tpu_custom_call" | custom-call | tf_op jit(solution)/shard_map/edges/pallas_call | solution.py:310
  34.0 59.7 %reduce_all.1 = (bf16[22528,128]{1,0:T(8,128)(2,1)}, f32[64,768]{1,0:T(8,128)}) custom-call(f32[4096,128]{1,0:T(8,128)} %get-tuple-element.31.keep_hbm, f32[4096,128]{1,0:T(8,128)} %get-tuple-element.32.give, bf16[2,4,64,768]{3,2,1,0:T(8,128)(2,1)} %bitcast.14, bf16[1024,768]{1,0:T(8,128)(2,1)} %get-tuple-element.34.hi_hbm, ...), custom_call_target="tpu_custom_call" | custom-call | tf_op jit(solution)/shard_map/reduce_all/pallas_call | solution.py:667
  93.7 7.5 %unpack.1 = (f32[3,768,768]{2,1,0:T(8,128)}, f32[1387,768]{1,0:T(8,128)}, f32[768]{0:T(1024)}, f32[64,768]{1,0:T(8,128)}, f32[32,768]{1,0:T(8,128)}) custom-call(bf16[22528,128]{1,0:T(8,128)(2,1)} %get-tuple-element.37.full_hbm, f32[64,768]{1,0:T(8,128)} %get-tuple-element.38.gs_in, f32[32,768]{1,0:T(8,128)} %get-tuple-element.39.gt_in), custom_call_target="tpu_custom_call" | custom-call | tf_op jit(solution)/shard_map/unpack/pallas_call | solution.py:790

commit v9 on v8

--- a/solution.py
+++ b/solution.py
@@ -395,7 +395,7 @@
     plane = [me.along(axis, k) for axis in ("x", "y", "z") for k in (1, 2, 3)]
     for p in (0, 1, 2):
         plane += [in_plane(p, j, k) for j, k in others[:9]]
-    greet(plane + [sibling])
+    greet(plane[::-1] + [sibling])
 
     pairs, step1, step6, side, own = {}, {}, {}, {}, {}
 
@@ -594,12 +594,12 @@
         def _():
             store(given, 0)
 
-    send_pair((0, 1))
     gz = []
     for k in (1, 3, 2):
         copy = push(g_ref.at[:, (z + k) % 4], g_in.at[k - 1], gz_s.at[k - 1], gz_r.at[k - 1], me.along("z", k))
         copy.start()
         gz.append(copy)
+    send_pair((0, 1))
     loads[0].wait()
     for load in loads[1:]:
         load.wait()

time: 102 us -> 102 us (level)
  no operation moved by 1% of the time
where the time goes in v9:
time: 102 us; the launch traced here: 101 us
  Pallas kernels  100 us (98%)
  between operations  1.3 us (1%)
    pallas_call x1, Pallas kernels, reduce_all(): pl.pallas_call(reduce_kernel, out_shape=(jax.ShapeDtypeStruct((2 * HALF_R...  59.8 us
    pallas_call x1, Pallas kernels, gather(): pl.pallas_call(gather_kernel, out_shape=(jax.ShapeDtypeStruct((2, 4, rows...  20.4 us
    pallas_call x1, Pallas kernels, edges(): pl.pallas_call(edge_kernel, out_shape=(jax.ShapeDtypeStruct((rows, width)...  12.3 us
    pallas_call x1, Pallas kernels, unpack(): pl.pallas_call(functools.partial(unpack_kernel, rels=rels, **scales), gri...  7.51 us

profile of v9, /device:TPU:1, one launch (start us, length us, event | category | flops | bytes accessed | tf_op | source)
XLA Modules:
  0.0 101.3 jit_solution(12134448567818981592)
XLA Ops:
  1.3 20.4 %gather_panels.1 = (bf16[2,4,64,768]{3,2,1,0:T(8,128)(2,1)}, bf16[2,4,2,32,768]{4,3,2,1,0:T(8,128)(2,1)}, s32[16,128]{1,0:T(8,128)}, s32[16,128]{1,0:T(8,128)}, ...) custom-call(bf16[64,768]{1,0:T(8,128)(2,1)} %h_ref.1, bf16[32,768]{1,0:T(8,128)(2,1)} %own_c.3, ...), custom_call_target="tpu_custom_call" | custom-call | tf_op jit(solution)/shard_map/gather_panels/pallas_call | solution.py:138
  21.7 12.3 %edges.1 = (bf16[512,768]{1,0:T(8,128)(2,1)}, bf16[1024,768]{1,0:T(8,128)(2,1)}, bf16[1024,768]{1,0:T(8,128)(2,1)}, f32[160,128]{1,0:T(8,128)}, f32[4096,128]{1,0:T(8,128)}, /*index=5*/f32[4096,128]{1,0:T(8,128)}) custom-call(s32[1]{0:T(128)} %bitcast.11.live_ref, s32[2048]{0:T(1024)} %bitcast.20, s32[2048]{0:T(1024)} %bitcast.21, s32[2048]{0:T(1024)} %bitcast.22, ...), custom_call_target="tpu_custom_call" | custom-call | tf_op jit(solution)/shard_map/edges/pallas_call | solution.py:310
  34.0 59.8 %reduce_all.1 = (bf16[22528,128]{1,0:T(8,128)(2,1)}, f32[64,768]{1,0:T(8,128)}) custom-call(f32[4096,128]{1,0:T(8,128)} %get-tuple-element.31.keep_hbm, f32[4096,128]{1,0:T(8,128)} %get-tuple-element.32.give, bf16[2,4,64,768]{3,2,1,0:T(8,128)(2,1)} %bitcast.14, bf16[1024,768]{1,0:T(8,128)(2,1)} %get-tuple-element.34.hi_hbm, ...), custom_call_target="tpu_custom_call" | custom-call | tf_op jit(solution)/shard_map/reduce_all/pallas_call | solution.py:667
  93.8 7.5 %unpack.1 = (f32[3,768,768]{2,1,0:T(8,128)}, f32[1387,768]{1,0:T(8,128)}, f32[768]{0:T(1024)}, f32[64,768]{1,0:T(8,128)}, f32[32,768]{1,0:T(8,128)}) custom-call(bf16[22528,128]{1,0:T(8,128)(2,1)} %get-tuple-element.37.full_hbm, f32[64,768]{1,0:T(8,128)} %get-tuple-element.38.gs_in, f32[32,768]{1,0:T(8,128)} %get-tuple-element.39.gt_in), custom_call_target="tpu_custom_call" | custom-call | tf_op jit(solution)/shard_map/unpack/pallas_call | solution.py:790
